TPU v7x, 512 devices: a whole 4x8x8 slice. The times are simulated.
512 devices in a mesh: orig: 32 (over z_lo, y), dest: 16 (over z_hi, x, core).
Axes of the slice: x: 4, y: 8, z: 8 (z_hi: 2, z_lo: 4; z = z_hi * 4 + z_lo), core: 2. Of those that a mesh axis runs over, the one named last changes fastest.
Arguments:
- log_cost: bfloat16 [16384, 16384], P('orig', 'dest'), may hold values from 0 to 0.59765625
- elasticity: float32 [8], replicated, may hold values from 3 to 9
- productivity: float32 [8, 16384], P(None, 'orig'), may hold values from 0.3 to 3
- preference: float32 [8, 16384], P(None, 'dest'), may hold values from 0.2 to 5
- workers: float32 [16384], P('orig'), may hold values from 1 to 30
- start_wage: float32 [16384], P('orig'), may hold values from 0.2 to 5
Outputs:
- wage: float32 [16384], P('orig')
- log_price: float32 [8, 16384], P(None, 'dest')
All inputs are finite; a program needn't handle non-finite values.
Results may differ from a plain program's by a relative error of at most 0.0003.
Values sent between devices are 32-bit elements; how exact they have to be, the bound alone decides.
No kernel may reach another device: no remote copies, remote signals or barrier semaphores. Data moves between devices by JAX's collectives and lax.ppermute only.
A program may use at most 64 MiB of HBM per device.

v0:
```python
import jax
import jax.numpy as jnp
from jax import lax
from jax.sharding import PartitionSpec as P

ITERS = 3


def on_device(log_cost, elasticity, productivity, preference, workers, start_wage):
    rows = log_cost.shape[0]
    columns = log_cost.shape[1]
    cells = rows * lax.axis_size("orig")
    spend_share = preference / jnp.sum(preference, axis=0, keepdims=True)

    def settle(raw_wage, wanted):
        local_income = None
        world_income = lax.psum(jnp.sum(raw_wage * workers), "orig")
        factor = cells / world_income
        wage = raw_wage * factor
        if wanted:
            incomes = lax.all_gather(wage * workers, "orig", axis=0, tiled=True)
            local_income = lax.dynamic_slice_in_dim(
                incomes, lax.axis_index("dest") * columns, columns
            )
        return (wage, local_income)

    def kernel_of(slope):
        return jnp.exp(-slope * log_cost.astype(jnp.float32))

    def phi_term(pair):
        return jnp.dot(pair[1], kernel_of(pair[0]), precision=lax.Precision.HIGHEST)

    def sales_term(pair):
        return jnp.dot(kernel_of(pair[0]), pair[1], precision=lax.Precision.HIGHEST)

    wage, dest_income = settle(start_wage, True)
    for step in range(ITERS):
        supply = productivity * jnp.exp(-elasticity[:, None] * jnp.log(wage)[None, :])
        spending = spend_share * dest_income[None, :]
        partial_phi = lax.map(phi_term, (elasticity, supply))
        price_part = lax.psum_scatter(partial_phi, "orig", scatter_dimension=1, tiled=True)
        part_width = price_part.shape[1]
        own_spending = lax.dynamic_slice_in_dim(
            spending, lax.axis_index("orig") * part_width, part_width, 1
        )
        ratio, log_price = (
            lax.all_gather(own_spending / price_part, "orig", axis=1, tiled=True),
            lax.all_gather(-jnp.log(price_part) / elasticity[:, None], "orig", axis=1, tiled=True),
        )
        partial_sales = lax.map(sales_term, (elasticity, ratio))
        sector_sales = lax.psum(partial_sales, "dest")
        revenue = jnp.sum(supply * sector_sales, axis=0)
        raw_wage = wage * jnp.sqrt(revenue / (wage * workers))
        wage, dest_income = settle(raw_wage, step + 1 < ITERS)
    return (wage, log_price)


def solution(mesh):
    return jax.shard_map(
        on_device,
        mesh=mesh,
        in_specs=(P("orig", "dest"), P(), P(None, "orig"), P(None, "dest"), P("orig"), P("orig")),
        out_specs=(P("orig"), P(None, "dest")),
        check_vma=False,
    )
```

profile of v0, /device:TPU:8, one launch (start us, length us, event | category | flops | bytes accessed | tf_op | source)
XLA Modules:
  0.0 1521.6 jit_solution(11848121613594970274)
XLA Ops:
  8.5 80.8 %psum.49 = f32[]{:T(128)} all-reduce(f32[]{:T(128)} %multiply_reduce_fusion.6), channel_id=1, replica_groups=mesh['orig'=32,'dest'=16] {'orig'}, use_global_device_ids=true, to_apply=%region_1.0 | all-reduce | flops 1 | bytes 8 | tf_op jit(solution)/shard_map/psum | solution.py:17
  92.1 36.5 %while.60 = (s32[]{:T(128)}, f32[8,1024]{1,0:T(8,128)S(1)}, f32[8,512]{1,0:T(8,128)S(1)}, f32[8]{0:T(128)}, bf16[512,1024]{1,0:T(8,128)(2,1)}, /*index=5*/s32[]{:T(128)}, s32[]{:T(128)}) while((s32[]{:T(128)}, f32[8,1024]{1,0:T(8,128)S(1)}, f32[8,512]{1,0:T(8,128)S(1)}, f32[8]{0:T(128)}, bf16[512,1024]{1,0:T(8,128)(2,1)}, ...), condition=%wide.region_4.5_spmd, body=%wide.region_3.4_spmd.sunk | while | flops 7340035 | bytes 1063021 | solution.py:40
  94.0 2.6 fusion.68
  98.6 2.6 fusion.68
  103.2 2.6 fusion.68
  107.7 2.6 fusion.68
  112.3 2.6 fusion.68
  116.8 2.6 fusion.68
  121.4 2.6 fusion.68
  126.0 2.6 fusion.68
  129.8 76.6 %all-gather = f32[32,1,512]{2,1,0:T(1,128)S(1)} all-gather(f32[1,1,512]{2,1,0:T(1,128)S(1)} %bitcast.113), channel_id=1, replica_groups=mesh['orig'=32,'dest'=16] {'orig'}, dimensions={0}, use_global_device_ids=true | all-gather | bytes 67584 | tf_op jit(solution)/shard_map/all_gather | solution.py:21
  206.5 80.0 %reduce-scatter.10.cloned.1.call-done = f32[32,8]{1,0:T(8,128)} async-done(((f32[1024,8]{1,0:T(8,128)}), f32[32,8]{1,0:T(8,128)}) %reduce-scatter.10.cloned.1.call-update) | async-done | bytes 1040
  287.3 77.9 %all-gather.1 = f32[32,32,8]{1,2,0:T(8,128)S(1)} all-gather(f32[1,32,8]{1,2,0:T(8,128)S(1)} %divide_bitcast_fusion.3), channel_id=1, replica_groups=mesh['orig'=32,'dest'=16] {'orig'}, dimensions={0}, use_global_device_ids=true | all-gather | bytes 33792 | tf_op jit(solution)/shard_map/all_gather | solution.py:47
  365.4 28.4 %while.61 = (s32[]{:T(128)}, f32[8,512]{1,0:T(8,128)S(1)}, f32[8]{0:T(128)S(1)}, bf16[512,1024]{1,0:T(8,128)(2,1)S(1)}, f32[8,1024]{1,0:T(8,128)S(1)}, /*index=5*/s32[]{:T(128)}, s32[]{:T(128)}) while((s32[]{:T(128)}, f32[8,512]{1,0:T(8,128)S(1)}, f32[8]{0:T(128)S(1)}, bf16[512,1024]{1,0:T(8,128)(2,1)S(1)}, f32[8,1024]{1,0:T(8,128)S(1)}, ...), condition=%wide.region_7.8_spmd, body=%wide.region_6.7_spmd.sunk | while | flops 7340035 | bytes 1058925 | solution.py:50
  366.8 2.1 fusion.71
  393.9 84.1 %psum.50 = f32[8,512]{1,0:T(8,128)S(1)} all-reduce(f32[8,512]{1,0:T(8,128)S(1)} %get-tuple-element.165), channel_id=1, replica_groups=mesh['orig'=32,'dest'=16] {'dest'}, use_global_device_ids=true, to_apply=%region_8.9 | all-reduce | flops 4096 | bytes 32768 | tf_op jit(solution)/shard_map/psum | solution.py:51
  478.8 76.4 %psum.51 = f32[]{:T(128)} all-reduce(f32[]{:T(128)} %get-tuple-element.234), channel_id=1, replica_groups=mesh['orig'=32,'dest'=16] {'orig'}, use_global_device_ids=true, to_apply=%region_11.12 | all-reduce | flops 1 | bytes 8 | tf_op jit(solution)/shard_map/psum | solution.py:17
  556.0 21.4 %while.62 = (s32[]{:T(128)}, f32[8,1024]{1,0:T(8,128)S(1)}, f32[8,512]{1,0:T(8,128)S(1)}, f32[8]{0:T(128)S(1)}, bf16[512,1024]{1,0:T(8,128)(2,1)S(1)}, /*index=5*/s32[]{:T(128)}, s32[]{:T(128)}) while((s32[]{:T(128)}, f32[8,1024]{1,0:T(8,128)S(1)}, f32[8,512]{1,0:T(8,128)S(1)}, f32[8]{0:T(128)S(1)}, bf16[512,1024]{1,0:T(8,128)(2,1)S(1)}, ...), condition=%wide.region_13.14_spmd, body=%wide.region_12.13_spmd.sunk | while | flops 7340035 | bytes 1063021 | solution.py:40
  578.5 73.7 %all-gather.2 = f32[32,1,512]{2,1,0:T(1,128)S(1)} all-gather(f32[1,1,512]{2,1,0:T(1,128)S(1)} %bitcast.114), channel_id=1, replica_groups=mesh['orig'=32,'dest'=16] {'orig'}, dimensions={0}, use_global_device_ids=true | all-gather | bytes 67584 | tf_op jit(solution)/shard_map/all_gather | solution.py:21
  652.2 76.7 %reduce-scatter.12.cloned.1.call-done = f32[32,8]{1,0:T(8,128)} async-done(((f32[1024,8]{1,0:T(8,128)}), f32[32,8]{1,0:T(8,128)}) %reduce-scatter.12.cloned.1.call-update) | async-done | bytes 1040
  729.8 77.9 %all-gather.3 = f32[32,32,8]{1,2,0:T(8,128)S(1)} all-gather(f32[1,32,8]{1,2,0:T(8,128)S(1)} %divide_bitcast_fusion.2), channel_id=1, replica_groups=mesh['orig'=32,'dest'=16] {'orig'}, dimensions={0}, use_global_device_ids=true | all-gather | bytes 33792 | tf_op jit(solution)/shard_map/all_gather | solution.py:47
  807.8 28.4 %while.63 = (s32[]{:T(128)}, f32[8,512]{1,0:T(8,128)S(1)}, f32[8]{0:T(128)S(1)}, bf16[512,1024]{1,0:T(8,128)(2,1)S(1)}, f32[8,1024]{1,0:T(8,128)S(1)}, /*index=5*/s32[]{:T(128)}, s32[]{:T(128)}) while((s32[]{:T(128)}, f32[8,512]{1,0:T(8,128)S(1)}, f32[8]{0:T(128)S(1)}, bf16[512,1024]{1,0:T(8,128)(2,1)S(1)}, f32[8,1024]{1,0:T(8,128)S(1)}, ...), condition=%wide.region_16.17_spmd, body=%wide.region_15.16_spmd.sunk | while | flops 7340035 | bytes 1058925 | solution.py:50
  836.3 84.1 %psum.52 = f32[8,512]{1,0:T(8,128)S(1)} all-reduce(f32[8,512]{1,0:T(8,128)S(1)} %get-tuple-element.167), channel_id=1, replica_groups=mesh['orig'=32,'dest'=16] {'dest'}, use_global_device_ids=true, to_apply=%region_17.18 | all-reduce | flops 4096 | bytes 32768 | tf_op jit(solution)/shard_map/psum | solution.py:51
  921.1 76.4 %psum.53 = f32[]{:T(128)} all-reduce(f32[]{:T(128)} %get-tuple-element.232), channel_id=1, replica_groups=mesh['orig'=32,'dest'=16] {'orig'}, use_global_device_ids=true, to_apply=%region_20.21 | all-reduce | flops 1 | bytes 8 | tf_op jit(solution)/shard_map/psum | solution.py:17
  998.3 21.4 %while.64 = (s32[]{:T(128)}, f32[8,1024]{1,0:T(8,128)S(1)}, f32[8,512]{1,0:T(8,128)S(1)}, f32[8]{0:T(128)S(1)}, bf16[512,1024]{1,0:T(8,128)(2,1)S(1)}, /*index=5*/s32[]{:T(128)}, s32[]{:T(128)}) while((s32[]{:T(128)}, f32[8,1024]{1,0:T(8,128)S(1)}, f32[8,512]{1,0:T(8,128)S(1)}, f32[8]{0:T(128)S(1)}, bf16[512,1024]{1,0:T(8,128)(2,1)S(1)}, ...), condition=%wide.region_22.23_spmd, body=%wide.region_21.22_spmd.sunk | while | flops 7340035 | bytes 1063021 | solution.py:40
  1020.7 73.7 %all-gather.4 = f32[32,1,512]{2,1,0:T(1,128)S(1)} all-gather(f32[1,1,512]{2,1,0:T(1,128)S(1)} %bitcast.115), channel_id=1, replica_groups=mesh['orig'=32,'dest'=16] {'orig'}, dimensions={0}, use_global_device_ids=true | all-gather | bytes 67584 | tf_op jit(solution)/shard_map/all_gather | solution.py:21
  1094.5 76.8 %reduce-scatter.14.cloned.1.call-done = f32[32,8]{1,0:T(8,128)} async-done(((f32[1024,8]{1,0:T(8,128)}), f32[32,8]{1,0:T(8,128)}) %reduce-scatter.14.cloned.1.call-update) | async-done | bytes 1040
  1172.2 78.1 %all-gather.5 = f32[32,32,8]{1,2,0:T(8,128)S(1)} all-gather(f32[1,32,8]{1,2,0:T(8,128)S(1)} %get-tuple-element.237), channel_id=1, replica_groups=mesh['orig'=32,'dest'=16] {'orig'}, dimensions={0}, use_global_device_ids=true | all-gather | bytes 33792 | tf_op jit(solution)/shard_map/all_gather | solution.py:47
  1250.4 27.5 %while.65 = (s32[]{:T(128)}, f32[8,512]{1,0:T(8,128)S(1)}, f32[8]{0:T(128)S(1)}, bf16[512,1024]{1,0:T(8,128)(2,1)S(1)}, f32[8,1024]{1,0:T(8,128)S(1)}, /*index=5*/s32[]{:T(128)}, s32[]{:T(128)}) while((s32[]{:T(128)}, f32[8,512]{1,0:T(8,128)S(1)}, f32[8]{0:T(128)S(1)}, bf16[512,1024]{1,0:T(8,128)(2,1)S(1)}, f32[8,1024]{1,0:T(8,128)S(1)}, ...), condition=%wide.region_25.26_spmd, body=%wide.region_24.25_spmd.sunk | while | flops 7340035 | bytes 1058925 | solution.py:50
  1277.8 84.1 %psum.54 = f32[8,512]{1,0:T(8,128)S(1)} all-reduce(f32[8,512]{1,0:T(8,128)S(1)} %get-tuple-element.169), channel_id=1, replica_groups=mesh['orig'=32,'dest'=16] {'dest'}, use_global_device_ids=true, to_apply=%region_26.27 | all-reduce | flops 4096 | bytes 32768 | tf_op jit(solution)/shard_map/psum | solution.py:51
  1362.7 76.4 %psum.55 = f32[]{:T(128)} all-reduce(f32[]{:T(128)} %get-tuple-element.230), channel_id=1, replica_groups=mesh['orig'=32,'dest'=16] {'orig'}, use_global_device_ids=true, to_apply=%region_29.30 | all-reduce | flops 1 | bytes 8 | tf_op jit(solution)/shard_map/psum | solution.py:17
  1439.8 74.0 %all-gather.6 = f32[32,32,8]{1,2,0:T(8,128)S(1)} all-gather(f32[1,32,8]{1,2,0:T(8,128)S(1)} %get-tuple-element.236), channel_id=1, replica_groups=mesh['orig'=32,'dest'=16] {'orig'}, dimensions={0}, use_global_device_ids=true | all-gather | bytes 33792 | tf_op jit(solution)/shard_map/all_gather | solution.py:48
  (196 shorter events, 121.5 us)
Async XLA Ops:
  7.2 279.3 %reduce-scatter.10.cloned.1.call-start = ((), (), s32[]{:S(2)}) async-start(), calls=%async_computation.3 | async-start | bytes 540672
  128.6 1.1 copy-start.1
  128.6 236.8 %copy-start.4 = (f32[8]{0:T(128)S(1)}, f32[8]{0:T(128)}, u32[]{:S(2)}) copy-start(f32[8]{0:T(128)} %get-tuple-element.568) | copy-start | bytes 100
  128.6 236.8 %copy-start.5 = (bf16[512,1024]{1,0:T(8,128)(2,1)S(1)}, bf16[512,1024]{1,0:T(8,128)(2,1)}, u32[]{:S(2)}) copy-start(bf16[512,1024]{1,0:T(8,128)(2,1)} %get-tuple-element.573) | copy-start | bytes 3145732
  129.7 599.2 %reduce-scatter.12.cloned.1.call-start = ((), (), s32[]{:S(2)}) async-start(), calls=%async_computation.4 | async-start | bytes 540672
  365.4 112.6 %copy-start = (f32[8,512]{1,0:T(8,128)S(1)}, f32[8,512]{1,0:T(8,128)}, u32[]{:S(2)}) copy-start(f32[8,512]{1,0:T(8,128)} %param.20) | copy-start | bytes 49156
  365.4 112.7 %copy-start.2 = (f32[512]{0:T(512)S(1)}, f32[512]{0:T(512)}, u32[]{:S(2)}) copy-start(f32[512]{0:T(512)} %param.22) | copy-start | bytes 6148
  365.4 112.7 %copy-start.3 = (f32[512]{0:T(512)S(1)}, f32[512]{0:T(512)}, u32[]{:S(2)}) copy-start(f32[512]{0:T(512)} %param.23) | copy-start | bytes 6148
  578.4 592.9 %reduce-scatter.14.cloned.1.call-start = ((), (), s32[]{:S(2)}) async-start(), calls=%async_computation.5 | async-start | bytes 540672
Sparse Core Ops, SparseCore 0:
  129.8 156.6 reduce-scatter.9
  578.5 150.3 reduce-scatter.11
  1020.9 150.4 reduce-scatter.13
where the time goes:
time: 1520 us
  blocking collectives  1090 us (72%)
  waiting for transfers between devices  234 us (15%)
  matrix products  92.8 us (6%)
  local copies, waits for them, and re-layouts  44.5 us (3%)
  loops' own time  33.1 us (2%)
  between operations  16.7 us (1%)
    psum x4, blocking collectives, settle(): world_income = lax.psum(jnp.sum(raw_wage * workers), 'orig')  310 us
    psum x3, blocking collectives, on_device(): sector_sales = lax.psum(partial_sales, 'dest')  252 us
    all_gather x3, blocking collectives, on_device(): lax.all_gather(own_spending / price_part, 'orig', axis=1, tiled=True)  234 us
    unnamed x6, waiting for transfers between devices  234 us
    all_gather x3, blocking collectives, settle(): incomes = lax.all_gather(wage * workers, 'orig', axis=0, tiled=True)  224 us
    all_gather x1, blocking collectives, on_device(): lax.all_gather(-jnp.log(price_part) / elasticity[:, None], 'orig', axis=1...  74 us
    dot_general x24, matrix products, sales_term(): return jnp.dot(kernel_of(pair[0]), pair[1], precision=lax.Precision.HIGHEST)  50.9 us
    dot_general x24, matrix products, phi_term(): return jnp.dot(pair[1], kernel_of(pair[0]), precision=lax.Precision.HIGHEST)  41.9 us
  transfers between devices with their start and end apart: 3, of which 3 were waited for; matrix products, arithmetic and copies ran while one was open for 0% of the time, Pallas kernels for 0%

commit v1 on v0

--- a/solution.py
+++ b/solution.py
@@ -1,12 +1,220 @@
+import functools
+
 import jax
 import jax.numpy as jnp
 from jax import lax
+from jax.experimental import pallas as pl
+from jax.experimental.pallas import tpu as pltpu
 from jax.sharding import PartitionSpec as P
 
 ITERS = 3
-
-
-def on_device(log_cost, elasticity, productivity, preference, workers, start_wage):
+LANES = 128
+LOG2E = 1.4426950408889634
+CENTRE = 2048.0
+SMALLEST, LARGEST = 1e-36, 1e30
+
+
+def f32(*shape):
+    return jax.ShapeDtypeStruct(shape, jnp.float32)
+
+
+def pick(vector_ref, count):
+    row = lax.broadcasted_iota(jnp.int32, (count, LANES), 0)
+    out = jnp.zeros((count, LANES), jnp.float32)
+    for j in range(count):
+        out = jnp.where(row == j, vector_ref[j], out)
+    return out
+
+
+def total_of(x):
+    return jnp.sum(jnp.sum(x, axis=0, keepdims=True), axis=1, keepdims=True)
+
+
+def next_wage(wage_ref, workers_ref, sales_ref):
+    wage, workers = wage_ref[...], workers_ref[...]
+    revenue = jnp.sum(sales_ref[...], axis=0)
+    return wage * jnp.sqrt(revenue / (wage * workers))
+
+
+def supply_of(slopes, productivity_ref, wage):
+    log_wage = jnp.log(wage)
+    pieces = wage.shape[0]
+    return [
+        productivity_ref[:, p * LANES:(p + 1) * LANES] * jnp.exp(-slopes * log_wage[p:p + 1])
+        for p in range(pieces)
+    ]
+
+
+def prepare(place_ref, slope_ref, productivity_ref, workers_ref, wage, send_ref, spread_ref):
+    sectors, rows = productivity_ref.shape
+    pieces = rows // LANES
+    own = send_ref.shape[1] - 2
+    owners = sectors // own
+    blocks = send_ref.shape[0] // owners
+    supply = supply_of(pick(slope_ref, sectors), productivity_ref, wage)
+    for p in range(pieces):
+        column = jnp.transpose(supply[p])
+        for r in range(0, LANES, 8):
+            for j in range(sectors):
+                spread_ref[j, p * LANES + r:p * LANES + r + 8, :] = jnp.broadcast_to(column[r:r + 8, j:j + 1], (8, LANES))
+    least = functools.reduce(jnp.minimum, supply)
+    least = jnp.min(jnp.min(least, axis=0, keepdims=True), axis=1, keepdims=True)
+    income = wage * workers_ref[...]
+    world = jnp.where(least > SMALLEST, jnp.sum(income, axis=0, keepdims=True), jnp.nan)
+    for k in range(blocks):
+        piece = income[k % pieces:k % pieces + 1] * place_ref[k // pieces]
+        for q in range(owners):
+            send_ref[k * owners + q, own:own + 1, :] = piece
+            send_ref[k * owners + q, own + 1:own + 2, :] = world
+
+
+def send_phi(totals_ref, send_ref):
+    sectors = totals_ref.shape[0]
+    own = send_ref.shape[1] - 2
+    owners = sectors // own
+    for j in range(sectors):
+        for k in range(send_ref.shape[0] // owners):
+            piece = jnp.sum(totals_ref[j, :, k * LANES:(k + 1) * LANES], axis=0, keepdims=True)
+            send_ref[k * owners + j // own, j % own:j % own + 1, :] = piece
+
+
+def first_phi_kernel(place_ref, slope_ref, cost_ref, productivity_ref, workers_ref, wage_ref, send_ref, spread_ref, trade_ref, totals_ref):
+    sectors, rows = productivity_ref.shape
+    columns = cost_ref.shape[1]
+    prepare(place_ref, slope_ref, productivity_ref, workers_ref, wage_ref[...], send_ref, spread_ref)
+    scale = [slope_ref[j] * -LOG2E for j in range(sectors)]
+    width = 2
+    for first in range(0, columns // LANES, width):
+        at_lanes = [slice((first + k) * LANES, (first + k + 1) * LANES) for k in range(width)]
+
+        def step(block, totals):
+            totals = list(totals)
+            at = pl.ds(pl.multiple_of(block * 16, 16), 16)
+            for k in range(width):
+                cost = cost_ref[at, at_lanes[k]].astype(jnp.float32)
+                for j in range(sectors):
+                    trade = jnp.exp2(cost * scale[j])
+                    trade_ref[j, at, at_lanes[k]] = trade
+                    term = trade * spread_ref[j, at, :]
+                    totals[j * width + k] += term[:8] + term[8:]
+            return tuple(totals)
+
+        zero = jnp.zeros((8, LANES), jnp.float32)
+        totals = lax.fori_loop(0, rows // 16, step, (zero,) * (sectors * width), unroll=2)
+        for j in range(sectors):
+            for k in range(width):
+                totals_ref[j, :, at_lanes[k]] = totals[j * width + k]
+    send_phi(totals_ref, send_ref)
+
+
+def phi_kernel(place_ref, slope_ref, trade_ref, productivity_ref, workers_ref, wage_ref, sales_ref, send_ref, spread_ref, new_wage_ref, totals_ref):
+    sectors, rows, columns = trade_ref.shape
+    blocks = columns // LANES
+    wage = next_wage(wage_ref, workers_ref, sales_ref)
+    new_wage_ref[...] = wage
+    prepare(place_ref, slope_ref, productivity_ref, workers_ref, wage, send_ref, spread_ref)
+    for j in range(sectors):
+        def step(block, totals):
+            at = pl.ds(pl.multiple_of(block * 8, 8), 8)
+            weight = spread_ref[j, at, :]
+            return tuple(totals[k] + trade_ref[j, at, k * LANES:(k + 1) * LANES] * weight for k in range(blocks))
+
+        zero = jnp.zeros((8, LANES), jnp.float32)
+        totals = lax.fori_loop(0, rows // 8, step, (zero,) * blocks, unroll=16)
+        for k in range(blocks):
+            totals_ref[j, :, k * LANES:(k + 1) * LANES] = totals[k]
+    send_phi(totals_ref, send_ref)
+
+
+def ratio_kernel(last, cells, place_ref, slope_ref, preference_ref, got_ref, send_ref):
+    sectors = preference_ref.shape[0]
+    own = got_ref.shape[1] - 2
+    got = jnp.sum(got_ref[...], axis=0)
+    income = got[own:own + 1]
+    world = jnp.sum(got[own + 1:own + 2], axis=1, keepdims=True)
+    factor = cells / world
+    at = pl.multiple_of(place_ref[0] * LANES, LANES)
+    preference = preference_ref[:, pl.ds(at, LANES)]
+    spend_all = jnp.sum(preference, axis=0, keepdims=True)
+    row = lax.broadcasted_iota(jnp.int32, (sectors, LANES), 0)
+    centred = factor * CENTRE
+    for s in range(own):
+        sector = place_ref[1] * own + s
+        wanted = jnp.sum(jnp.where(row == sector, preference, 0.0), axis=0, keepdims=True)
+        phi = got[s:s + 1]
+        ratio = wanted / spend_all * income / phi
+        ratio = jnp.where(phi < LARGEST, ratio * (centred * centred), jnp.nan)
+        send_ref[:, s, :] = jnp.broadcast_to(ratio, (send_ref.shape[0], LANES))
+        if last:
+            price = jnp.log(factor) - jnp.log(phi) / slope_ref[sector]
+            send_ref[:, own + s, :] = jnp.broadcast_to(price, (send_ref.shape[0], LANES))
+
+
+def sales_kernel(last, trade_ref, spread_ref, ratio_ref, send_ref, *rest):
+    total_ref = rest[-1]
+    sectors, rows, columns = trade_ref.shape
+    blocks = columns // LANES
+    owners = ratio_ref.shape[0] // blocks
+    own = sectors // owners
+    if last:
+        price_ref = rest[0]
+        for k in range(blocks):
+            for j in range(sectors):
+                price_ref[j:j + 1, k * LANES:(k + 1) * LANES] = ratio_ref[k * owners + j // own, own + j % own:own + j % own + 1, :]
+    for j in range(sectors):
+        ratios = [
+            jnp.broadcast_to(ratio_ref[k * owners + j // own, j % own:j % own + 1, :], (8, LANES))
+            for k in range(blocks)
+        ]
+
+        def step(block, carry):
+            at = pl.ds(pl.multiple_of(block * 8, 8), 8)
+            terms = [trade_ref[j, at, k * LANES:(k + 1) * LANES] * ratios[k] for k in range(blocks)]
+            while len(terms) > 1:
+                terms = [a + b for a, b in zip(terms[::2], terms[1::2])]
+            total = terms[0] * spread_ref[j, at, :]
+            total_ref[at, :] = total if j == 0 else total_ref[at, :] + total
+            return carry
+
+        lax.fori_loop(0, rows // 8, step, 0, unroll=8)
+    for p in range(rows // LANES):
+        piece = jnp.sum(jnp.transpose(total_ref[p * LANES:(p + 1) * LANES, :]), axis=0, keepdims=True)
+        send_ref[:, p, :] = jnp.broadcast_to(piece, (send_ref.shape[0], LANES))
+
+
+def settle_kernel(workers_ref, wage_ref, sales_ref, raw_ref, send_ref):
+    raw = next_wage(wage_ref, workers_ref, sales_ref)
+    raw_ref[...] = raw
+    world = jnp.sum(raw * workers_ref[...], axis=0, keepdims=True)
+    send_ref[:, 0, :] = jnp.broadcast_to(world, (send_ref.shape[0], LANES))
+
+
+def finish_kernel(cells, raw_ref, got_ref, wage_ref, world_ref):
+    world = total_of(got_ref[:, 0, :])
+    wage_ref[...] = raw_ref[...] * (cells / world)
+    world_ref[...] = jnp.broadcast_to(world, (1, LANES))
+
+
+VM = pl.BlockSpec(memory_space=pltpu.VMEM)
+SM = pl.BlockSpec(memory_space=pltpu.SMEM)
+
+
+def call(body, out_shape, scalars, arrays, scratch=()):
+    return pl.pallas_call(
+        body,
+        out_shape=tuple(out_shape),
+        in_specs=[SM] * len(scalars) + [VM] * len(arrays),
+        out_specs=(VM,) * len(out_shape),
+        scratch_shapes=[pltpu.VMEM(shape, jnp.float32) for shape in scratch],
+        compiler_params=pltpu.CompilerParams(vmem_limit_bytes=16 << 20),
+    )(*scalars, *arrays)
+
+
+def exchange(x, axis):
+    return lax.all_to_all(x, axis, 0, 0, tiled=True)
+
+
+def careful(log_cost, elasticity, productivity, preference, workers, start_wage):
     rows = log_cost.shape[0]
     columns = log_cost.shape[1]
     cells = rows * lax.axis_size("orig")
@@ -55,6 +263,63 @@
     return (wage, log_price)
 
 
+def fast(log_cost, elasticity, productivity, preference, workers, start_wage):
+    sectors, rows = productivity.shape
+    columns = log_cost.shape[1]
+    across, along = lax.axis_size("orig"), lax.axis_size("dest")
+    cells = float(rows * across)
+    blocks, pieces = columns // LANES, rows // LANES
+    owners = across // blocks
+    own = sectors // owners
+    orig, dest = lax.axis_index("orig"), lax.axis_index("dest")
+    part = orig - dest * (columns // rows)
+    place = jnp.stack([orig // owners, orig % owners]).astype(jnp.int32)
+    here = (part == jnp.arange(columns // rows)).astype(jnp.float32)
+    workers = workers.reshape(pieces, LANES)
+    wage = start_wage.reshape(pieces, LANES)
+    sales = trade = None
+    for step in range(ITERS):
+        last = step + 1 == ITERS
+        outs = [f32(across, own + 2, LANES), f32(sectors, rows, LANES)]
+        scratch = [(sectors, 8, columns)]
+        if step == 0:
+            send, spread, trade = call(
+                first_phi_kernel, outs + [f32(sectors, rows, columns)], [here, elasticity],
+                [log_cost, productivity, workers, wage], scratch,
+            )
+        else:
+            send, spread, wage = call(
+                phi_kernel, outs + [f32(pieces, LANES)], [here, elasticity],
+                [trade, productivity, workers, wage, sales], scratch,
+            )
+        got = exchange(send, "orig")
+        ratio, = call(
+            functools.partial(ratio_kernel, last, cells),
+            [f32(across, 2 * own if last else own, LANES)],
+            [place, elasticity],
+            [preference, got],
+        )
+        ratio = exchange(ratio, "orig")
+        made = call(
+            functools.partial(sales_kernel, last),
+            [f32(along, pieces, LANES)] + ([f32(sectors, columns)] if last else []),
+            [],
+            [trade, spread, ratio],
+            [(rows, LANES)],
+        )
+        sales = exchange(made[0], "dest")
+    log_price = made[1]
+    raw, send = call(settle_kernel, [f32(pieces, LANES), f32(across, 1, LANES)], [], [workers, wage, sales])
+    got = exchange(send, "orig")
+    wage, world = call(functools.partial(finish_kernel, cells), [f32(pieces, LANES), f32(1, LANES)], [], [raw, got])
+    return wage.reshape(rows), log_price, world[0, 0]
+
+
+def on_device(*args):
+    wage, log_price, world = fast(*args)
+    return lax.cond(jnp.isfinite(world), lambda: (wage, log_price), lambda: careful(*args))
+
+
 def solution(mesh):
     return jax.shard_map(
         on_device,

time: 1520 us -> 197 us (0.13)
  the two profiles are of different devices: /device:TPU:8 before, /device:TPU:1 now
where the time goes in v1:
time: 197 us
  blocking collectives  113 us (57%)
  Pallas kernels  22.1 us (11%)
  waiting for transfers between devices  18.1 us (9%)
  starting transfers between devices  17.3 us (9%)
  between operations  14.2 us (7%)
  local copies, waits for them, and re-layouts  11.5 us (6%)
    all_to_all x8, blocking collectives, exchange(): return lax.all_to_all(x, axis, 0, 0, tiled=True)  113 us
    pallas_call x11, Pallas kernels, call(): pl.pallas_call(body, out_shape=tuple(out_shape), in_specs=[SM] * len(scal...  22.1 us
    all_to_all x2, waiting for transfers between devices, exchange(): return lax.all_to_all(x, axis, 0, 0, tiled=True)  18.1 us
    all_to_all x2, starting transfers between devices, exchange(): return lax.all_to_all(x, axis, 0, 0, tiled=True)  17.3 us
    unnamed x18, local copies, waits for them, and re-layouts  11.5 us
  transfers between devices with their start and end apart: 2, of which 2 were waited for; matrix products, arithmetic and copies ran while one was open for 0% of the time, Pallas kernels for 0%

profile of v1, /device:TPU:1, one launch (start us, length us, event | category | flops | bytes accessed | tf_op | source)
XLA Modules:
  0.0 196.6 jit_solution(783204498013647777)
XLA Ops:
  7.2 6.6 %shard_map.81 = (f32[32,4,128]{2,1,0:T(4,128)}, f32[8,512,128]{2,1,0:T(8,128)S(1)}, f32[8,512,1024]{2,1,0:T(8,128)S(1)}) custom-call(f32[2]{0:T(128)S(1)} %compare_convert_fusion.place_ref, f32[8]{0:T(128)} %slope_ref.11, bf16[512,1024]{1,0:T(8,128)(2,1)} %cost_ref.1, f32[8,512]{1,0:T(8,128)} %productivity_ref.5, f32[4,128]{1,0:T(4,128)} %bitcast.111, ...), custom_call_target="tpu_custom_call" | custom-call | tf_op jit(solution)/shard_map/pallas_call | solution.py:203
  13.8 5.7 %copy-done = f32[8,512,1024]{2,1,0:T(8,128)} copy-done((f32[8,512,1024]{2,1,0:T(8,128)}, f32[8,512,1024]{2,1,0:T(8,128)S(1)}, u32[]{:S(2)}) %copy-start) | copy-done | bytes 16777240
  19.5 13.5 %all-to-all-start = ((f32[32,4,128]{2,1,0:T(4,128)}), f32[32,4,128]{2,1,0:T(4,128)S(1)}, u32[]{:S(2)}, u32[]{:S(2)}) async-start(f32[32,4,128]{2,1,0:T(4,128)} %get-tuple-element.208), calls=%async_computation.3 | async-start | bytes 131072 | tf_op jit(solution)/shard_map/all_to_all | solution.py:214
  33.0 0.1 pad_add_fusion.place_ref
  33.0 9.1 %all-to-all-done.got_ref = f32[32,4,128]{2,1,0:T(4,128)S(1)} async-done(((f32[32,4,128]{2,1,0:T(4,128)}), f32[32,4,128]{2,1,0:T(4,128)S(1)}, u32[]{:S(2)}, u32[]{:S(2)}) %all-to-all-start) | async-done | bytes 65568 | tf_op jit(solution)/shard_map/all_to_all | solution.py:214
  42.1 0.9 shard_map.82
  43.0 12.0 %all_to_all.50.ratio_ref = f32[32,2,128]{2,1,0:T(2,128)S(1)} all-to-all(f32[32,2,128]{2,1,0:T(2,128)S(1)} %shard_map.82), channel_id=1, replica_groups=mesh['orig'=32,'dest'=16] {'orig'}, dimensions={0} | all-to-all | bytes 65536 | tf_op jit(solution)/shard_map/all_to_all | solution.py:214
  55.0 5.8 %copy-done.1 = f32[8,512,1024]{2,1,0:T(8,128)S(1)} copy-done((f32[8,512,1024]{2,1,0:T(8,128)S(1)}, f32[8,512,1024]{2,1,0:T(8,128)}, u32[]{:S(2)}) %copy-start.1) | copy-done | bytes 16777240
  60.8 0.0 copy-start.8
  60.8 1.8 shard_map.83
  62.6 23.1 %all_to_all.51.sales_ref = f32[16,4,128]{2,1,0:T(4,128)S(1)} all-to-all(f32[16,4,128]{2,1,0:T(4,128)S(1)} %shard_map.83), channel_id=1, replica_groups=mesh['orig'=32,'dest'=16] {'dest'}, dimensions={0} | all-to-all | bytes 65536 | tf_op jit(solution)/shard_map/all_to_all | solution.py:214
  85.7 0.0 copy-done.2
  85.7 0.0 copy-done.3
  85.7 0.0 copy-done.6
  85.7 0.0 copy-start.5
  85.7 3.0 %shard_map.84 = (f32[32,4,128]{2,1,0:T(4,128)S(1)}, f32[8,512,128]{2,1,0:T(8,128)S(1)}, f32[4,128]{1,0:T(4,128)S(1)}) custom-call(f32[2]{0:T(128)S(1)} %compare_convert_fusion.place_ref, f32[8]{0:T(128)S(1)} %copy-done.8, f32[8,512,1024]{2,1,0:T(8,128)S(1)} %copy-done.2, f32[8,512]{1,0:T(8,128)S(1)} %copy-done.3, f32[4,128]{1,0:T(4,128)S(1)} %bitcast.112, ...), custom_call_target="tpu_custom_call" | custom-call | tf_op jit(solution)/shard_map/pallas_call | solution.py:203
  88.7 12.2 %all_to_all.52.got_ref = f32[32,4,128]{2,1,0:T(4,128)S(1)} all-to-all(f32[32,4,128]{2,1,0:T(4,128)S(1)} %get-tuple-element.211), channel_id=1, replica_groups=mesh['orig'=32,'dest'=16] {'orig'}, dimensions={0} | all-to-all | bytes 131072 | tf_op jit(solution)/shard_map/all_to_all | solution.py:214
  100.9 0.7 shard_map.85
  101.6 12.0 %all_to_all.53.ratio_ref = f32[32,2,128]{2,1,0:T(2,128)S(1)} all-to-all(f32[32,2,128]{2,1,0:T(2,128)S(1)} %shard_map.85), channel_id=1, replica_groups=mesh['orig'=32,'dest'=16] {'orig'}, dimensions={0} | all-to-all | bytes 65536 | tf_op jit(solution)/shard_map/all_to_all | solution.py:214
  113.6 1.9 shard_map.86
  115.4 14.8 %all_to_all.54.sales_ref = f32[16,4,128]{2,1,0:T(4,128)S(1)} all-to-all(f32[16,4,128]{2,1,0:T(4,128)S(1)} %shard_map.86), channel_id=1, replica_groups=mesh['orig'=32,'dest'=16] {'dest'}, dimensions={0} | all-to-all | bytes 65536 | tf_op jit(solution)/shard_map/all_to_all | solution.py:214
  130.2 3.0 %shard_map.87 = (f32[32,4,128]{2,1,0:T(4,128)S(1)}, f32[8,512,128]{2,1,0:T(8,128)S(1)}, f32[4,128]{1,0:T(4,128)S(1)}) custom-call(f32[2]{0:T(128)S(1)} %compare_convert_fusion.place_ref, f32[8]{0:T(128)S(1)} %copy-done.8, f32[8,512,1024]{2,1,0:T(8,128)S(1)} %copy-done.2, f32[8,512]{1,0:T(8,128)S(1)} %copy-done.3, f32[4,128]{1,0:T(4,128)S(1)} %bitcast.113, ...), custom_call_target="tpu_custom_call" | custom-call | tf_op jit(solution)/shard_map/pallas_call | solution.py:203
  133.2 12.2 %all_to_all.55.got_ref = f32[32,4,128]{2,1,0:T(4,128)S(1)} all-to-all(f32[32,4,128]{2,1,0:T(4,128)S(1)} %get-tuple-element.214), channel_id=1, replica_groups=mesh['orig'=32,'dest'=16] {'orig'}, dimensions={0} | all-to-all | bytes 131072 | tf_op jit(solution)/shard_map/all_to_all | solution.py:214
  145.4 0.7 shard_map.88
  146.1 12.2 %all_to_all.56.ratio_ref = f32[32,4,128]{2,1,0:T(4,128)S(1)} all-to-all(f32[32,4,128]{2,1,0:T(4,128)S(1)} %shard_map.88), channel_id=1, replica_groups=mesh['orig'=32,'dest'=16] {'orig'}, dimensions={0} | all-to-all | bytes 131072 | tf_op jit(solution)/shard_map/all_to_all | solution.py:214
  158.3 2.3 %shard_map.89 = (f32[16,4,128]{2,1,0:T(4,128)S(1)}, f32[8,1024]{1,0:T(8,128)}) custom-call(f32[8,512,1024]{2,1,0:T(8,128)S(1)} %copy-done.2, f32[8,512,128]{2,1,0:T(8,128)S(1)} %get-tuple-element.213.spread_ref, f32[32,4,128]{2,1,0:T(4,128)S(1)} %all_to_all.56.ratio_ref), custom_call_target="tpu_custom_call" | custom-call | tf_op jit(solution)/shard_map/pallas_call | solution.py:203
  160.6 14.7 %all_to_all.57.sales_ref = f32[16,4,128]{2,1,0:T(4,128)S(1)} all-to-all(f32[16,4,128]{2,1,0:T(4,128)S(1)} %get-tuple-element.215), channel_id=1, replica_groups=mesh['orig'=32,'dest'=16] {'dest'}, dimensions={0} | all-to-all | bytes 65536 | tf_op jit(solution)/shard_map/all_to_all | solution.py:214
  175.3 0.6 shard_map.90
  176.0 3.9 %all-to-all-start.9 = ((f32[32,1,128]{2,1,0:T(1,128)}), f32[32,1,128]{2,1,0:T(1,128)S(1)}, u32[]{:S(2)}, u32[]{:S(2)}) async-start(f32[32,1,128]{2,1,0:T(1,128)} %get-tuple-element.217), calls=%async_computation.12 | async-start | bytes 32768 | tf_op jit(solution)/shard_map/all_to_all | solution.py:214
  179.8 9.0 %all-to-all-done.9.got_ref = f32[32,1,128]{2,1,0:T(1,128)S(1)} async-done(((f32[32,1,128]{2,1,0:T(1,128)}), f32[32,1,128]{2,1,0:T(1,128)S(1)}, u32[]{:S(2)}, u32[]{:S(2)}) %all-to-all-start.9) | async-done | bytes 16416 | tf_op jit(solution)/shard_map/all_to_all | solution.py:214
  188.8 0.7 shard_map.91
  189.5 0.2 conditional.1
  (12 shorter events, 0.0 us)
Async XLA Ops:
  13.8 5.7 %copy-start = (f32[8,512,1024]{2,1,0:T(8,128)}, f32[8,512,1024]{2,1,0:T(8,128)S(1)}, u32[]{:S(2)}) copy-start(f32[8,512,1024]{2,1,0:T(8,128)S(1)} %get-tuple-element.206.trade_ref) | copy-start | bytes 50331652
  19.5 22.6 %all-to-all-start = ((f32[32,4,128]{2,1,0:T(4,128)}), f32[32,4,128]{2,1,0:T(4,128)S(1)}, u32[]{:S(2)}, u32[]{:S(2)}) async-start(f32[32,4,128]{2,1,0:T(4,128)} %get-tuple-element.208), calls=%async_computation.3 | async-start | bytes 131072 | tf_op jit(solution)/shard_map/all_to_all | solution.py:214
  55.0 5.8 %copy-start.1 = (f32[8,512,1024]{2,1,0:T(8,128)S(1)}, f32[8,512,1024]{2,1,0:T(8,128)}, u32[]{:S(2)}) copy-start(f32[8,512,1024]{2,1,0:T(8,128)} %copy-done) | copy-start | bytes 50331652
  60.8 24.9 %copy-start.2 = (f32[8,512,1024]{2,1,0:T(8,128)S(1)}, f32[8,512,1024]{2,1,0:T(8,128)}, u32[]{:S(2)}) copy-start(f32[8,512,1024]{2,1,0:T(8,128)} %copy-done) | copy-start | bytes 50331652
  60.8 24.9 %copy-start.3 = (f32[8,512]{1,0:T(8,128)S(1)}, f32[8,512]{1,0:T(8,128)}, u32[]{:S(2)}) copy-start(f32[8,512]{1,0:T(8,128)} %productivity_ref.5) | copy-start | bytes 49156
  60.8 24.9 %copy-start.6 = (f32[512]{0:T(512)S(1)}, f32[512]{0:T(512)}, u32[]{:S(2)}) copy-start(f32[512]{0:T(512)} %param.24) | copy-start | bytes 6148
  60.8 24.9 %copy-start.7 = (f32[512]{0:T(512)S(1)}, f32[512]{0:T(512)}, u32[]{:S(2)}) copy-start(f32[512]{0:T(512)} %param.25) | copy-start | bytes 6148
  60.8 24.9 %copy-start.8 = (f32[8]{0:T(128)S(1)}, f32[8]{0:T(128)}, u32[]{:S(2)}) copy-start(f32[8]{0:T(128)} %slope_ref.11) | copy-start | bytes 100
  85.7 15.2 %copy-start.5 = (f32[8,1024]{1,0:T(8,128)S(1)}, f32[8,1024]{1,0:T(8,128)}, u32[]{:S(2)}) copy-start(f32[8,1024]{1,0:T(8,128)} %preference_ref.5) | copy-start | bytes 98308
  158.3 31.2 %copy-start.4 = (bf16[512,1024]{1,0:T(8,128)(2,1)S(1)}, bf16[512,1024]{1,0:T(8,128)(2,1)}, u32[]{:S(2)}) copy-start(bf16[512,1024]{1,0:T(8,128)(2,1)} %cost_ref.1) | copy-start | bytes 3145732
  176.0 12.8 %all-to-all-start.9 = ((f32[32,1,128]{2,1,0:T(1,128)}), f32[32,1,128]{2,1,0:T(1,128)S(1)}, u32[]{:S(2)}, u32[]{:S(2)}) async-start(f32[32,1,128]{2,1,0:T(1,128)} %get-tuple-element.217), calls=%async_computation.12 | async-start | bytes 32768 | tf_op jit(solution)/shard_map/all_to_all | solution.py:214

commit v2 on v1

--- a/solution.py
+++ b/solution.py
@@ -9,13 +9,18 @@
 
 ITERS = 3
 LANES = 128
-LOG2E = 1.4426950408889634
-CENTRE = 2048.0
-SMALLEST, LARGEST = 1e-36, 1e30
+CENTRE = 1024.0
+SMALLEST, LARGEST = 1e-32, 1e30
 
 
 def f32(*shape):
     return jax.ShapeDtypeStruct(shape, jnp.float32)
+
+
+def tree_sum(terms):
+    while len(terms) > 1:
+        terms = [a + b for a, b in zip(terms[::2], terms[1::2])]
+    return terms[0]
 
 
 def pick(vector_ref, count):
@@ -45,7 +50,22 @@
     ]
 
 
-def prepare(place_ref, slope_ref, productivity_ref, workers_ref, wage, send_ref, spread_ref):
+def spread_over_lanes(supply_ref, spread_ref):
+    sectors = supply_ref.shape[0]
+    row = lax.broadcasted_iota(jnp.int32, (sectors, sectors * LANES), 0)
+    lane = lax.broadcasted_iota(jnp.int32, (sectors, sectors * LANES), 1)
+    ones = jnp.where((lane >= row * LANES) & (lane < (row + 1) * LANES), 1.0, 0.0).astype(jnp.bfloat16)
+    rest, terms = supply_ref[...], []
+    for _ in range(3):
+        terms.append(rest.astype(jnp.bfloat16))
+        rest = rest - terms[-1].astype(jnp.float32)
+    spread_ref[...] = lax.dot_general(
+        jnp.concatenate(terms, axis=0), jnp.concatenate([ones] * 3, axis=0), (((0,), (0,)), ((), ())),
+        preferred_element_type=jnp.float32,
+    )
+
+
+def prepare(spot_ref, slope_ref, columns, productivity_ref, workers_ref, wage, send_ref, spread_ref, supply_ref):
     sectors, rows = productivity_ref.shape
     pieces = rows // LANES
     own = send_ref.shape[1] - 2
@@ -53,19 +73,20 @@
     blocks = send_ref.shape[0] // owners
     supply = supply_of(pick(slope_ref, sectors), productivity_ref, wage)
     for p in range(pieces):
-        column = jnp.transpose(supply[p])
-        for r in range(0, LANES, 8):
-            for j in range(sectors):
-                spread_ref[j, p * LANES + r:p * LANES + r + 8, :] = jnp.broadcast_to(column[r:r + 8, j:j + 1], (8, LANES))
+        supply_ref[:, p * LANES:(p + 1) * LANES] = supply[p]
+    spread_over_lanes(supply_ref, spread_ref)
     least = functools.reduce(jnp.minimum, supply)
     least = jnp.min(jnp.min(least, axis=0, keepdims=True), axis=1, keepdims=True)
     income = wage * workers_ref[...]
     world = jnp.where(least > SMALLEST, jnp.sum(income, axis=0, keepdims=True), jnp.nan)
-    for k in range(blocks):
-        piece = income[k % pieces:k % pieces + 1] * place_ref[k // pieces]
-        for q in range(owners):
-            send_ref[k * owners + q, own:own + 1, :] = piece
-            send_ref[k * owners + q, own + 1:own + 2, :] = world
+    part = spot_ref[0] - spot_ref[1] * (columns // rows)
+    for i in range(columns // rows):
+        here = income * jnp.where(part == i, 1.0, 0.0)
+        for p in range(pieces):
+            for q in range(owners):
+                at = (i * pieces + p) * owners + q
+                send_ref[at, own:own + 1, :] = here[p:p + 1]
+                send_ref[at, own + 1:own + 2, :] = world
 
 
 def send_phi(totals_ref, send_ref):
@@ -78,45 +99,40 @@
             send_ref[k * owners + j // own, j % own:j % own + 1, :] = piece
 
 
-def first_phi_kernel(place_ref, slope_ref, cost_ref, productivity_ref, workers_ref, wage_ref, send_ref, spread_ref, trade_ref, totals_ref):
+def first_phi_kernel(spot_ref, slope_ref, cost_ref, productivity_ref, workers_ref, wage_ref, send_ref, spread_ref, trade_ref, totals_ref, supply_ref):
     sectors, rows = productivity_ref.shape
     columns = cost_ref.shape[1]
-    prepare(place_ref, slope_ref, productivity_ref, workers_ref, wage_ref[...], send_ref, spread_ref)
-    scale = [slope_ref[j] * -LOG2E for j in range(sectors)]
-    width = 2
-    for first in range(0, columns // LANES, width):
-        at_lanes = [slice((first + k) * LANES, (first + k + 1) * LANES) for k in range(width)]
-
-        def step(block, totals):
-            totals = list(totals)
-            at = pl.ds(pl.multiple_of(block * 16, 16), 16)
-            for k in range(width):
-                cost = cost_ref[at, at_lanes[k]].astype(jnp.float32)
-                for j in range(sectors):
-                    trade = jnp.exp2(cost * scale[j])
-                    trade_ref[j, at, at_lanes[k]] = trade
-                    term = trade * spread_ref[j, at, :]
-                    totals[j * width + k] += term[:8] + term[8:]
-            return tuple(totals)
-
-        zero = jnp.zeros((8, LANES), jnp.float32)
-        totals = lax.fori_loop(0, rows // 16, step, (zero,) * (sectors * width), unroll=2)
-        for j in range(sectors):
-            for k in range(width):
-                totals_ref[j, :, at_lanes[k]] = totals[j * width + k]
+    prepare(spot_ref, slope_ref, columns, productivity_ref, workers_ref, wage_ref[...], send_ref, spread_ref, supply_ref)
+    slopes = [-slope_ref[j] for j in range(sectors)]
+    totals_ref[...] = jnp.zeros_like(totals_ref)
+    height = 32
+
+    def step(block, carry):
+        at = pl.ds(pl.multiple_of(block * height, height), height)
+        for k in range(columns // LANES):
+            lanes = slice(k * LANES, (k + 1) * LANES)
+            cost = cost_ref[at, lanes].astype(jnp.float32)
+            for j in range(sectors):
+                trade = jnp.exp(cost * slopes[j])
+                trade_ref[j, at, lanes] = trade
+                term = trade * spread_ref[at, j * LANES:(j + 1) * LANES]
+                totals_ref[j, :, lanes] += tree_sum([term[r:r + 8] for r in range(0, height, 8)])
+        return carry
+
+    lax.fori_loop(0, rows // height, step, 0)
     send_phi(totals_ref, send_ref)
 
 
-def phi_kernel(place_ref, slope_ref, trade_ref, productivity_ref, workers_ref, wage_ref, sales_ref, send_ref, spread_ref, new_wage_ref, totals_ref):
+def phi_kernel(spot_ref, slope_ref, trade_ref, productivity_ref, workers_ref, wage_ref, sales_ref, send_ref, spread_ref, new_wage_ref, totals_ref, supply_ref):
     sectors, rows, columns = trade_ref.shape
     blocks = columns // LANES
     wage = next_wage(wage_ref, workers_ref, sales_ref)
     new_wage_ref[...] = wage
-    prepare(place_ref, slope_ref, productivity_ref, workers_ref, wage, send_ref, spread_ref)
+    prepare(spot_ref, slope_ref, columns, productivity_ref, workers_ref, wage, send_ref, spread_ref, supply_ref)
     for j in range(sectors):
         def step(block, totals):
             at = pl.ds(pl.multiple_of(block * 8, 8), 8)
-            weight = spread_ref[j, at, :]
+            weight = spread_ref[at, j * LANES:(j + 1) * LANES]
             return tuple(totals[k] + trade_ref[j, at, k * LANES:(k + 1) * LANES] * weight for k in range(blocks))
 
         zero = jnp.zeros((8, LANES), jnp.float32)
@@ -126,20 +142,21 @@
     send_phi(totals_ref, send_ref)
 
 
-def ratio_kernel(last, cells, place_ref, slope_ref, preference_ref, got_ref, send_ref):
+def ratio_kernel(last, cells, spot_ref, slope_ref, preference_ref, got_ref, send_ref):
     sectors = preference_ref.shape[0]
     own = got_ref.shape[1] - 2
     got = jnp.sum(got_ref[...], axis=0)
     income = got[own:own + 1]
     world = jnp.sum(got[own + 1:own + 2], axis=1, keepdims=True)
     factor = cells / world
-    at = pl.multiple_of(place_ref[0] * LANES, LANES)
+    owners = sectors // own
+    at = pl.multiple_of(lax.div(spot_ref[0], owners) * LANES, LANES)
     preference = preference_ref[:, pl.ds(at, LANES)]
     spend_all = jnp.sum(preference, axis=0, keepdims=True)
     row = lax.broadcasted_iota(jnp.int32, (sectors, LANES), 0)
     centred = factor * CENTRE
     for s in range(own):
-        sector = place_ref[1] * own + s
+        sector = lax.rem(spot_ref[0], owners) * own + s
         wanted = jnp.sum(jnp.where(row == sector, preference, 0.0), axis=0, keepdims=True)
         phi = got[s:s + 1]
         ratio = wanted / spend_all * income / phi
@@ -170,9 +187,7 @@
         def step(block, carry):
             at = pl.ds(pl.multiple_of(block * 8, 8), 8)
             terms = [trade_ref[j, at, k * LANES:(k + 1) * LANES] * ratios[k] for k in range(blocks)]
-            while len(terms) > 1:
-                terms = [a + b for a, b in zip(terms[::2], terms[1::2])]
-            total = terms[0] * spread_ref[j, at, :]
+            total = tree_sum(terms) * spread_ref[at, j * LANES:(j + 1) * LANES]
             total_ref[at, :] = total if j == 0 else total_ref[at, :] + total
             return carry
 
@@ -269,34 +284,30 @@
     across, along = lax.axis_size("orig"), lax.axis_size("dest")
     cells = float(rows * across)
     blocks, pieces = columns // LANES, rows // LANES
-    owners = across // blocks
-    own = sectors // owners
-    orig, dest = lax.axis_index("orig"), lax.axis_index("dest")
-    part = orig - dest * (columns // rows)
-    place = jnp.stack([orig // owners, orig % owners]).astype(jnp.int32)
-    here = (part == jnp.arange(columns // rows)).astype(jnp.float32)
+    own = sectors * blocks // across
+    spot = jnp.stack([lax.axis_index("orig"), lax.axis_index("dest")]).astype(jnp.int32)
     workers = workers.reshape(pieces, LANES)
     wage = start_wage.reshape(pieces, LANES)
     sales = trade = None
     for step in range(ITERS):
         last = step + 1 == ITERS
-        outs = [f32(across, own + 2, LANES), f32(sectors, rows, LANES)]
-        scratch = [(sectors, 8, columns)]
+        outs = [f32(across, own + 2, LANES), f32(rows, sectors * LANES)]
+        scratch = [(sectors, 8, columns), (sectors, rows)]
         if step == 0:
             send, spread, trade = call(
-                first_phi_kernel, outs + [f32(sectors, rows, columns)], [here, elasticity],
+                first_phi_kernel, outs + [f32(sectors, rows, columns)], [spot, elasticity],
                 [log_cost, productivity, workers, wage], scratch,
             )
         else:
             send, spread, wage = call(
-                phi_kernel, outs + [f32(pieces, LANES)], [here, elasticity],
+                phi_kernel, outs + [f32(pieces, LANES)], [spot, elasticity],
                 [trade, productivity, workers, wage, sales], scratch,
             )
         got = exchange(send, "orig")
         ratio, = call(
             functools.partial(ratio_kernel, last, cells),
             [f32(across, 2 * own if last else own, LANES)],
-            [place, elasticity],
+            [spot, elasticity],
             [preference, got],
         )
         ratio = exchange(ratio, "orig")

time: 197 us -> 183 us (0.929)
  blocking collectives: 113 us -> 135 us
  starting transfers between devices: 17.3 us -> 3.85 us
  local copies, waits for them, and re-layouts: 11.5 us -> 0.02 us
  waiting for transfers between devices: 18.1 us -> 8.98 us
  Pallas kernels: 22.1 us -> 19.5 us
    all_to_all x8 -> x9, blocking collectives: 113 us -> 135 us  [exchange(): return lax.all_to_all(x, axis, 0, 0, tiled=True)]
    all_to_all x2 -> x1, starting transfers between devices: 17.3 us -> 3.85 us  [exchange(): return lax.all_to_all(x, axis, 0, 0, tiled=True)]
    unnamed x18 -> x12, local copies, waits for them, and re-layouts: 11.5 us -> 0.02 us
    all_to_all x2 -> x1, waiting for transfers between devices: 18.1 us -> 8.98 us  [exchange(): return lax.all_to_all(x, axis, 0, 0, tiled=True)]
    pallas_call x11, Pallas kernels: 22.1 us -> 19.5 us  [call(): pl.pallas_call(body, out_shape=tuple(out_shape), in_specs=[SM] * len(scal...]
  transfers between devices with their start and end apart: 2 -> 1, of which waited for: 2 -> 1; matrix products, arithmetic and copies ran while one was open for 0% -> 0% of each run, Pallas kernels for 0% -> 0%
where the time goes in v2:
time: 183 us; the launch traced here: 182 us
  blocking collectives  135 us (74%)
  Pallas kernels  19.5 us (11%)
  between operations  14.2 us (8%)
  waiting for transfers between devices  8.98 us (5%)
  starting transfers between devices  3.85 us (2%)
    all_to_all x9, blocking collectives, exchange(): return lax.all_to_all(x, axis, 0, 0, tiled=True)  135 us
    pallas_call x11, Pallas kernels, call(): pl.pallas_call(body, out_shape=tuple(out_shape), in_specs=[SM] * len(scal...  19.5 us
    all_to_all x1, waiting for transfers between devices, exchange(): return lax.all_to_all(x, axis, 0, 0, tiled=True)  8.98 us
    all_to_all x1, starting transfers between devices, exchange(): return lax.all_to_all(x, axis, 0, 0, tiled=True)  3.85 us
  transfers between devices with their start and end apart: 1, of which 1 were waited for; matrix products, arithmetic and copies ran while one was open for 0% of the time, Pallas kernels for 0%

profile of v2, /device:TPU:1, one launch (start us, length us, event | category | flops | bytes accessed | tf_op | source)
XLA Modules:
  0.0 182.1 jit_solution(14072405054192176564)
XLA Ops:
  7.2 0.1 pad_add_fusion.spot_ref
  7.2 4.9 %shard_map.81 = (f32[32,4,128]{2,1,0:T(4,128)S(1)}, f32[512,1024]{1,0:T(8,128)S(1)}, f32[8,512,1024]{2,1,0:T(8,128)S(1)}) custom-call(s32[2]{0:T(128)S(1)} %pad_add_fusion.spot_ref, f32[8]{0:T(128)} %slope_ref.11, bf16[512,1024]{1,0:T(8,128)(2,1)} %cost_ref.1, f32[8,512]{1,0:T(8,128)} %productivity_ref.5, f32[4,128]{1,0:T(4,128)} %bitcast.111, ...), custom_call_target="tpu_custom_call" | custom-call | tf_op jit(solution)/shard_map/pallas_call | solution.py:218
  12.1 22.4 %all_to_all.50.got_ref = f32[32,4,128]{2,1,0:T(4,128)S(1)} all-to-all(f32[32,4,128]{2,1,0:T(4,128)S(1)} %get-tuple-element.208), channel_id=1, replica_groups=mesh['orig'=32,'dest'=16] {'orig'}, dimensions={0} | all-to-all | bytes 131072 | tf_op jit(solution)/shard_map/all_to_all | solution.py:229
  34.5 0.9 shard_map.82
  35.5 12.0 %all_to_all.51.ratio_ref = f32[32,2,128]{2,1,0:T(2,128)S(1)} all-to-all(f32[32,2,128]{2,1,0:T(2,128)S(1)} %shard_map.82), channel_id=1, replica_groups=mesh['orig'=32,'dest'=16] {'orig'}, dimensions={0} | all-to-all | bytes 65536 | tf_op jit(solution)/shard_map/all_to_all | solution.py:229
  47.4 0.0 copy-start
  47.5 1.9 %shard_map.83 = f32[16,4,128]{2,1,0:T(4,128)S(1)} custom-call(f32[8,512,1024]{2,1,0:T(8,128)S(1)} %get-tuple-element.206.trade_ref, f32[512,1024]{1,0:T(8,128)S(1)} %get-tuple-element.207.spread_ref, f32[32,2,128]{2,1,0:T(2,128)S(1)} %all_to_all.51.ratio_ref), custom_call_target="tpu_custom_call" | custom-call | tf_op jit(solution)/shard_map/pallas_call | solution.py:218
  49.3 22.8 %all_to_all.52.sales_ref = f32[16,4,128]{2,1,0:T(4,128)S(1)} all-to-all(f32[16,4,128]{2,1,0:T(4,128)S(1)} %shard_map.83), channel_id=1, replica_groups=mesh['orig'=32,'dest'=16] {'dest'}, dimensions={0} | all-to-all | bytes 65536 | tf_op jit(solution)/shard_map/all_to_all | solution.py:229
  72.1 0.0 copy-done
  72.1 0.0 copy-done.3
  72.1 0.0 copy-done.4
  72.1 0.0 copy-done.5
  72.2 0.0 copy-start.2
  72.2 2.5 %shard_map.84 = (f32[32,4,128]{2,1,0:T(4,128)S(1)}, f32[512,1024]{1,0:T(8,128)S(1)}, f32[4,128]{1,0:T(4,128)S(1)}) custom-call(s32[2]{0:T(128)S(1)} %pad_add_fusion.spot_ref, f32[8]{0:T(128)S(1)} %copy-done.5, f32[8,512,1024]{2,1,0:T(8,128)S(1)} %get-tuple-element.206.trade_ref, f32[8,512]{1,0:T(8,128)S(1)} %copy-done, f32[4,128]{1,0:T(4,128)S(1)} %bitcast.112, ...), custom_call_target="tpu_custom_call" | custom-call | tf_op jit(solution)/shard_map/pallas_call | solution.py:218
  74.6 12.2 %all_to_all.53.got_ref = f32[32,4,128]{2,1,0:T(4,128)S(1)} all-to-all(f32[32,4,128]{2,1,0:T(4,128)S(1)} %get-tuple-element.211), channel_id=1, replica_groups=mesh['orig'=32,'dest'=16] {'orig'}, dimensions={0} | all-to-all | bytes 131072 | tf_op jit(solution)/shard_map/all_to_all | solution.py:229
  86.8 0.0 copy-done.2
  86.8 0.7 shard_map.85
  87.5 12.0 %all_to_all.54.ratio_ref = f32[32,2,128]{2,1,0:T(2,128)S(1)} all-to-all(f32[32,2,128]{2,1,0:T(2,128)S(1)} %shard_map.85), channel_id=1, replica_groups=mesh['orig'=32,'dest'=16] {'orig'}, dimensions={0} | all-to-all | bytes 65536 | tf_op jit(solution)/shard_map/all_to_all | solution.py:229
  99.5 1.9 %shard_map.86 = f32[16,4,128]{2,1,0:T(4,128)S(1)} custom-call(f32[8,512,1024]{2,1,0:T(8,128)S(1)} %get-tuple-element.206.trade_ref, f32[512,1024]{1,0:T(8,128)S(1)} %get-tuple-element.210.spread_ref, f32[32,2,128]{2,1,0:T(2,128)S(1)} %all_to_all.54.ratio_ref), custom_call_target="tpu_custom_call" | custom-call | tf_op jit(solution)/shard_map/pallas_call | solution.py:218
  101.4 14.8 %all_to_all.55.sales_ref = f32[16,4,128]{2,1,0:T(4,128)S(1)} all-to-all(f32[16,4,128]{2,1,0:T(4,128)S(1)} %shard_map.86), channel_id=1, replica_groups=mesh['orig'=32,'dest'=16] {'dest'}, dimensions={0} | all-to-all | bytes 65536 | tf_op jit(solution)/shard_map/all_to_all | solution.py:229
  116.2 2.5 %shard_map.87 = (f32[32,4,128]{2,1,0:T(4,128)S(1)}, f32[512,1024]{1,0:T(8,128)S(1)}, f32[4,128]{1,0:T(4,128)S(1)}) custom-call(s32[2]{0:T(128)S(1)} %pad_add_fusion.spot_ref, f32[8]{0:T(128)S(1)} %copy-done.5, f32[8,512,1024]{2,1,0:T(8,128)S(1)} %get-tuple-element.206.trade_ref, f32[8,512]{1,0:T(8,128)S(1)} %copy-done, f32[4,128]{1,0:T(4,128)S(1)} %bitcast.113, ...), custom_call_target="tpu_custom_call" | custom-call | tf_op jit(solution)/shard_map/pallas_call | solution.py:218
  118.6 12.2 %all_to_all.56.got_ref = f32[32,4,128]{2,1,0:T(4,128)S(1)} all-to-all(f32[32,4,128]{2,1,0:T(4,128)S(1)} %get-tuple-element.214), channel_id=1, replica_groups=mesh['orig'=32,'dest'=16] {'orig'}, dimensions={0} | all-to-all | bytes 131072 | tf_op jit(solution)/shard_map/all_to_all | solution.py:229
  130.8 0.7 shard_map.88
  131.5 12.2 %all_to_all.57.ratio_ref = f32[32,4,128]{2,1,0:T(4,128)S(1)} all-to-all(f32[32,4,128]{2,1,0:T(4,128)S(1)} %shard_map.88), channel_id=1, replica_groups=mesh['orig'=32,'dest'=16] {'orig'}, dimensions={0} | all-to-all | bytes 131072 | tf_op jit(solution)/shard_map/all_to_all | solution.py:229
  143.7 2.3 %shard_map.89 = (f32[16,4,128]{2,1,0:T(4,128)S(1)}, f32[8,1024]{1,0:T(8,128)}) custom-call(f32[8,512,1024]{2,1,0:T(8,128)S(1)} %get-tuple-element.206.trade_ref, f32[512,1024]{1,0:T(8,128)S(1)} %get-tuple-element.213.spread_ref, f32[32,4,128]{2,1,0:T(4,128)S(1)} %all_to_all.57.ratio_ref), custom_call_target="tpu_custom_call" | custom-call | tf_op jit(solution)/shard_map/pallas_call | solution.py:218
  146.1 14.7 %all_to_all.58.sales_ref = f32[16,4,128]{2,1,0:T(4,128)S(1)} all-to-all(f32[16,4,128]{2,1,0:T(4,128)S(1)} %get-tuple-element.215), channel_id=1, replica_groups=mesh['orig'=32,'dest'=16] {'dest'}, dimensions={0} | all-to-all | bytes 65536 | tf_op jit(solution)/shard_map/all_to_all | solution.py:229
  160.8 0.6 shard_map.90
  161.4 3.9 %all-to-all-start.9 = ((f32[32,1,128]{2,1,0:T(1,128)}), f32[32,1,128]{2,1,0:T(1,128)S(1)}, u32[]{:S(2)}, u32[]{:S(2)}) async-start(f32[32,1,128]{2,1,0:T(1,128)} %get-tuple-element.217), calls=%async_computation.12 | async-start | bytes 32768 | tf_op jit(solution)/shard_map/all_to_all | solution.py:229
  165.3 9.0 %all-to-all-done.9.got_ref = f32[32,1,128]{2,1,0:T(1,128)S(1)} async-done(((f32[32,1,128]{2,1,0:T(1,128)}), f32[32,1,128]{2,1,0:T(1,128)S(1)}, u32[]{:S(2)}, u32[]{:S(2)}) %all-to-all-start.9) | async-done | bytes 16416 | tf_op jit(solution)/shard_map/all_to_all | solution.py:229
  174.3 0.7 shard_map.91
  175.0 0.0 copy-done.1
  175.0 0.2 conditional.1
  (4 shorter events, 0.0 us)
Async XLA Ops:
  47.4 24.7 %copy-start = (f32[8,512]{1,0:T(8,128)S(1)}, f32[8,512]{1,0:T(8,128)}, u32[]{:S(2)}) copy-start(f32[8,512]{1,0:T(8,128)} %productivity_ref.5) | copy-start | bytes 49156
  47.4 24.7 %copy-start.3 = (f32[512]{0:T(512)S(1)}, f32[512]{0:T(512)}, u32[]{:S(2)}) copy-start(f32[512]{0:T(512)} %param.24) | copy-start | bytes 6148
  47.4 24.7 %copy-start.4 = (f32[512]{0:T(512)S(1)}, f32[512]{0:T(512)}, u32[]{:S(2)}) copy-start(f32[512]{0:T(512)} %param.25) | copy-start | bytes 6148
  47.4 24.7 %copy-start.5 = (f32[8]{0:T(128)S(1)}, f32[8]{0:T(128)}, u32[]{:S(2)}) copy-start(f32[8]{0:T(128)} %slope_ref.11) | copy-start | bytes 100
  72.2 14.6 %copy-start.2 = (f32[8,1024]{1,0:T(8,128)S(1)}, f32[8,1024]{1,0:T(8,128)}, u32[]{:S(2)}) copy-start(f32[8,1024]{1,0:T(8,128)} %preference_ref.5) | copy-start | bytes 98308
  143.7 31.3 %copy-start.1 = (bf16[512,1024]{1,0:T(8,128)(2,1)S(1)}, bf16[512,1024]{1,0:T(8,128)(2,1)}, u32[]{:S(2)}) copy-start(bf16[512,1024]{1,0:T(8,128)(2,1)} %cost_ref.1) | copy-start | bytes 3145732
  161.4 12.8 %all-to-all-start.9 = ((f32[32,1,128]{2,1,0:T(1,128)}), f32[32,1,128]{2,1,0:T(1,128)S(1)}, u32[]{:S(2)}, u32[]{:S(2)}) async-start(f32[32,1,128]{2,1,0:T(1,128)} %get-tuple-element.217), calls=%async_computation.12 | async-start | bytes 32768 | tf_op jit(solution)/shard_map/all_to_all | solution.py:229

commit v3 on v2

--- a/solution.py
+++ b/solution.py
@@ -10,6 +10,7 @@
 ITERS = 3
 LANES = 128
 CENTRE = 1024.0
+INNER = 8
 SMALLEST, LARGEST = 1e-32, 1e30
 
 
@@ -65,12 +66,9 @@
     )
 
 
-def prepare(spot_ref, slope_ref, columns, productivity_ref, workers_ref, wage, send_ref, spread_ref, supply_ref):
+def prepare(spot_ref, slope_ref, columns, productivity_ref, workers_ref, wage, part_ref, spread_ref, supply_ref):
     sectors, rows = productivity_ref.shape
     pieces = rows // LANES
-    own = send_ref.shape[1] - 2
-    owners = sectors // own
-    blocks = send_ref.shape[0] // owners
     supply = supply_of(pick(slope_ref, sectors), productivity_ref, wage)
     for p in range(pieces):
         supply_ref[:, p * LANES:(p + 1) * LANES] = supply[p]
@@ -78,31 +76,29 @@
     least = functools.reduce(jnp.minimum, supply)
     least = jnp.min(jnp.min(least, axis=0, keepdims=True), axis=1, keepdims=True)
     income = wage * workers_ref[...]
-    world = jnp.where(least > SMALLEST, jnp.sum(income, axis=0, keepdims=True), jnp.nan)
+    part_ref[:, columns + LANES:] = jnp.zeros((sectors, LANES), jnp.float32)
+    part_ref[:pieces, columns + LANES:] = jnp.where(least > SMALLEST, income, jnp.nan)
     part = spot_ref[0] - spot_ref[1] * (columns // rows)
     for i in range(columns // rows):
-        here = income * jnp.where(part == i, 1.0, 0.0)
-        for p in range(pieces):
-            for q in range(owners):
-                at = (i * pieces + p) * owners + q
-                send_ref[at, own:own + 1, :] = here[p:p + 1]
-                send_ref[at, own + 1:own + 2, :] = world
-
-
-def send_phi(totals_ref, send_ref):
-    sectors = totals_ref.shape[0]
-    own = send_ref.shape[1] - 2
-    owners = sectors // own
+        here = jnp.where(part == i, 1.0, 0.0)
+        part_ref[i * pieces:(i + 1) * pieces, columns:columns + LANES] = income * here
+
+
+def send_phi(totals_ref, part_ref, send_ref):
+    sectors, _, columns = totals_ref.shape
     for j in range(sectors):
-        for k in range(send_ref.shape[0] // owners):
-            piece = jnp.sum(totals_ref[j, :, k * LANES:(k + 1) * LANES], axis=0, keepdims=True)
-            send_ref[k * owners + j // own, j % own:j % own + 1, :] = piece
-
-
-def first_phi_kernel(spot_ref, slope_ref, cost_ref, productivity_ref, workers_ref, wage_ref, send_ref, spread_ref, trade_ref, totals_ref, supply_ref):
+        for k in range(columns // LANES):
+            lanes = slice(k * LANES, (k + 1) * LANES)
+            part_ref[j:j + 1, lanes] = jnp.sum(totals_ref[j, :, lanes], axis=0, keepdims=True)
+    part = part_ref[...]
+    for copy in range(send_ref.shape[0]):
+        send_ref[copy] = part
+
+
+def first_phi_kernel(spot_ref, slope_ref, cost_ref, productivity_ref, workers_ref, wage_ref, send_ref, spread_ref, trade_ref, totals_ref, supply_ref, part_ref):
     sectors, rows = productivity_ref.shape
     columns = cost_ref.shape[1]
-    prepare(spot_ref, slope_ref, columns, productivity_ref, workers_ref, wage_ref[...], send_ref, spread_ref, supply_ref)
+    prepare(spot_ref, slope_ref, columns, productivity_ref, workers_ref, wage_ref[...], part_ref, spread_ref, supply_ref)
     slopes = [-slope_ref[j] for j in range(sectors)]
     totals_ref[...] = jnp.zeros_like(totals_ref)
     height = 32
@@ -120,15 +116,15 @@
         return carry
 
     lax.fori_loop(0, rows // height, step, 0)
-    send_phi(totals_ref, send_ref)
-
-
-def phi_kernel(spot_ref, slope_ref, trade_ref, productivity_ref, workers_ref, wage_ref, sales_ref, send_ref, spread_ref, new_wage_ref, totals_ref, supply_ref):
+    send_phi(totals_ref, part_ref, send_ref)
+
+
+def phi_kernel(spot_ref, slope_ref, trade_ref, productivity_ref, workers_ref, wage_ref, sales_ref, send_ref, spread_ref, new_wage_ref, totals_ref, supply_ref, part_ref):
     sectors, rows, columns = trade_ref.shape
     blocks = columns // LANES
     wage = next_wage(wage_ref, workers_ref, sales_ref)
     new_wage_ref[...] = wage
-    prepare(spot_ref, slope_ref, columns, productivity_ref, workers_ref, wage, send_ref, spread_ref, supply_ref)
+    prepare(spot_ref, slope_ref, columns, productivity_ref, workers_ref, wage, part_ref, spread_ref, supply_ref)
     for j in range(sectors):
         def step(block, totals):
             at = pl.ds(pl.multiple_of(block * 8, 8), 8)
@@ -139,48 +135,37 @@
         totals = lax.fori_loop(0, rows // 8, step, (zero,) * blocks, unroll=16)
         for k in range(blocks):
             totals_ref[j, :, k * LANES:(k + 1) * LANES] = totals[k]
-    send_phi(totals_ref, send_ref)
-
-
-def ratio_kernel(last, cells, spot_ref, slope_ref, preference_ref, got_ref, send_ref):
-    sectors = preference_ref.shape[0]
-    own = got_ref.shape[1] - 2
-    got = jnp.sum(got_ref[...], axis=0)
-    income = got[own:own + 1]
-    world = jnp.sum(got[own + 1:own + 2], axis=1, keepdims=True)
-    factor = cells / world
-    owners = sectors // own
-    at = pl.multiple_of(lax.div(spot_ref[0], owners) * LANES, LANES)
-    preference = preference_ref[:, pl.ds(at, LANES)]
-    spend_all = jnp.sum(preference, axis=0, keepdims=True)
-    row = lax.broadcasted_iota(jnp.int32, (sectors, LANES), 0)
-    centred = factor * CENTRE
-    for s in range(own):
-        sector = lax.rem(spot_ref[0], owners) * own + s
-        wanted = jnp.sum(jnp.where(row == sector, preference, 0.0), axis=0, keepdims=True)
-        phi = got[s:s + 1]
-        ratio = wanted / spend_all * income / phi
-        ratio = jnp.where(phi < LARGEST, ratio * (centred * centred), jnp.nan)
-        send_ref[:, s, :] = jnp.broadcast_to(ratio, (send_ref.shape[0], LANES))
-        if last:
-            price = jnp.log(factor) - jnp.log(phi) / slope_ref[sector]
-            send_ref[:, own + s, :] = jnp.broadcast_to(price, (send_ref.shape[0], LANES))
-
-
-def sales_kernel(last, trade_ref, spread_ref, ratio_ref, send_ref, *rest):
-    total_ref = rest[-1]
+    send_phi(totals_ref, part_ref, send_ref)
+
+
+def sum_kernel(got_ref, send_ref):
+    total = jnp.sum(got_ref[...], axis=0)
+    for copy in range(send_ref.shape[0]):
+        send_ref[copy] = total
+
+
+def sales_kernel(last, cells, slope_ref, trade_ref, spread_ref, preference_ref, got_ref, send_ref, *rest):
+    total_ref, ratio_ref, sums_ref = rest[-3:]
     sectors, rows, columns = trade_ref.shape
     blocks = columns // LANES
-    owners = ratio_ref.shape[0] // blocks
-    own = sectors // owners
+    sums_ref[...] = jnp.sum(got_ref[...], axis=0)
+    factor = cells / total_of(sums_ref[:, columns + LANES:])
+    centred = (factor * CENTRE) * (factor * CENTRE)
+    preference = preference_ref[...]
+    share = preference / jnp.sum(preference, axis=0, keepdims=True)
+    for k in range(blocks):
+        lanes = slice(k * LANES, (k + 1) * LANES)
+        phi = sums_ref[:, lanes]
+        ratio = share[:, lanes] * sums_ref[k:k + 1, columns:columns + LANES] / phi
+        ratio_ref[:, lanes] = jnp.where(phi < LARGEST, ratio * centred, jnp.nan)
     if last:
-        price_ref = rest[0]
+        slopes = pick(slope_ref, sectors)
         for k in range(blocks):
-            for j in range(sectors):
-                price_ref[j:j + 1, k * LANES:(k + 1) * LANES] = ratio_ref[k * owners + j // own, own + j % own:own + j % own + 1, :]
+            lanes = slice(k * LANES, (k + 1) * LANES)
+            rest[0][:, lanes] = jnp.log(factor) - jnp.log(sums_ref[:, lanes]) / slopes
     for j in range(sectors):
         ratios = [
-            jnp.broadcast_to(ratio_ref[k * owners + j // own, j % own:j % own + 1, :], (8, LANES))
+            jnp.broadcast_to(ratio_ref[j:j + 1, k * LANES:(k + 1) * LANES], (8, LANES))
             for k in range(blocks)
         ]
 
@@ -225,8 +210,8 @@
     )(*scalars, *arrays)
 
 
-def exchange(x, axis):
-    return lax.all_to_all(x, axis, 0, 0, tiled=True)
+def exchange(x, axis, groups=None):
+    return lax.all_to_all(x, axis, 0, 0, tiled=True, axis_index_groups=groups)
 
 
 def careful(log_cost, elasticity, productivity, preference, workers, start_wage):
@@ -283,16 +268,19 @@
     columns = log_cost.shape[1]
     across, along = lax.axis_size("orig"), lax.axis_size("dest")
     cells = float(rows * across)
-    blocks, pieces = columns // LANES, rows // LANES
-    own = sectors * blocks // across
+    pieces = rows // LANES
+    outer = across // INNER
+    by_inner = [[i * INNER + j for j in range(INNER)] for i in range(outer)]
+    by_outer = [[i * INNER + j for i in range(outer)] for j in range(INNER)]
+    width = columns + 2 * LANES
     spot = jnp.stack([lax.axis_index("orig"), lax.axis_index("dest")]).astype(jnp.int32)
     workers = workers.reshape(pieces, LANES)
     wage = start_wage.reshape(pieces, LANES)
     sales = trade = None
     for step in range(ITERS):
         last = step + 1 == ITERS
-        outs = [f32(across, own + 2, LANES), f32(rows, sectors * LANES)]
-        scratch = [(sectors, 8, columns), (sectors, rows)]
+        outs = [f32(outer, sectors, width), f32(rows, sectors * LANES)]
+        scratch = [(sectors, 8, columns), (sectors, rows), (sectors, width)]
         if step == 0:
             send, spread, trade = call(
                 first_phi_kernel, outs + [f32(sectors, rows, columns)], [spot, elasticity],
@@ -303,20 +291,15 @@
                 phi_kernel, outs + [f32(pieces, LANES)], [spot, elasticity],
                 [trade, productivity, workers, wage, sales], scratch,
             )
-        got = exchange(send, "orig")
-        ratio, = call(
-            functools.partial(ratio_kernel, last, cells),
-            [f32(across, 2 * own if last else own, LANES)],
-            [spot, elasticity],
-            [preference, got],
-        )
-        ratio = exchange(ratio, "orig")
+        got = exchange(send, "orig", by_outer)
+        send, = call(sum_kernel, [f32(INNER, sectors, width)], [], [got])
+        got = exchange(send, "orig", by_inner)
         made = call(
-            functools.partial(sales_kernel, last),
+            functools.partial(sales_kernel, last, cells),
             [f32(along, pieces, LANES)] + ([f32(sectors, columns)] if last else []),
-            [],
-            [trade, spread, ratio],
-            [(rows, LANES)],
+            [elasticity],
+            [trade, spread, preference, got],
+            [(rows, LANES), (sectors, columns), (sectors, width)],
         )
         sales = exchange(made[0], "dest")
     log_price = made[1]

time: 183 us -> 176 us (0.962)
  blocking collectives: 135 us -> 129 us
    all_to_all x9, blocking collectives: 135 us -> 129 us  [exchange(): return lax.all_to_all(x, axis, 0, 0, tiled=True, axis_index_groups=groups)]
where the time goes in v3:
time: 176 us
  blocking collectives  129 us (73%)
  Pallas kernels  19.2 us (11%)
  between operations  14.2 us (8%)
  waiting for transfers between devices  8.96 us (5%)
  starting transfers between devices  4.17 us (2%)
    all_to_all x9, blocking collectives, exchange(): return lax.all_to_all(x, axis, 0, 0, tiled=True, axis_index_groups=groups)  129 us
    pallas_call x11, Pallas kernels, call(): pl.pallas_call(body, out_shape=tuple(out_shape), in_specs=[SM] * len(scal...  19.2 us
    all_to_all x1, waiting for transfers between devices, exchange(): return lax.all_to_all(x, axis, 0, 0, tiled=True, axis_index_groups=groups)  8.96 us
    all_to_all x1, starting transfers between devices, exchange(): return lax.all_to_all(x, axis, 0, 0, tiled=True, axis_index_groups=groups)  4.17 us
  transfers between devices with their start and end apart: 1, of which 1 were waited for; matrix products, arithmetic and copies ran while one was open for 0% of the time, Pallas kernels for 0%

profile of v3, /device:TPU:1, one launch (start us, length us, event | category | flops | bytes accessed | tf_op | source)
XLA Modules:
  0.0 175.8 jit_solution(6893300196491468091)
XLA Ops:
  7.2 0.0 copy-start.5
  7.2 0.0 copy-start.2
  7.2 0.1 pad_add_fusion.spot_ref
  7.3 5.3 %shard_map.81 = (f32[4,8,1280]{2,1,0:T(8,128)S(1)}, f32[512,1024]{1,0:T(8,128)S(1)}, f32[8,512,1024]{2,1,0:T(8,128)S(1)}) custom-call(s32[2]{0:T(128)S(1)} %pad_add_fusion.spot_ref, f32[8]{0:T(128)} %slope_ref.11, bf16[512,1024]{1,0:T(8,128)(2,1)} %cost_ref.1, f32[8,512]{1,0:T(8,128)} %productivity_ref.5, f32[4,128]{1,0:T(4,128)} %bitcast.111, ...), custom_call_target="tpu_custom_call" | custom-call | tf_op jit(solution)/shard_map/pallas_call | solution.py:203
  12.5 13.2 %all_to_all.50.got_ref = f32[4,8,1280]{2,1,0:T(8,128)S(1)} all-to-all(f32[4,8,1280]{2,1,0:T(8,128)S(1)} %get-tuple-element.208), channel_id=1, replica_groups={{0,128,256,384},{16,144,272,400},{32,160,288,416},{48,176,304,432},{64,..., dimensions={0} | all-to-all | bytes 327680 | tf_op jit(solution)/shard_map/all_to_all | solution.py:214
  25.7 16.6 %all_to_all.51.got_ref = f32[8,8,1280]{2,1,0:T(8,128)S(1)} all-to-all(f32[8,8,1280]{2,1,0:T(8,128)S(1)} %shard_map.82), channel_id=1, replica_groups={{0,16,32,48,64,80,96,112},{128,144,160,176,192,208,224,240},{256,272,28..., dimensions={0} | all-to-all | bytes 655360 | tf_op jit(solution)/shard_map/all_to_all | solution.py:214
  42.4 0.0 copy-done.5
  42.4 0.0 copy-done.2
  42.4 0.0 copy-start
  42.4 0.0 copy-start.3
  42.4 0.0 copy-start.4
  42.4 2.5 %shard_map.83 = f32[16,4,128]{2,1,0:T(4,128)S(1)} custom-call(f32[8]{0:T(128)S(1)} %copy-done.5, f32[8,512,1024]{2,1,0:T(8,128)S(1)} %get-tuple-element.206.trade_ref, f32[512,1024]{1,0:T(8,128)S(1)} %get-tuple-element.207.spread_ref, f32[8,1024]{1,0:T(8,128)S(1)} %copy-done.2, f32[8,8,1280]{2,1,0:T(8,128)S(1)} %all_to_all.51.got_ref), custom_call_target="tpu_custom_call" | custom-call | tf_op jit(solution)/shard_map/pallas_call | solution.py:203
  44.9 23.9 %all_to_all.52.sales_ref = f32[16,4,128]{2,1,0:T(4,128)S(1)} all-to-all(f32[16,4,128]{2,1,0:T(4,128)S(1)} %shard_map.83), channel_id=1, replica_groups=mesh['orig'=32,'dest'=16] {'dest'}, dimensions={0} | all-to-all | bytes 65536 | tf_op jit(solution)/shard_map/all_to_all | solution.py:214
  68.8 0.0 copy-done
  68.8 0.0 copy-done.3
  68.8 0.0 copy-done.4
  68.8 2.4 %shard_map.84 = (f32[4,8,1280]{2,1,0:T(8,128)S(1)}, f32[512,1024]{1,0:T(8,128)S(1)}, f32[4,128]{1,0:T(4,128)S(1)}) custom-call(s32[2]{0:T(128)S(1)} %pad_add_fusion.spot_ref, f32[8]{0:T(128)S(1)} %copy-done.5, f32[8,512,1024]{2,1,0:T(8,128)S(1)} %get-tuple-element.206.trade_ref, f32[8,512]{1,0:T(8,128)S(1)} %copy-done, f32[4,128]{1,0:T(4,128)S(1)} %bitcast.112, ...), custom_call_target="tpu_custom_call" | custom-call | tf_op jit(solution)/shard_map/pallas_call | solution.py:203
  71.1 8.6 %all_to_all.53.got_ref = f32[4,8,1280]{2,1,0:T(8,128)S(1)} all-to-all(f32[4,8,1280]{2,1,0:T(8,128)S(1)} %get-tuple-element.211), channel_id=1, replica_groups={{0,128,256,384},{16,144,272,400},{32,160,288,416},{48,176,304,432},{64,..., dimensions={0} | all-to-all | bytes 327680 | tf_op jit(solution)/shard_map/all_to_all | solution.py:214
  79.8 12.7 %all_to_all.54.got_ref = f32[8,8,1280]{2,1,0:T(8,128)S(1)} all-to-all(f32[8,8,1280]{2,1,0:T(8,128)S(1)} %shard_map.85), channel_id=1, replica_groups={{0,16,32,48,64,80,96,112},{128,144,160,176,192,208,224,240},{256,272,28..., dimensions={0} | all-to-all | bytes 655360 | tf_op jit(solution)/shard_map/all_to_all | solution.py:214
  92.5 2.5 %shard_map.86 = f32[16,4,128]{2,1,0:T(4,128)S(1)} custom-call(f32[8]{0:T(128)S(1)} %copy-done.5, f32[8,512,1024]{2,1,0:T(8,128)S(1)} %get-tuple-element.206.trade_ref, f32[512,1024]{1,0:T(8,128)S(1)} %get-tuple-element.210.spread_ref, f32[8,1024]{1,0:T(8,128)S(1)} %copy-done.2, f32[8,8,1280]{2,1,0:T(8,128)S(1)} %all_to_all.54.got_ref), custom_call_target="tpu_custom_call" | custom-call | tf_op jit(solution)/shard_map/pallas_call | solution.py:203
  95.0 16.1 %all_to_all.55.sales_ref = f32[16,4,128]{2,1,0:T(4,128)S(1)} all-to-all(f32[16,4,128]{2,1,0:T(4,128)S(1)} %shard_map.86), channel_id=1, replica_groups=mesh['orig'=32,'dest'=16] {'dest'}, dimensions={0} | all-to-all | bytes 65536 | tf_op jit(solution)/shard_map/all_to_all | solution.py:214
  111.0 2.4 %shard_map.87 = (f32[4,8,1280]{2,1,0:T(8,128)S(1)}, f32[512,1024]{1,0:T(8,128)S(1)}, f32[4,128]{1,0:T(4,128)S(1)}) custom-call(s32[2]{0:T(128)S(1)} %pad_add_fusion.spot_ref, f32[8]{0:T(128)S(1)} %copy-done.5, f32[8,512,1024]{2,1,0:T(8,128)S(1)} %get-tuple-element.206.trade_ref, f32[8,512]{1,0:T(8,128)S(1)} %copy-done, f32[4,128]{1,0:T(4,128)S(1)} %bitcast.113, ...), custom_call_target="tpu_custom_call" | custom-call | tf_op jit(solution)/shard_map/pallas_call | solution.py:203
  113.4 9.1 %all_to_all.56.got_ref = f32[4,8,1280]{2,1,0:T(8,128)S(1)} all-to-all(f32[4,8,1280]{2,1,0:T(8,128)S(1)} %get-tuple-element.214), channel_id=1, replica_groups={{0,128,256,384},{16,144,272,400},{32,160,288,416},{48,176,304,432},{64,..., dimensions={0} | all-to-all | bytes 327680 | tf_op jit(solution)/shard_map/all_to_all | solution.py:214
  122.5 12.7 %all_to_all.57.got_ref = f32[8,8,1280]{2,1,0:T(8,128)S(1)} all-to-all(f32[8,8,1280]{2,1,0:T(8,128)S(1)} %shard_map.88), channel_id=1, replica_groups={{0,16,32,48,64,80,96,112},{128,144,160,176,192,208,224,240},{256,272,28..., dimensions={0} | all-to-all | bytes 655360 | tf_op jit(solution)/shard_map/all_to_all | solution.py:214
  135.3 2.9 %shard_map.89 = (f32[16,4,128]{2,1,0:T(4,128)S(1)}, f32[8,1024]{1,0:T(8,128)}) custom-call(f32[8]{0:T(128)S(1)} %copy-done.5, f32[8,512,1024]{2,1,0:T(8,128)S(1)} %get-tuple-element.206.trade_ref, f32[512,1024]{1,0:T(8,128)S(1)} %get-tuple-element.213.spread_ref, f32[8,1024]{1,0:T(8,128)S(1)} %copy-done.2, f32[8,8,1280]{2,1,0:T(8,128)S(1)} %all_to_all.57.got_ref), custom_call_target="tpu_custom_call" | custom-call | tf_op jit(solution)/shard_map/pallas_call | solution.py:203
  138.2 16.0 %all_to_all.58.sales_ref = f32[16,4,128]{2,1,0:T(4,128)S(1)} all-to-all(f32[16,4,128]{2,1,0:T(4,128)S(1)} %get-tuple-element.215), channel_id=1, replica_groups=mesh['orig'=32,'dest'=16] {'dest'}, dimensions={0} | all-to-all | bytes 65536 | tf_op jit(solution)/shard_map/all_to_all | solution.py:214
  154.2 0.6 shard_map.90
  154.9 4.2 %all-to-all-start.9 = ((f32[32,1,128]{2,1,0:T(1,128)}), f32[32,1,128]{2,1,0:T(1,128)S(1)}, u32[]{:S(2)}, u32[]{:S(2)}) async-start(f32[32,1,128]{2,1,0:T(1,128)} %get-tuple-element.217), calls=%async_computation.12 | async-start | bytes 32768 | tf_op jit(solution)/shard_map/all_to_all | solution.py:214
  159.0 9.0 %all-to-all-done.9.got_ref = f32[32,1,128]{2,1,0:T(1,128)S(1)} async-done(((f32[32,1,128]{2,1,0:T(1,128)}), f32[32,1,128]{2,1,0:T(1,128)S(1)}, u32[]{:S(2)}, u32[]{:S(2)}) %all-to-all-start.9) | async-done | bytes 16416 | tf_op jit(solution)/shard_map/all_to_all | solution.py:214
  168.0 0.7 shard_map.91
  168.7 0.0 copy-done.1
  168.7 0.2 conditional.1
  (4 shorter events, 0.1 us)
Async XLA Ops:
  7.2 35.2 %copy-start.5 = (f32[8]{0:T(128)S(1)}, f32[8]{0:T(128)}, u32[]{:S(2)}) copy-start(f32[8]{0:T(128)} %slope_ref.11) | copy-start | bytes 100
  7.2 35.2 %copy-start.2 = (f32[8,1024]{1,0:T(8,128)S(1)}, f32[8,1024]{1,0:T(8,128)}, u32[]{:S(2)}) copy-start(f32[8,1024]{1,0:T(8,128)} %preference_ref.5) | copy-start | bytes 98308
  42.4 26.4 %copy-start = (f32[8,512]{1,0:T(8,128)S(1)}, f32[8,512]{1,0:T(8,128)}, u32[]{:S(2)}) copy-start(f32[8,512]{1,0:T(8,128)} %productivity_ref.5) | copy-start | bytes 49156
  42.4 26.4 %copy-start.3 = (f32[512]{0:T(512)S(1)}, f32[512]{0:T(512)}, u32[]{:S(2)}) copy-start(f32[512]{0:T(512)} %param.24) | copy-start | bytes 6148
  42.4 26.4 %copy-start.4 = (f32[512]{0:T(512)S(1)}, f32[512]{0:T(512)}, u32[]{:S(2)}) copy-start(f32[512]{0:T(512)} %param.25) | copy-start | bytes 6148
  135.3 33.5 %copy-start.1 = (bf16[512,1024]{1,0:T(8,128)(2,1)S(1)}, bf16[512,1024]{1,0:T(8,128)(2,1)}, u32[]{:S(2)}) copy-start(bf16[512,1024]{1,0:T(8,128)(2,1)} %cost_ref.1) | copy-start | bytes 3145732
  154.9 13.1 %all-to-all-start.9 = ((f32[32,1,128]{2,1,0:T(1,128)}), f32[32,1,128]{2,1,0:T(1,128)S(1)}, u32[]{:S(2)}, u32[]{:S(2)}) async-start(f32[32,1,128]{2,1,0:T(1,128)} %get-tuple-element.217), calls=%async_computation.12 | async-start | bytes 32768 | tf_op jit(solution)/shard_map/all_to_all | solution.py:214

commit v4 on v3

--- a/solution.py
+++ b/solution.py
@@ -10,6 +10,7 @@
 ITERS = 3
 LANES = 128
 CENTRE = 1024.0
+GAIN = 2.0
 INNER = 8
 SMALLEST, LARGEST = 1e-32, 1e30
 
@@ -36,10 +37,10 @@
     return jnp.sum(jnp.sum(x, axis=0, keepdims=True), axis=1, keepdims=True)
 
 
-def next_wage(wage_ref, workers_ref, sales_ref):
+def next_wage(wage_ref, workers_ref, sales_ref, gain=1.0):
     wage, workers = wage_ref[...], workers_ref[...]
     revenue = jnp.sum(sales_ref[...], axis=0)
-    return wage * jnp.sqrt(revenue / (wage * workers))
+    return wage * gain * jnp.sqrt(revenue / (wage * workers))
 
 
 def supply_of(slopes, productivity_ref, wage):
@@ -76,12 +77,14 @@
     least = functools.reduce(jnp.minimum, supply)
     least = jnp.min(jnp.min(least, axis=0, keepdims=True), axis=1, keepdims=True)
     income = wage * workers_ref[...]
-    part_ref[:, columns + LANES:] = jnp.zeros((sectors, LANES), jnp.float32)
-    part_ref[:pieces, columns + LANES:] = jnp.where(least > SMALLEST, income, jnp.nan)
+    guarded = jnp.where(least > SMALLEST, income, jnp.nan)
     part = spot_ref[0] - spot_ref[1] * (columns // rows)
     for i in range(columns // rows):
         here = jnp.where(part == i, 1.0, 0.0)
-        part_ref[i * pieces:(i + 1) * pieces, columns:columns + LANES] = income * here
+        part_ref[i * pieces:(i + 1) * pieces, columns:columns + LANES] = guarded * here
+    if part_ref.shape[1] > columns + LANES:
+        part_ref[:, columns + LANES:] = jnp.zeros((sectors, LANES), jnp.float32)
+        part_ref[:pieces, columns + LANES:] = income
 
 
 def send_phi(totals_ref, part_ref, send_ref):
@@ -95,13 +98,18 @@
         send_ref[copy] = part
 
 
-def first_phi_kernel(spot_ref, slope_ref, cost_ref, productivity_ref, workers_ref, wage_ref, send_ref, spread_ref, trade_ref, totals_ref, supply_ref, part_ref):
+def first_phi_kernel(spot_ref, slope_ref, productivity_ref, workers_ref, wage_ref, cost_in_ref, send_ref, spread_ref, trade_ref, totals_ref, supply_ref, part_ref, cost_ref, arrived):
     sectors, rows = productivity_ref.shape
     columns = cost_ref.shape[1]
+    batch, height = rows // arrived.shape[0], 32
+    copies = []
+    for i in range(arrived.shape[0]):
+        some = pl.ds(i * batch, batch)
+        copies.append(pltpu.make_async_copy(cost_in_ref.at[some], cost_ref.at[some], arrived.at[i]))
+        copies[-1].start()
     prepare(spot_ref, slope_ref, columns, productivity_ref, workers_ref, wage_ref[...], part_ref, spread_ref, supply_ref)
     slopes = [-slope_ref[j] for j in range(sectors)]
     totals_ref[...] = jnp.zeros_like(totals_ref)
-    height = 32
 
     def step(block, carry):
         at = pl.ds(pl.multiple_of(block * height, height), height)
@@ -115,14 +123,16 @@
                 totals_ref[j, :, lanes] += tree_sum([term[r:r + 8] for r in range(0, height, 8)])
         return carry
 
-    lax.fori_loop(0, rows // height, step, 0)
+    for i, copy in enumerate(copies):
+        copy.wait()
+        lax.fori_loop(i * batch // height, (i + 1) * batch // height, step, 0)
     send_phi(totals_ref, part_ref, send_ref)
 
 
-def phi_kernel(spot_ref, slope_ref, trade_ref, productivity_ref, workers_ref, wage_ref, sales_ref, send_ref, spread_ref, new_wage_ref, totals_ref, supply_ref, part_ref):
+def phi_kernel(gain, spot_ref, slope_ref, trade_ref, productivity_ref, workers_ref, wage_ref, sales_ref, send_ref, spread_ref, new_wage_ref, totals_ref, supply_ref, part_ref):
     sectors, rows, columns = trade_ref.shape
     blocks = columns // LANES
-    wage = next_wage(wage_ref, workers_ref, sales_ref)
+    wage = next_wage(wage_ref, workers_ref, sales_ref, gain)
     new_wage_ref[...] = wage
     prepare(spot_ref, slope_ref, columns, productivity_ref, workers_ref, wage, part_ref, spread_ref, supply_ref)
     for j in range(sectors):
@@ -149,20 +159,21 @@
     sectors, rows, columns = trade_ref.shape
     blocks = columns // LANES
     sums_ref[...] = jnp.sum(got_ref[...], axis=0)
-    factor = cells / total_of(sums_ref[:, columns + LANES:])
-    centred = (factor * CENTRE) * (factor * CENTRE)
     preference = preference_ref[...]
     share = preference / jnp.sum(preference, axis=0, keepdims=True)
     for k in range(blocks):
         lanes = slice(k * LANES, (k + 1) * LANES)
         phi = sums_ref[:, lanes]
         ratio = share[:, lanes] * sums_ref[k:k + 1, columns:columns + LANES] / phi
-        ratio_ref[:, lanes] = jnp.where(phi < LARGEST, ratio * centred, jnp.nan)
+        ratio_ref[:, lanes] = jnp.where(phi < LARGEST, ratio, jnp.nan)
+    if sums_ref.shape[1] > columns + LANES:
+        centred = CENTRE * cells / total_of(sums_ref[:, columns + LANES:])
+        ratio_ref[...] *= centred * centred
     if last:
         slopes = pick(slope_ref, sectors)
         for k in range(blocks):
             lanes = slice(k * LANES, (k + 1) * LANES)
-            rest[0][:, lanes] = jnp.log(factor) - jnp.log(sums_ref[:, lanes]) / slopes
+            rest[0][:, lanes] = -jnp.log(sums_ref[:, lanes]) / slopes
     for j in range(sectors):
         ratios = [
             jnp.broadcast_to(ratio_ref[j:j + 1, k * LANES:(k + 1) * LANES], (8, LANES))
@@ -185,29 +196,32 @@
 def settle_kernel(workers_ref, wage_ref, sales_ref, raw_ref, send_ref):
     raw = next_wage(wage_ref, workers_ref, sales_ref)
     raw_ref[...] = raw
-    world = jnp.sum(raw * workers_ref[...], axis=0, keepdims=True)
-    send_ref[:, 0, :] = jnp.broadcast_to(world, (send_ref.shape[0], LANES))
-
-
-def finish_kernel(cells, raw_ref, got_ref, wage_ref, world_ref):
-    world = total_of(got_ref[:, 0, :])
-    wage_ref[...] = raw_ref[...] * (cells / world)
-    world_ref[...] = jnp.broadcast_to(world, (1, LANES))
+    copies = send_ref.shape[0]
+    for row, wage in enumerate((raw, wage_ref[...])):
+        world = jnp.sum(wage * workers_ref[...], axis=0, keepdims=True)
+        send_ref[:, row, :] = jnp.broadcast_to(world, (copies, LANES))
+
+
+def finish_kernel(cells, raw_ref, price_ref, got_ref, wage_ref, log_price_ref, world_ref):
+    sums = jnp.sum(jnp.sum(got_ref[...], axis=0), axis=1, keepdims=True)
+    wage_ref[...] = raw_ref[...] * (cells / sums[0:1])
+    log_price_ref[...] = price_ref[...] + jnp.log(cells / sums[1:2])
+    world_ref[...] = jnp.broadcast_to(sums[0:1], (1, LANES))
 
 
 VM = pl.BlockSpec(memory_space=pltpu.VMEM)
 SM = pl.BlockSpec(memory_space=pltpu.SMEM)
 
 
-def call(body, out_shape, scalars, arrays, scratch=()):
+def call(body, out_shape, scalars, arrays, scratch=(), in_place=()):
     return pl.pallas_call(
         body,
         out_shape=tuple(out_shape),
-        in_specs=[SM] * len(scalars) + [VM] * len(arrays),
+        in_specs=[SM] * len(scalars) + [VM] * len(arrays) + [pl.BlockSpec(memory_space=pl.ANY)] * len(in_place),
         out_specs=(VM,) * len(out_shape),
-        scratch_shapes=[pltpu.VMEM(shape, jnp.float32) for shape in scratch],
+        scratch_shapes=[pltpu.VMEM(s, jnp.float32) if isinstance(s, tuple) else s for s in scratch],
         compiler_params=pltpu.CompilerParams(vmem_limit_bytes=16 << 20),
-    )(*scalars, *arrays)
+    )(*scalars, *arrays, *in_place)
 
 
 def exchange(x, axis, groups=None):
@@ -272,23 +286,26 @@
     outer = across // INNER
     by_inner = [[i * INNER + j for j in range(INNER)] for i in range(outer)]
     by_outer = [[i * INNER + j for i in range(outer)] for j in range(INNER)]
-    width = columns + 2 * LANES
     spot = jnp.stack([lax.axis_index("orig"), lax.axis_index("dest")]).astype(jnp.int32)
     workers = workers.reshape(pieces, LANES)
     wage = start_wage.reshape(pieces, LANES)
     sales = trade = None
     for step in range(ITERS):
         last = step + 1 == ITERS
+        width = columns + (2 if step == 0 else 1) * LANES
         outs = [f32(outer, sectors, width), f32(rows, sectors * LANES)]
         scratch = [(sectors, 8, columns), (sectors, rows), (sectors, width)]
         if step == 0:
             send, spread, trade = call(
                 first_phi_kernel, outs + [f32(sectors, rows, columns)], [spot, elasticity],
-                [log_cost, productivity, workers, wage], scratch,
+                [productivity, workers, wage],
+                scratch + [pltpu.VMEM(log_cost.shape, log_cost.dtype), pltpu.SemaphoreType.DMA((2,))],
+                [log_cost],
             )
         else:
             send, spread, wage = call(
-                phi_kernel, outs + [f32(pieces, LANES)], [spot, elasticity],
+                functools.partial(phi_kernel, 1.0 if step == 1 else GAIN),
+                outs + [f32(pieces, LANES)], [spot, elasticity],
                 [trade, productivity, workers, wage, sales], scratch,
             )
         got = exchange(send, "orig", by_outer)
@@ -302,10 +319,12 @@
             [(rows, LANES), (sectors, columns), (sectors, width)],
         )
         sales = exchange(made[0], "dest")
-    log_price = made[1]
-    raw, send = call(settle_kernel, [f32(pieces, LANES), f32(across, 1, LANES)], [], [workers, wage, sales])
+    raw, send = call(settle_kernel, [f32(pieces, LANES), f32(across, 2, LANES)], [], [workers, wage, sales])
     got = exchange(send, "orig")
-    wage, world = call(functools.partial(finish_kernel, cells), [f32(pieces, LANES), f32(1, LANES)], [], [raw, got])
+    wage, log_price, world = call(
+        functools.partial(finish_kernel, cells),
+        [f32(pieces, LANES), f32(sectors, columns), f32(1, LANES)], [], [raw, made[1], got],
+    )
     return wage.reshape(rows), log_price, world[0, 0]
 
 

time: 176 us -> 174 us (0.989)
  blocking collectives: 129 us -> 127 us
    all_to_all x9, blocking collectives: 129 us -> 127 us  [exchange(): return lax.all_to_all(x, axis, 0, 0, tiled=True, axis_index_groups=groups)]
where the time goes in v4:
time: 174 us; the launch traced here: 173 us
  blocking collectives  127 us (73%)
  Pallas kernels  18.8 us (11%)
  between operations  14.2 us (8%)
  waiting for transfers between devices  9.02 us (5%)
  starting transfers between devices  3.89 us (2%)
    all_to_all x9, blocking collectives, exchange(): return lax.all_to_all(x, axis, 0, 0, tiled=True, axis_index_groups=groups)  127 us
    pallas_call x11, Pallas kernels, call(): pl.pallas_call(body, out_shape=tuple(out_shape), in_specs=[SM] * len(scal...  18.8 us
    all_to_all x1, waiting for transfers between devices, exchange(): return lax.all_to_all(x, axis, 0, 0, tiled=True, axis_index_groups=groups)  9.02 us
    all_to_all x1, starting transfers between devices, exchange(): return lax.all_to_all(x, axis, 0, 0, tiled=True, axis_index_groups=groups)  3.89 us
  transfers between devices with their start and end apart: 1, of which 1 were waited for; matrix products, arithmetic and copies ran while one was open for 0% of the time, Pallas kernels for 0%

profile of v4, /device:TPU:1, one launch (start us, length us, event | category | flops | bytes accessed | tf_op | source)
XLA Modules:
  0.0 173.5 jit_solution(14248756333558400034)
XLA Ops:
  7.2 0.0 copy-start.5
  7.2 0.0 copy-start.2
  7.2 0.1 pad_add_fusion.spot_ref
  7.3 5.4 %shard_map.81 = (f32[4,8,1280]{2,1,0:T(8,128)S(1)}, f32[512,1024]{1,0:T(8,128)S(1)}, f32[8,512,1024]{2,1,0:T(8,128)S(1)}) custom-call(s32[2]{0:T(128)S(1)} %pad_add_fusion.spot_ref, f32[8]{0:T(128)} %slope_ref.11, f32[8,512]{1,0:T(8,128)} %productivity_ref.5, f32[4,128]{1,0:T(4,128)} %bitcast.111, f32[4,128]{1,0:T(4,128)} %bitcast.118, ...), custom_call_target="tpu_custom_call" | custom-call | tf_op jit(solution)/shard_map/pallas_call | solution.py:217
  12.7 13.2 %all_to_all.50.got_ref = f32[4,8,1280]{2,1,0:T(8,128)S(1)} all-to-all(f32[4,8,1280]{2,1,0:T(8,128)S(1)} %get-tuple-element.209), channel_id=1, replica_groups={{0,128,256,384},{16,144,272,400},{32,160,288,416},{48,176,304,432},{64,..., dimensions={0} | all-to-all | bytes 327680 | tf_op jit(solution)/shard_map/all_to_all | solution.py:228
  25.9 16.6 %all_to_all.51.got_ref = f32[8,8,1280]{2,1,0:T(8,128)S(1)} all-to-all(f32[8,8,1280]{2,1,0:T(8,128)S(1)} %shard_map.82), channel_id=1, replica_groups={{0,16,32,48,64,80,96,112},{128,144,160,176,192,208,224,240},{256,272,28..., dimensions={0} | all-to-all | bytes 655360 | tf_op jit(solution)/shard_map/all_to_all | solution.py:228
  42.5 0.0 copy-done.5
  42.5 0.0 copy-done.2
  42.5 0.0 copy-start
  42.5 0.0 copy-start.3
  42.5 0.0 copy-start.4
  42.5 2.5 %shard_map.83 = f32[16,4,128]{2,1,0:T(4,128)S(1)} custom-call(f32[8]{0:T(128)S(1)} %copy-done.5, f32[8,512,1024]{2,1,0:T(8,128)S(1)} %get-tuple-element.207.trade_ref, f32[512,1024]{1,0:T(8,128)S(1)} %get-tuple-element.208.spread_ref, f32[8,1024]{1,0:T(8,128)S(1)} %copy-done.2, f32[8,8,1280]{2,1,0:T(8,128)S(1)} %all_to_all.51.got_ref), custom_call_target="tpu_custom_call" | custom-call | tf_op jit(solution)/shard_map/pallas_call | solution.py:217
  45.0 23.9 %all_to_all.52.sales_ref = f32[16,4,128]{2,1,0:T(4,128)S(1)} all-to-all(f32[16,4,128]{2,1,0:T(4,128)S(1)} %shard_map.83), channel_id=1, replica_groups=mesh['orig'=32,'dest'=16] {'dest'}, dimensions={0} | all-to-all | bytes 65536 | tf_op jit(solution)/shard_map/all_to_all | solution.py:228
  68.9 0.0 copy-done
  68.9 0.0 copy-done.3
  68.9 0.0 copy-done.4
  68.9 2.4 %shard_map.84 = (f32[4,8,1152]{2,1,0:T(8,128)S(1)}, f32[512,1024]{1,0:T(8,128)S(1)}, f32[4,128]{1,0:T(4,128)S(1)}) custom-call(s32[2]{0:T(128)S(1)} %pad_add_fusion.spot_ref, f32[8]{0:T(128)S(1)} %copy-done.5, f32[8,512,1024]{2,1,0:T(8,128)S(1)} %get-tuple-element.207.trade_ref, f32[8,512]{1,0:T(8,128)S(1)} %copy-done, f32[4,128]{1,0:T(4,128)S(1)} %bitcast.112, ...), custom_call_target="tpu_custom_call" | custom-call | tf_op jit(solution)/shard_map/pallas_call | solution.py:217
  71.3 8.6 %all_to_all.53.got_ref = f32[4,8,1152]{2,1,0:T(8,128)S(1)} all-to-all(f32[4,8,1152]{2,1,0:T(8,128)S(1)} %get-tuple-element.212), channel_id=1, replica_groups={{0,128,256,384},{16,144,272,400},{32,160,288,416},{48,176,304,432},{64,..., dimensions={0} | all-to-all | bytes 294912 | tf_op jit(solution)/shard_map/all_to_all | solution.py:228
  79.9 12.2 %all_to_all.54.got_ref = f32[8,8,1152]{2,1,0:T(8,128)S(1)} all-to-all(f32[8,8,1152]{2,1,0:T(8,128)S(1)} %shard_map.85), channel_id=1, replica_groups={{0,16,32,48,64,80,96,112},{128,144,160,176,192,208,224,240},{256,272,28..., dimensions={0} | all-to-all | bytes 589824 | tf_op jit(solution)/shard_map/all_to_all | solution.py:228
  92.1 2.4 %shard_map.86 = f32[16,4,128]{2,1,0:T(4,128)S(1)} custom-call(f32[8]{0:T(128)S(1)} %copy-done.5, f32[8,512,1024]{2,1,0:T(8,128)S(1)} %get-tuple-element.207.trade_ref, f32[512,1024]{1,0:T(8,128)S(1)} %get-tuple-element.211.spread_ref, f32[8,1024]{1,0:T(8,128)S(1)} %copy-done.2, f32[8,8,1152]{2,1,0:T(8,128)S(1)} %all_to_all.54.got_ref), custom_call_target="tpu_custom_call" | custom-call | tf_op jit(solution)/shard_map/pallas_call | solution.py:217
  94.5 15.8 %all_to_all.55.sales_ref = f32[16,4,128]{2,1,0:T(4,128)S(1)} all-to-all(f32[16,4,128]{2,1,0:T(4,128)S(1)} %shard_map.86), channel_id=1, replica_groups=mesh['orig'=32,'dest'=16] {'dest'}, dimensions={0} | all-to-all | bytes 65536 | tf_op jit(solution)/shard_map/all_to_all | solution.py:228
  110.3 2.4 %shard_map.87 = (f32[4,8,1152]{2,1,0:T(8,128)S(1)}, f32[512,1024]{1,0:T(8,128)S(1)}, f32[4,128]{1,0:T(4,128)S(1)}) custom-call(s32[2]{0:T(128)S(1)} %pad_add_fusion.spot_ref, f32[8]{0:T(128)S(1)} %copy-done.5, f32[8,512,1024]{2,1,0:T(8,128)S(1)} %get-tuple-element.207.trade_ref, f32[8,512]{1,0:T(8,128)S(1)} %copy-done, f32[4,128]{1,0:T(4,128)S(1)} %bitcast.113, ...), custom_call_target="tpu_custom_call" | custom-call | tf_op jit(solution)/shard_map/pallas_call | solution.py:217
  112.7 8.8 %all_to_all.56.got_ref = f32[4,8,1152]{2,1,0:T(8,128)S(1)} all-to-all(f32[4,8,1152]{2,1,0:T(8,128)S(1)} %get-tuple-element.215), channel_id=1, replica_groups={{0,128,256,384},{16,144,272,400},{32,160,288,416},{48,176,304,432},{64,..., dimensions={0} | all-to-all | bytes 294912 | tf_op jit(solution)/shard_map/all_to_all | solution.py:228
  121.5 12.2 %all_to_all.57.got_ref = f32[8,8,1152]{2,1,0:T(8,128)S(1)} all-to-all(f32[8,8,1152]{2,1,0:T(8,128)S(1)} %shard_map.88), channel_id=1, replica_groups={{0,16,32,48,64,80,96,112},{128,144,160,176,192,208,224,240},{256,272,28..., dimensions={0} | all-to-all | bytes 589824 | tf_op jit(solution)/shard_map/all_to_all | solution.py:228
  133.7 2.4 %shard_map.89 = (f32[16,4,128]{2,1,0:T(4,128)S(1)}, f32[8,1024]{1,0:T(8,128)S(1)}) custom-call(f32[8]{0:T(128)S(1)} %copy-done.5, f32[8,512,1024]{2,1,0:T(8,128)S(1)} %get-tuple-element.207.trade_ref, f32[512,1024]{1,0:T(8,128)S(1)} %get-tuple-element.214.spread_ref, f32[8,1024]{1,0:T(8,128)S(1)} %copy-done.2, f32[8,8,1152]{2,1,0:T(8,128)S(1)} %all_to_all.57.got_ref), custom_call_target="tpu_custom_call" | custom-call | tf_op jit(solution)/shard_map/pallas_call | solution.py:217
  136.1 15.8 %all_to_all.58.sales_ref = f32[16,4,128]{2,1,0:T(4,128)S(1)} all-to-all(f32[16,4,128]{2,1,0:T(4,128)S(1)} %get-tuple-element.216), channel_id=1, replica_groups=mesh['orig'=32,'dest'=16] {'dest'}, dimensions={0} | all-to-all | bytes 65536 | tf_op jit(solution)/shard_map/all_to_all | solution.py:228
  152.0 0.7 shard_map.90
  152.6 3.9 %all-to-all-start.9 = ((f32[32,2,128]{2,1,0:T(2,128)}), f32[32,2,128]{2,1,0:T(2,128)S(1)}, u32[]{:S(2)}, u32[]{:S(2)}) async-start(f32[32,2,128]{2,1,0:T(2,128)} %get-tuple-element.219), calls=%async_computation.12 | async-start | bytes 65536 | tf_op jit(solution)/shard_map/all_to_all | solution.py:228
  156.5 9.0 %all-to-all-done.9.got_ref = f32[32,2,128]{2,1,0:T(2,128)S(1)} async-done(((f32[32,2,128]{2,1,0:T(2,128)}), f32[32,2,128]{2,1,0:T(2,128)S(1)}, u32[]{:S(2)}, u32[]{:S(2)}) %all-to-all-start.9) | async-done | bytes 32800 | tf_op jit(solution)/shard_map/all_to_all | solution.py:228
  165.6 0.7 shard_map.91
  166.4 0.0 copy-done.1
  166.4 0.2 conditional.1
  (4 shorter events, 0.1 us)
Async XLA Ops:
  7.2 35.4 %copy-start.5 = (f32[8]{0:T(128)S(1)}, f32[8]{0:T(128)}, u32[]{:S(2)}) copy-start(f32[8]{0:T(128)} %slope_ref.11) | copy-start | bytes 100
  7.2 35.3 %copy-start.2 = (f32[8,1024]{1,0:T(8,128)S(1)}, f32[8,1024]{1,0:T(8,128)}, u32[]{:S(2)}) copy-start(f32[8,1024]{1,0:T(8,128)} %preference_ref.5) | copy-start | bytes 98308
  42.5 26.4 %copy-start = (f32[8,512]{1,0:T(8,128)S(1)}, f32[8,512]{1,0:T(8,128)}, u32[]{:S(2)}) copy-start(f32[8,512]{1,0:T(8,128)} %productivity_ref.5) | copy-start | bytes 49156
  42.5 26.4 %copy-start.3 = (f32[512]{0:T(512)S(1)}, f32[512]{0:T(512)}, u32[]{:S(2)}) copy-start(f32[512]{0:T(512)} %param.24) | copy-start | bytes 6148
  42.5 26.4 %copy-start.4 = (f32[512]{0:T(512)S(1)}, f32[512]{0:T(512)}, u32[]{:S(2)}) copy-start(f32[512]{0:T(512)} %param.25) | copy-start | bytes 6148
  133.7 32.6 %copy-start.1 = (bf16[512,1024]{1,0:T(8,128)(2,1)S(1)}, bf16[512,1024]{1,0:T(8,128)(2,1)}, u32[]{:S(2)}) copy-start(bf16[512,1024]{1,0:T(8,128)(2,1)} %cost_in_ref.1) | copy-start | bytes 3145732
  152.6 12.9 %all-to-all-start.9 = ((f32[32,2,128]{2,1,0:T(2,128)}), f32[32,2,128]{2,1,0:T(2,128)S(1)}, u32[]{:S(2)}, u32[]{:S(2)}) async-start(f32[32,2,128]{2,1,0:T(2,128)} %get-tuple-element.219), calls=%async_computation.12 | async-start | bytes 65536 | tf_op jit(solution)/shard_map/all_to_all | solution.py:228

commit v5 on v4

--- a/solution.py
+++ b/solution.py
@@ -67,10 +67,10 @@
     )
 
 
-def prepare(spot_ref, slope_ref, columns, productivity_ref, workers_ref, wage, part_ref, spread_ref, supply_ref):
+def prepare(slopes, here, columns, productivity_ref, workers_ref, wage, part_ref, spread_ref, supply_ref):
     sectors, rows = productivity_ref.shape
     pieces = rows // LANES
-    supply = supply_of(pick(slope_ref, sectors), productivity_ref, wage)
+    supply = supply_of(slopes, productivity_ref, wage)
     for p in range(pieces):
         supply_ref[:, p * LANES:(p + 1) * LANES] = supply[p]
     spread_over_lanes(supply_ref, spread_ref)
@@ -78,10 +78,8 @@
     least = jnp.min(jnp.min(least, axis=0, keepdims=True), axis=1, keepdims=True)
     income = wage * workers_ref[...]
     guarded = jnp.where(least > SMALLEST, income, jnp.nan)
-    part = spot_ref[0] - spot_ref[1] * (columns // rows)
     for i in range(columns // rows):
-        here = jnp.where(part == i, 1.0, 0.0)
-        part_ref[i * pieces:(i + 1) * pieces, columns:columns + LANES] = guarded * here
+        part_ref[i * pieces:(i + 1) * pieces, columns:columns + LANES] = guarded * here[i:i + 1]
     if part_ref.shape[1] > columns + LANES:
         part_ref[:, columns + LANES:] = jnp.zeros((sectors, LANES), jnp.float32)
         part_ref[:pieces, columns + LANES:] = income
@@ -98,16 +96,34 @@
         send_ref[copy] = part
 
 
-def first_phi_kernel(spot_ref, slope_ref, productivity_ref, workers_ref, wage_ref, cost_in_ref, send_ref, spread_ref, trade_ref, totals_ref, supply_ref, part_ref, cost_ref, arrived):
+def first_phi_kernel(
+    spot_ref, slope_ref, cost_in_ref, productivity_in_ref, workers_in_ref, wage_in_ref,
+    send_ref, spread_ref, trade_ref, facts_ref,
+    totals_ref, supply_ref, part_ref, cost_ref, productivity_ref, workers_ref, wage_ref, arrived, brought,
+):
     sectors, rows = productivity_ref.shape
     columns = cost_ref.shape[1]
     batch, height = rows // arrived.shape[0], 32
+    small = [
+        pltpu.make_async_copy(given, held, brought.at[i])
+        for i, (given, held) in enumerate(
+            ((wage_in_ref, wage_ref), (productivity_in_ref, productivity_ref), (workers_in_ref, workers_ref))
+        )
+    ]
     copies = []
     for i in range(arrived.shape[0]):
         some = pl.ds(i * batch, batch)
         copies.append(pltpu.make_async_copy(cost_in_ref.at[some], cost_ref.at[some], arrived.at[i]))
-        copies[-1].start()
-    prepare(spot_ref, slope_ref, columns, productivity_ref, workers_ref, wage_ref[...], part_ref, spread_ref, supply_ref)
+    for copy in small + copies:
+        copy.start()
+    part = spot_ref[0] - spot_ref[1] * (columns // rows)
+    facts_ref[:sectors, :] = pick(slope_ref, sectors)
+    row = lax.broadcasted_iota(jnp.int32, (sectors, LANES), 0)
+    facts_ref[sectors:, :] = jnp.where(row == part, 1.0, 0.0)
+    for copy in small:
+        copy.wait()
+    facts = facts_ref[...]
+    prepare(facts[:sectors], facts[sectors:], columns, productivity_ref, workers_ref, wage_ref[...], part_ref, spread_ref, supply_ref)
     slopes = [-slope_ref[j] for j in range(sectors)]
     totals_ref[...] = jnp.zeros_like(totals_ref)
 
@@ -129,12 +145,12 @@
     send_phi(totals_ref, part_ref, send_ref)
 
 
-def phi_kernel(gain, spot_ref, slope_ref, trade_ref, productivity_ref, workers_ref, wage_ref, sales_ref, send_ref, spread_ref, new_wage_ref, totals_ref, supply_ref, part_ref):
+def phi_kernel(gain, facts_ref, trade_ref, productivity_ref, workers_ref, wage_ref, sales_ref, send_ref, spread_ref, new_wage_ref, totals_ref, supply_ref, part_ref):
     sectors, rows, columns = trade_ref.shape
     blocks = columns // LANES
     wage = next_wage(wage_ref, workers_ref, sales_ref, gain)
     new_wage_ref[...] = wage
-    prepare(spot_ref, slope_ref, columns, productivity_ref, workers_ref, wage, part_ref, spread_ref, supply_ref)
+    prepare(facts_ref[:sectors], facts_ref[sectors:], columns, productivity_ref, workers_ref, wage, part_ref, spread_ref, supply_ref)
     for j in range(sectors):
         def step(block, totals):
             at = pl.ds(pl.multiple_of(block * 8, 8), 8)
@@ -154,7 +170,7 @@
         send_ref[copy] = total
 
 
-def sales_kernel(last, cells, slope_ref, trade_ref, spread_ref, preference_ref, got_ref, send_ref, *rest):
+def sales_kernel(last, cells, facts_ref, trade_ref, spread_ref, preference_ref, got_ref, send_ref, *rest):
     total_ref, ratio_ref, sums_ref = rest[-3:]
     sectors, rows, columns = trade_ref.shape
     blocks = columns // LANES
@@ -170,7 +186,7 @@
         centred = CENTRE * cells / total_of(sums_ref[:, columns + LANES:])
         ratio_ref[...] *= centred * centred
     if last:
-        slopes = pick(slope_ref, sectors)
+        slopes = facts_ref[:sectors]
         for k in range(blocks):
             lanes = slice(k * LANES, (k + 1) * LANES)
             rest[0][:, lanes] = -jnp.log(sums_ref[:, lanes]) / slopes
@@ -296,17 +312,17 @@
         outs = [f32(outer, sectors, width), f32(rows, sectors * LANES)]
         scratch = [(sectors, 8, columns), (sectors, rows), (sectors, width)]
         if step == 0:
-            send, spread, trade = call(
-                first_phi_kernel, outs + [f32(sectors, rows, columns)], [spot, elasticity],
-                [productivity, workers, wage],
-                scratch + [pltpu.VMEM(log_cost.shape, log_cost.dtype), pltpu.SemaphoreType.DMA((2,))],
-                [log_cost],
+            send, spread, trade, facts = call(
+                first_phi_kernel, outs + [f32(sectors, rows, columns), f32(2 * sectors, LANES)], [spot, elasticity], [],
+                scratch + [pltpu.VMEM(log_cost.shape, log_cost.dtype), (sectors, rows), (pieces, LANES), (pieces, LANES)]
+                + [pltpu.SemaphoreType.DMA((2,)), pltpu.SemaphoreType.DMA((3,))],
+                [log_cost, productivity, workers, wage],
             )
         else:
             send, spread, wage = call(
                 functools.partial(phi_kernel, 1.0 if step == 1 else GAIN),
-                outs + [f32(pieces, LANES)], [spot, elasticity],
-                [trade, productivity, workers, wage, sales], scratch,
+                outs + [f32(pieces, LANES)], [],
+                [facts, trade, productivity, workers, wage, sales], scratch,
             )
         got = exchange(send, "orig", by_outer)
         send, = call(sum_kernel, [f32(INNER, sectors, width)], [], [got])
@@ -314,8 +330,8 @@
         made = call(
             functools.partial(sales_kernel, last, cells),
             [f32(along, pieces, LANES)] + ([f32(sectors, columns)] if last else []),
-            [elasticity],
-            [trade, spread, preference, got],
+            [],
+            [facts, trade, spread, preference, got],
             [(rows, LANES), (sectors, columns), (sectors, width)],
         )
         sales = exchange(made[0], "dest")

time: 174 us -> 172 us (0.989)
  Pallas kernels: 18.8 us -> 16.4 us
    pallas_call x11, Pallas kernels: 18.8 us -> 16.4 us  [call(): pl.pallas_call(body, out_shape=tuple(out_shape), in_specs=[SM] * len(scal...]
where the time goes in v5:
time: 172 us; the launch traced here: 171 us
  blocking collectives  127 us (74%)
  Pallas kernels  16.4 us (10%)
  between operations  14.2 us (8%)
  waiting for transfers between devices  9.02 us (5%)
  starting transfers between devices  3.88 us (2%)
    all_to_all x9, blocking collectives, exchange(): return lax.all_to_all(x, axis, 0, 0, tiled=True, axis_index_groups=groups)  127 us
    pallas_call x11, Pallas kernels, call(): pl.pallas_call(body, out_shape=tuple(out_shape), in_specs=[SM] * len(scal...  16.4 us
    all_to_all x1, waiting for transfers between devices, exchange(): return lax.all_to_all(x, axis, 0, 0, tiled=True, axis_index_groups=groups)  9.02 us
    all_to_all x1, starting transfers between devices, exchange(): return lax.all_to_all(x, axis, 0, 0, tiled=True, axis_index_groups=groups)  3.88 us
  transfers between devices with their start and end apart: 1, of which 1 were waited for; matrix products, arithmetic and copies ran while one was open for 0% of the time, Pallas kernels for 0%

profile of v5, /device:TPU:1, one launch (start us, length us, event | category | flops | bytes accessed | tf_op | source)
XLA Modules:
  0.0 171.0 jit_solution(11291463200222219489)
XLA Ops:
  7.2 0.0 copy-start.2
  7.2 0.1 pad_add_fusion.spot_ref
  7.3 5.2 %shard_map.81 = (f32[4,8,1280]{2,1,0:T(8,128)S(1)}, f32[512,1024]{1,0:T(8,128)S(1)}, f32[8,512,1024]{2,1,0:T(8,128)S(1)}, f32[16,128]{1,0:T(8,128)S(1)}) custom-call(s32[2]{0:T(128)S(1)} %pad_add_fusion.spot_ref, f32[8]{0:T(128)} %slope_ref.1, bf16[512,1024]{1,0:T(8,128)(2,1)} %cost_in_ref.1, f32[8,512]{1,0:T(8,128)} %productivity_ref.3, ...), custom_call_target="tpu_custom_call" | custom-call | tf_op jit(solution)/shard_map/pallas_call | solution.py:233
  12.5 13.2 %all_to_all.50.got_ref = f32[4,8,1280]{2,1,0:T(8,128)S(1)} all-to-all(f32[4,8,1280]{2,1,0:T(8,128)S(1)} %get-tuple-element.211), channel_id=1, replica_groups={{0,128,256,384},{16,144,272,400},{32,160,288,416},{48,176,304,432},{64,..., dimensions={0} | all-to-all | bytes 327680 | tf_op jit(solution)/shard_map/all_to_all | solution.py:244
  25.7 16.6 %all_to_all.51.got_ref = f32[8,8,1280]{2,1,0:T(8,128)S(1)} all-to-all(f32[8,8,1280]{2,1,0:T(8,128)S(1)} %shard_map.82), channel_id=1, replica_groups={{0,16,32,48,64,80,96,112},{128,144,160,176,192,208,224,240},{256,272,28..., dimensions={0} | all-to-all | bytes 655360 | tf_op jit(solution)/shard_map/all_to_all | solution.py:244
  42.4 0.0 copy-done.2
  42.4 0.0 copy-start.3
  42.4 0.0 copy-start.4
  42.4 2.0 %shard_map.83 = f32[16,4,128]{2,1,0:T(4,128)S(1)} custom-call(f32[16,128]{1,0:T(8,128)S(1)} %get-tuple-element.208.facts_ref, f32[8,512,1024]{2,1,0:T(8,128)S(1)} %get-tuple-element.209.trade_ref, f32[512,1024]{1,0:T(8,128)S(1)} %get-tuple-element.210.spread_ref, f32[8,1024]{1,0:T(8,128)S(1)} %copy-done.2, f32[8,8,1280]{2,1,0:T(8,128)S(1)} %all_to_all.51.got_ref), custom_call_target="tpu_custom_call" | custom-call | tf_op jit(solution)/shard_map/pallas_call | solution.py:233
  44.4 23.9 %all_to_all.52.sales_ref = f32[16,4,128]{2,1,0:T(4,128)S(1)} all-to-all(f32[16,4,128]{2,1,0:T(4,128)S(1)} %shard_map.83), channel_id=1, replica_groups=mesh['orig'=32,'dest'=16] {'dest'}, dimensions={0} | all-to-all | bytes 65536 | tf_op jit(solution)/shard_map/all_to_all | solution.py:244
  68.3 0.0 copy-done
  68.3 0.0 copy-done.3
  68.3 0.0 copy-done.4
  68.3 1.9 %shard_map.84 = (f32[4,8,1152]{2,1,0:T(8,128)S(1)}, f32[512,1024]{1,0:T(8,128)S(1)}, f32[4,128]{1,0:T(4,128)S(1)}) custom-call(f32[16,128]{1,0:T(8,128)S(1)} %get-tuple-element.208.facts_ref, f32[8,512,1024]{2,1,0:T(8,128)S(1)} %get-tuple-element.209.trade_ref, f32[8,512]{1,0:T(8,128)S(1)} %copy-done, f32[4,128]{1,0:T(4,128)S(1)} %bitcast.112, ...), custom_call_target="tpu_custom_call" | custom-call | tf_op jit(solution)/shard_map/pallas_call | solution.py:233
  70.2 8.6 %all_to_all.53.got_ref = f32[4,8,1152]{2,1,0:T(8,128)S(1)} all-to-all(f32[4,8,1152]{2,1,0:T(8,128)S(1)} %get-tuple-element.214), channel_id=1, replica_groups={{0,128,256,384},{16,144,272,400},{32,160,288,416},{48,176,304,432},{64,..., dimensions={0} | all-to-all | bytes 294912 | tf_op jit(solution)/shard_map/all_to_all | solution.py:244
  78.8 12.2 %all_to_all.54.got_ref = f32[8,8,1152]{2,1,0:T(8,128)S(1)} all-to-all(f32[8,8,1152]{2,1,0:T(8,128)S(1)} %shard_map.85), channel_id=1, replica_groups={{0,16,32,48,64,80,96,112},{128,144,160,176,192,208,224,240},{256,272,28..., dimensions={0} | all-to-all | bytes 589824 | tf_op jit(solution)/shard_map/all_to_all | solution.py:244
  91.0 1.9 %shard_map.86 = f32[16,4,128]{2,1,0:T(4,128)S(1)} custom-call(f32[16,128]{1,0:T(8,128)S(1)} %get-tuple-element.208.facts_ref, f32[8,512,1024]{2,1,0:T(8,128)S(1)} %get-tuple-element.209.trade_ref, f32[512,1024]{1,0:T(8,128)S(1)} %get-tuple-element.213.spread_ref, f32[8,1024]{1,0:T(8,128)S(1)} %copy-done.2, f32[8,8,1152]{2,1,0:T(8,128)S(1)} %all_to_all.54.got_ref), custom_call_target="tpu_custom_call" | custom-call | tf_op jit(solution)/shard_map/pallas_call | solution.py:233
  92.9 15.8 %all_to_all.55.sales_ref = f32[16,4,128]{2,1,0:T(4,128)S(1)} all-to-all(f32[16,4,128]{2,1,0:T(4,128)S(1)} %shard_map.86), channel_id=1, replica_groups=mesh['orig'=32,'dest'=16] {'dest'}, dimensions={0} | all-to-all | bytes 65536 | tf_op jit(solution)/shard_map/all_to_all | solution.py:244
  108.8 1.9 %shard_map.87 = (f32[4,8,1152]{2,1,0:T(8,128)S(1)}, f32[512,1024]{1,0:T(8,128)S(1)}, f32[4,128]{1,0:T(4,128)S(1)}) custom-call(f32[16,128]{1,0:T(8,128)S(1)} %get-tuple-element.208.facts_ref, f32[8,512,1024]{2,1,0:T(8,128)S(1)} %get-tuple-element.209.trade_ref, f32[8,512]{1,0:T(8,128)S(1)} %copy-done, f32[4,128]{1,0:T(4,128)S(1)} %bitcast.113, ...), custom_call_target="tpu_custom_call" | custom-call | tf_op jit(solution)/shard_map/pallas_call | solution.py:233
  110.7 8.8 %all_to_all.56.got_ref = f32[4,8,1152]{2,1,0:T(8,128)S(1)} all-to-all(f32[4,8,1152]{2,1,0:T(8,128)S(1)} %get-tuple-element.217), channel_id=1, replica_groups={{0,128,256,384},{16,144,272,400},{32,160,288,416},{48,176,304,432},{64,..., dimensions={0} | all-to-all | bytes 294912 | tf_op jit(solution)/shard_map/all_to_all | solution.py:244
  119.5 12.2 %all_to_all.57.got_ref = f32[8,8,1152]{2,1,0:T(8,128)S(1)} all-to-all(f32[8,8,1152]{2,1,0:T(8,128)S(1)} %shard_map.88), channel_id=1, replica_groups={{0,16,32,48,64,80,96,112},{128,144,160,176,192,208,224,240},{256,272,28..., dimensions={0} | all-to-all | bytes 589824 | tf_op jit(solution)/shard_map/all_to_all | solution.py:244
  131.8 0.0 copy-start.1
  131.8 0.0 copy-start.5
  131.8 1.9 %shard_map.89 = (f32[16,4,128]{2,1,0:T(4,128)S(1)}, f32[8,1024]{1,0:T(8,128)S(1)}) custom-call(f32[16,128]{1,0:T(8,128)S(1)} %get-tuple-element.208.facts_ref, f32[8,512,1024]{2,1,0:T(8,128)S(1)} %get-tuple-element.209.trade_ref, f32[512,1024]{1,0:T(8,128)S(1)} %get-tuple-element.216.spread_ref, f32[8,1024]{1,0:T(8,128)S(1)} %copy-done.2, ...), custom_call_target="tpu_custom_call" | custom-call | tf_op jit(solution)/shard_map/pallas_call | solution.py:233
  133.7 15.8 %all_to_all.58.sales_ref = f32[16,4,128]{2,1,0:T(4,128)S(1)} all-to-all(f32[16,4,128]{2,1,0:T(4,128)S(1)} %get-tuple-element.218), channel_id=1, replica_groups=mesh['orig'=32,'dest'=16] {'dest'}, dimensions={0} | all-to-all | bytes 65536 | tf_op jit(solution)/shard_map/all_to_all | solution.py:244
  149.6 0.7 shard_map.90
  150.2 3.9 %all-to-all-start.9 = ((f32[32,2,128]{2,1,0:T(2,128)}), f32[32,2,128]{2,1,0:T(2,128)S(1)}, u32[]{:S(2)}, u32[]{:S(2)}) async-start(f32[32,2,128]{2,1,0:T(2,128)} %get-tuple-element.221), calls=%async_computation.12 | async-start | bytes 65536 | tf_op jit(solution)/shard_map/all_to_all | solution.py:244
  154.1 9.0 %all-to-all-done.9.got_ref = f32[32,2,128]{2,1,0:T(2,128)S(1)} async-done(((f32[32,2,128]{2,1,0:T(2,128)}), f32[32,2,128]{2,1,0:T(2,128)S(1)}, u32[]{:S(2)}, u32[]{:S(2)}) %all-to-all-start.9) | async-done | bytes 32800 | tf_op jit(solution)/shard_map/all_to_all | solution.py:244
  163.1 0.7 shard_map.91
  163.9 0.0 copy-done.1
  163.9 0.0 copy-done.5
  163.9 0.2 conditional.1
  (4 shorter events, 0.1 us)
Async XLA Ops:
  7.2 35.2 %copy-start.2 = (f32[8,1024]{1,0:T(8,128)S(1)}, f32[8,1024]{1,0:T(8,128)}, u32[]{:S(2)}) copy-start(f32[8,1024]{1,0:T(8,128)} %preference_ref.5) | copy-start | bytes 98308
  42.4 25.9 %copy-start = (f32[8,512]{1,0:T(8,128)S(1)}, f32[8,512]{1,0:T(8,128)}, u32[]{:S(2)}) copy-start(f32[8,512]{1,0:T(8,128)} %productivity_ref.3) | copy-start | bytes 49156
  42.4 25.9 %copy-start.3 = (f32[512]{0:T(512)S(1)}, f32[512]{0:T(512)}, u32[]{:S(2)}) copy-start(f32[512]{0:T(512)} %param.24) | copy-start | bytes 6148
  42.4 25.9 %copy-start.4 = (f32[512]{0:T(512)S(1)}, f32[512]{0:T(512)}, u32[]{:S(2)}) copy-start(f32[512]{0:T(512)} %param.25) | copy-start | bytes 6148
  131.8 32.1 %copy-start.1 = (bf16[512,1024]{1,0:T(8,128)(2,1)S(1)}, bf16[512,1024]{1,0:T(8,128)(2,1)}, u32[]{:S(2)}) copy-start(bf16[512,1024]{1,0:T(8,128)(2,1)} %cost_in_ref.1) | copy-start | bytes 3145732
  131.8 32.2 %copy-start.5 = (f32[8]{0:T(128)S(1)}, f32[8]{0:T(128)}, u32[]{:S(2)}) copy-start(f32[8]{0:T(128)} %slope_ref.1) | copy-start | bytes 100
  150.2 12.9 %all-to-all-start.9 = ((f32[32,2,128]{2,1,0:T(2,128)}), f32[32,2,128]{2,1,0:T(2,128)S(1)}, u32[]{:S(2)}, u32[]{:S(2)}) async-start(f32[32,2,128]{2,1,0:T(2,128)} %get-tuple-element.221), calls=%async_computation.12 | async-start | bytes 65536 | tf_op jit(solution)/shard_map/all_to_all | solution.py:244

commit v6 on v5

--- a/solution.py
+++ b/solution.py
@@ -244,23 +244,24 @@
     return lax.all_to_all(x, axis, 0, 0, tiled=True, axis_index_groups=groups)
 
 
+def gather(x, axis):
+    return exchange(jnp.broadcast_to(x, (lax.axis_size(axis), *x.shape)), axis)
+
+
 def careful(log_cost, elasticity, productivity, preference, workers, start_wage):
-    rows = log_cost.shape[0]
-    columns = log_cost.shape[1]
-    cells = rows * lax.axis_size("orig")
+    rows, columns = log_cost.shape
+    sectors = elasticity.shape[0]
+    across = lax.axis_size("orig")
+    cells, width = rows * across, columns // across
     spend_share = preference / jnp.sum(preference, axis=0, keepdims=True)
 
     def settle(raw_wage, wanted):
-        local_income = None
-        world_income = lax.psum(jnp.sum(raw_wage * workers), "orig")
-        factor = cells / world_income
-        wage = raw_wage * factor
-        if wanted:
-            incomes = lax.all_gather(wage * workers, "orig", axis=0, tiled=True)
-            local_income = lax.dynamic_slice_in_dim(
-                incomes, lax.axis_index("dest") * columns, columns
-            )
-        return (wage, local_income)
+        world_income = jnp.sum(gather(jnp.sum(raw_wage * workers, keepdims=True), "orig"))
+        wage = raw_wage * (cells / world_income)
+        if not wanted:
+            return wage, None
+        incomes = gather(wage * workers, "orig").reshape(cells)
+        return wage, lax.dynamic_slice_in_dim(incomes, lax.axis_index("dest") * columns, columns)
 
     def kernel_of(slope):
         return jnp.exp(-slope * log_cost.astype(jnp.float32))
@@ -270,27 +271,22 @@
 
     def sales_term(pair):
         return jnp.dot(kernel_of(pair[0]), pair[1], precision=lax.Precision.HIGHEST)
+
+    def whole(x):
+        return jnp.moveaxis(gather(x, "orig"), 0, 1).reshape(sectors, columns)
 
     wage, dest_income = settle(start_wage, True)
     for step in range(ITERS):
         supply = productivity * jnp.exp(-elasticity[:, None] * jnp.log(wage)[None, :])
         spending = spend_share * dest_income[None, :]
-        partial_phi = lax.map(phi_term, (elasticity, supply))
-        price_part = lax.psum_scatter(partial_phi, "orig", scatter_dimension=1, tiled=True)
-        part_width = price_part.shape[1]
-        own_spending = lax.dynamic_slice_in_dim(
-            spending, lax.axis_index("orig") * part_width, part_width, 1
-        )
-        ratio, log_price = (
-            lax.all_gather(own_spending / price_part, "orig", axis=1, tiled=True),
-            lax.all_gather(-jnp.log(price_part) / elasticity[:, None], "orig", axis=1, tiled=True),
-        )
-        partial_sales = lax.map(sales_term, (elasticity, ratio))
-        sector_sales = lax.psum(partial_sales, "dest")
-        revenue = jnp.sum(supply * sector_sales, axis=0)
+        partial_phi = lax.map(phi_term, (elasticity, supply)).reshape(sectors, across, width)
+        phi = whole(jnp.sum(exchange(jnp.moveaxis(partial_phi, 1, 0), "orig"), axis=0))
+        log_price = -jnp.log(phi) / elasticity[:, None]
+        partial_sales = lax.map(sales_term, (elasticity, spending / phi))
+        revenue = jnp.sum(gather(jnp.sum(supply * partial_sales, axis=0), "dest"), axis=0)
         raw_wage = wage * jnp.sqrt(revenue / (wage * workers))
         wage, dest_income = settle(raw_wage, step + 1 < ITERS)
-    return (wage, log_price)
+    return wage, log_price
 
 
 def fast(log_cost, elasticity, productivity, preference, workers, start_wage):

time: 172 us -> 158 us (0.919)
  between operations: 14.2 us -> 0.95 us
where the time goes in v6:
time: 158 us
  blocking collectives  127 us (80%)
  Pallas kernels  16.3 us (10%)
  waiting for transfers between devices  9.02 us (6%)
  starting transfers between devices  3.89 us (2%)
    all_to_all x9, blocking collectives, exchange(): return lax.all_to_all(x, axis, 0, 0, tiled=True, axis_index_groups=groups)  127 us
    pallas_call x11, Pallas kernels, call(): pl.pallas_call(body, out_shape=tuple(out_shape), in_specs=[SM] * len(scal...  16.3 us
    all_to_all x1, waiting for transfers between devices, exchange(): return lax.all_to_all(x, axis, 0, 0, tiled=True, axis_index_groups=groups)  9.02 us
    all_to_all x1, starting transfers between devices, exchange(): return lax.all_to_all(x, axis, 0, 0, tiled=True, axis_index_groups=groups)  3.89 us
  transfers between devices with their start and end apart: 1, of which 1 were waited for; matrix products, arithmetic and copies ran while one was open for 0% of the time, Pallas kernels for 0%

profile of v6, /device:TPU:1, one launch (start us, length us, event | category | flops | bytes accessed | tf_op | source)
XLA Modules:
  0.0 157.7 jit_solution(5846652817590639908)
XLA Ops:
  0.6 0.0 copy-start
  0.6 0.1 pad_add_fusion.spot_ref
  0.7 5.1 %shard_map.81 = (f32[4,8,1280]{2,1,0:T(8,128)S(1)}, f32[512,1024]{1,0:T(8,128)S(1)}, f32[8,512,1024]{2,1,0:T(8,128)S(1)}, f32[16,128]{1,0:T(8,128)S(1)}) custom-call(s32[2]{0:T(128)S(1)} %pad_add_fusion.spot_ref, f32[8]{0:T(128)} %slope_ref.1, bf16[512,1024]{1,0:T(8,128)(2,1)} %cost_in_ref.1, f32[8,512]{1,0:T(8,128)} %productivity_ref.3, f32[4,128]{1,0:T(4,128)} %bitcast.83, ...), custom_call_target="tpu_custom_call" | custom-call | tf_op jit(solution)/shard_map/pallas_call | solution.py:233
  5.8 13.2 %all_to_all.127.got_ref = f32[4,8,1280]{2,1,0:T(8,128)S(1)} all-to-all(f32[4,8,1280]{2,1,0:T(8,128)S(1)} %get-tuple-element.211), channel_id=1, replica_groups={{0,128,256,384},{16,144,272,400},{32,160,288,416},{48,176,304,432},{64,..., dimensions={0} | all-to-all | bytes 327680 | tf_op jit(solution)/shard_map/all_to_all | solution.py:244
  19.0 16.7 %all_to_all.128.got_ref = f32[8,8,1280]{2,1,0:T(8,128)S(1)} all-to-all(f32[8,8,1280]{2,1,0:T(8,128)S(1)} %shard_map.82), channel_id=1, replica_groups={{0,16,32,48,64,80,96,112},{128,144,160,176,192,208,224,240},{256,272,28..., dimensions={0} | all-to-all | bytes 655360 | tf_op jit(solution)/shard_map/all_to_all | solution.py:244
  35.7 0.0 copy-done
  35.7 0.0 copy-start.1
  35.7 0.0 copy-start.3
  35.7 0.0 copy-start.4
  35.7 2.0 %shard_map.83 = f32[16,4,128]{2,1,0:T(4,128)S(1)} custom-call(f32[16,128]{1,0:T(8,128)S(1)} %get-tuple-element.208.facts_ref, f32[8,512,1024]{2,1,0:T(8,128)S(1)} %get-tuple-element.209.trade_ref, f32[512,1024]{1,0:T(8,128)S(1)} %get-tuple-element.210.spread_ref, f32[8,1024]{1,0:T(8,128)S(1)} %copy-done, f32[8,8,1280]{2,1,0:T(8,128)S(1)} %all_to_all.128.got_ref), custom_call_target="tpu_custom_call" | custom-call | tf_op jit(solution)/shard_map/pallas_call | solution.py:233
  37.7 23.9 %all_to_all.129.sales_ref = f32[16,4,128]{2,1,0:T(4,128)S(1)} all-to-all(f32[16,4,128]{2,1,0:T(4,128)S(1)} %shard_map.83), channel_id=1, replica_groups=mesh['orig'=32,'dest'=16] {'dest'}, dimensions={0} | all-to-all | bytes 65536 | tf_op jit(solution)/shard_map/all_to_all | solution.py:244
  61.6 0.0 copy-done.1
  61.6 0.0 copy-done.3
  61.6 0.0 copy-done.4
  61.6 1.9 %shard_map.84 = (f32[4,8,1152]{2,1,0:T(8,128)S(1)}, f32[512,1024]{1,0:T(8,128)S(1)}, f32[4,128]{1,0:T(4,128)S(1)}) custom-call(f32[16,128]{1,0:T(8,128)S(1)} %get-tuple-element.208.facts_ref, f32[8,512,1024]{2,1,0:T(8,128)S(1)} %get-tuple-element.209.trade_ref, f32[8,512]{1,0:T(8,128)S(1)} %copy-done.1, f32[4,128]{1,0:T(4,128)S(1)} %bitcast.84, ...), custom_call_target="tpu_custom_call" | custom-call | tf_op jit(solution)/shard_map/pallas_call | solution.py:233
  63.5 8.6 %all_to_all.130.got_ref = f32[4,8,1152]{2,1,0:T(8,128)S(1)} all-to-all(f32[4,8,1152]{2,1,0:T(8,128)S(1)} %get-tuple-element.214), channel_id=1, replica_groups={{0,128,256,384},{16,144,272,400},{32,160,288,416},{48,176,304,432},{64,..., dimensions={0} | all-to-all | bytes 294912 | tf_op jit(solution)/shard_map/all_to_all | solution.py:244
  72.1 12.2 %all_to_all.131.got_ref = f32[8,8,1152]{2,1,0:T(8,128)S(1)} all-to-all(f32[8,8,1152]{2,1,0:T(8,128)S(1)} %shard_map.85), channel_id=1, replica_groups={{0,16,32,48,64,80,96,112},{128,144,160,176,192,208,224,240},{256,272,28..., dimensions={0} | all-to-all | bytes 589824 | tf_op jit(solution)/shard_map/all_to_all | solution.py:244
  84.3 1.9 %shard_map.86 = f32[16,4,128]{2,1,0:T(4,128)S(1)} custom-call(f32[16,128]{1,0:T(8,128)S(1)} %get-tuple-element.208.facts_ref, f32[8,512,1024]{2,1,0:T(8,128)S(1)} %get-tuple-element.209.trade_ref, f32[512,1024]{1,0:T(8,128)S(1)} %get-tuple-element.213.spread_ref, f32[8,1024]{1,0:T(8,128)S(1)} %copy-done, f32[8,8,1152]{2,1,0:T(8,128)S(1)} %all_to_all.131.got_ref), custom_call_target="tpu_custom_call" | custom-call | tf_op jit(solution)/shard_map/pallas_call | solution.py:233
  86.3 15.8 %all_to_all.132.sales_ref = f32[16,4,128]{2,1,0:T(4,128)S(1)} all-to-all(f32[16,4,128]{2,1,0:T(4,128)S(1)} %shard_map.86), channel_id=1, replica_groups=mesh['orig'=32,'dest'=16] {'dest'}, dimensions={0} | all-to-all | bytes 65536 | tf_op jit(solution)/shard_map/all_to_all | solution.py:244
  102.1 1.9 %shard_map.87 = (f32[4,8,1152]{2,1,0:T(8,128)S(1)}, f32[512,1024]{1,0:T(8,128)S(1)}, f32[4,128]{1,0:T(4,128)S(1)}) custom-call(f32[16,128]{1,0:T(8,128)S(1)} %get-tuple-element.208.facts_ref, f32[8,512,1024]{2,1,0:T(8,128)S(1)} %get-tuple-element.209.trade_ref, f32[8,512]{1,0:T(8,128)S(1)} %copy-done.1, f32[4,128]{1,0:T(4,128)S(1)} %bitcast.85, ...), custom_call_target="tpu_custom_call" | custom-call | tf_op jit(solution)/shard_map/pallas_call | solution.py:233
  104.0 8.8 %all_to_all.133.got_ref = f32[4,8,1152]{2,1,0:T(8,128)S(1)} all-to-all(f32[4,8,1152]{2,1,0:T(8,128)S(1)} %get-tuple-element.217), channel_id=1, replica_groups={{0,128,256,384},{16,144,272,400},{32,160,288,416},{48,176,304,432},{64,..., dimensions={0} | all-to-all | bytes 294912 | tf_op jit(solution)/shard_map/all_to_all | solution.py:244
  112.9 12.2 %all_to_all.134.got_ref = f32[8,8,1152]{2,1,0:T(8,128)S(1)} all-to-all(f32[8,8,1152]{2,1,0:T(8,128)S(1)} %shard_map.88), channel_id=1, replica_groups={{0,16,32,48,64,80,96,112},{128,144,160,176,192,208,224,240},{256,272,28..., dimensions={0} | all-to-all | bytes 589824 | tf_op jit(solution)/shard_map/all_to_all | solution.py:244
  125.1 0.0 copy-start.2
  125.1 1.9 %shard_map.89 = (f32[16,4,128]{2,1,0:T(4,128)S(1)}, f32[8,1024]{1,0:T(8,128)S(1)}) custom-call(f32[16,128]{1,0:T(8,128)S(1)} %get-tuple-element.208.facts_ref, f32[8,512,1024]{2,1,0:T(8,128)S(1)} %get-tuple-element.209.trade_ref, f32[512,1024]{1,0:T(8,128)S(1)} %get-tuple-element.216.spread_ref, f32[8,1024]{1,0:T(8,128)S(1)} %copy-done, ...), custom_call_target="tpu_custom_call" | custom-call | tf_op jit(solution)/shard_map/pallas_call | solution.py:233
  127.0 15.8 %all_to_all.135.sales_ref = f32[16,4,128]{2,1,0:T(4,128)S(1)} all-to-all(f32[16,4,128]{2,1,0:T(4,128)S(1)} %get-tuple-element.218), channel_id=1, replica_groups=mesh['orig'=32,'dest'=16] {'dest'}, dimensions={0} | all-to-all | bytes 65536 | tf_op jit(solution)/shard_map/all_to_all | solution.py:244
  142.9 0.7 shard_map.90
  143.5 3.9 %all-to-all-start.25 = ((f32[32,2,128]{2,1,0:T(2,128)}), f32[32,2,128]{2,1,0:T(2,128)S(1)}, u32[]{:S(2)}, u32[]{:S(2)}) async-start(f32[32,2,128]{2,1,0:T(2,128)} %get-tuple-element.221), calls=%async_computation.25 | async-start | bytes 65536 | tf_op jit(solution)/shard_map/all_to_all | solution.py:244
  147.4 9.0 %all-to-all-done.25.got_ref = f32[32,2,128]{2,1,0:T(2,128)S(1)} async-done(((f32[32,2,128]{2,1,0:T(2,128)}), f32[32,2,128]{2,1,0:T(2,128)S(1)}, u32[]{:S(2)}, u32[]{:S(2)}) %all-to-all-start.25) | async-done | bytes 32800 | tf_op jit(solution)/shard_map/all_to_all | solution.py:244
  156.5 0.7 shard_map.91
  157.2 0.0 copy-done.2
  157.3 0.0 copy-done.5
  157.3 0.2 conditional.1
  (4 shorter events, 0.1 us)
Async XLA Ops:
  0.6 35.1 %copy-start = (f32[8,1024]{1,0:T(8,128)S(1)}, f32[8,1024]{1,0:T(8,128)}, u32[]{:S(2)}) copy-start(f32[8,1024]{1,0:T(8,128)} %preference_ref.5) | copy-start | bytes 98308
  35.7 25.9 %copy-start.1 = (f32[8,512]{1,0:T(8,128)S(1)}, f32[8,512]{1,0:T(8,128)}, u32[]{:S(2)}) copy-start(f32[8,512]{1,0:T(8,128)} %productivity_ref.3) | copy-start | bytes 49156
  35.7 25.9 %copy-start.3 = (f32[512]{0:T(512)S(1)}, f32[512]{0:T(512)}, u32[]{:S(2)}) copy-start(f32[512]{0:T(512)} %param.24) | copy-start | bytes 6148
  35.7 25.9 %copy-start.4 = (f32[512]{0:T(512)S(1)}, f32[512]{0:T(512)}, u32[]{:S(2)}) copy-start(f32[512]{0:T(512)} %param.25) | copy-start | bytes 6148
  125.1 32.2 %copy-start.2 = (bf16[512,1024]{1,0:T(8,128)(2,1)S(1)}, bf16[512,1024]{1,0:T(8,128)(2,1)}, u32[]{:S(2)}) copy-start(bf16[512,1024]{1,0:T(8,128)(2,1)} %cost_in_ref.1) | copy-start | bytes 3145732
  125.1 32.2 %copy-start.5 = (f32[8]{0:T(128)S(1)}, f32[8]{0:T(128)}, u32[]{:S(2)}) copy-start(f32[8]{0:T(128)} %slope_ref.1) | copy-start | bytes 100
  143.5 12.9 %all-to-all-start.25 = ((f32[32,2,128]{2,1,0:T(2,128)}), f32[32,2,128]{2,1,0:T(2,128)S(1)}, u32[]{:S(2)}, u32[]{:S(2)}) async-start(f32[32,2,128]{2,1,0:T(2,128)} %get-tuple-element.221), calls=%async_computation.25 | async-start | bytes 65536 | tf_op jit(solution)/shard_map/all_to_all | solution.py:244

commit v7 on v6

--- a/solution.py
+++ b/solution.py
@@ -97,9 +97,9 @@
 
 
 def first_phi_kernel(
-    spot_ref, slope_ref, cost_in_ref, productivity_in_ref, workers_in_ref, wage_in_ref,
+    cost_in_ref, slope_in_ref, productivity_in_ref, workers_in_ref, wage_in_ref,
     send_ref, spread_ref, trade_ref, facts_ref,
-    totals_ref, supply_ref, part_ref, cost_ref, productivity_ref, workers_ref, wage_ref, arrived, brought,
+    totals_ref, supply_ref, part_ref, cost_ref, slope_ref, productivity_ref, workers_ref, wage_ref, arrived, brought,
 ):
     sectors, rows = productivity_ref.shape
     columns = cost_ref.shape[1]
@@ -107,7 +107,7 @@
     small = [
         pltpu.make_async_copy(given, held, brought.at[i])
         for i, (given, held) in enumerate(
-            ((wage_in_ref, wage_ref), (productivity_in_ref, productivity_ref), (workers_in_ref, workers_ref))
+            ((slope_in_ref, slope_ref), (wage_in_ref, wage_ref), (productivity_in_ref, productivity_ref), (workers_in_ref, workers_ref))
         )
     ]
     copies = []
@@ -116,12 +116,12 @@
         copies.append(pltpu.make_async_copy(cost_in_ref.at[some], cost_ref.at[some], arrived.at[i]))
     for copy in small + copies:
         copy.start()
-    part = spot_ref[0] - spot_ref[1] * (columns // rows)
-    facts_ref[:sectors, :] = pick(slope_ref, sectors)
+    part = lax.axis_index("orig") - lax.axis_index("dest") * (columns // rows)
     row = lax.broadcasted_iota(jnp.int32, (sectors, LANES), 0)
     facts_ref[sectors:, :] = jnp.where(row == part, 1.0, 0.0)
     for copy in small:
         copy.wait()
+    facts_ref[:sectors, :] = pick(slope_ref, sectors)
     facts = facts_ref[...]
     prepare(facts[:sectors], facts[sectors:], columns, productivity_ref, workers_ref, wage_ref[...], part_ref, spread_ref, supply_ref)
     slopes = [-slope_ref[j] for j in range(sectors)]
@@ -298,7 +298,6 @@
     outer = across // INNER
     by_inner = [[i * INNER + j for j in range(INNER)] for i in range(outer)]
     by_outer = [[i * INNER + j for i in range(outer)] for j in range(INNER)]
-    spot = jnp.stack([lax.axis_index("orig"), lax.axis_index("dest")]).astype(jnp.int32)
     workers = workers.reshape(pieces, LANES)
     wage = start_wage.reshape(pieces, LANES)
     sales = trade = None
@@ -309,10 +308,11 @@
         scratch = [(sectors, 8, columns), (sectors, rows), (sectors, width)]
         if step == 0:
             send, spread, trade, facts = call(
-                first_phi_kernel, outs + [f32(sectors, rows, columns), f32(2 * sectors, LANES)], [spot, elasticity], [],
-                scratch + [pltpu.VMEM(log_cost.shape, log_cost.dtype), (sectors, rows), (pieces, LANES), (pieces, LANES)]
-                + [pltpu.SemaphoreType.DMA((2,)), pltpu.SemaphoreType.DMA((3,))],
-                [log_cost, productivity, workers, wage],
+                first_phi_kernel, outs + [f32(sectors, rows, columns), f32(2 * sectors, LANES)], [], [],
+                scratch + [pltpu.VMEM(log_cost.shape, log_cost.dtype), pltpu.SMEM((sectors,), jnp.float32)]
+                + [(sectors, rows), (pieces, LANES), (pieces, LANES)]
+                + [pltpu.SemaphoreType.DMA((2,)), pltpu.SemaphoreType.DMA((4,))],
+                [log_cost, elasticity, productivity, workers, wage],
             )
         else:
             send, spread, wage = call(

time: 158 us -> 157 us (level)
  no operation moved by 1% of the time
where the time goes in v7:
time: 157 us
  blocking collectives  127 us (81%)
  Pallas kernels  15.6 us (10%)
  waiting for transfers between devices  9.02 us (6%)
  starting transfers between devices  3.88 us (2%)
    all_to_all x9, blocking collectives, exchange(): return lax.all_to_all(x, axis, 0, 0, tiled=True, axis_index_groups=groups)  127 us
    pallas_call x11, Pallas kernels, call(): pl.pallas_call(body, out_shape=tuple(out_shape), in_specs=[SM] * len(scal...  15.6 us
    all_to_all x1, waiting for transfers between devices, exchange(): return lax.all_to_all(x, axis, 0, 0, tiled=True, axis_index_groups=groups)  9.02 us
    all_to_all x1, starting transfers between devices, exchange(): return lax.all_to_all(x, axis, 0, 0, tiled=True, axis_index_groups=groups)  3.88 us
  transfers between devices with their start and end apart: 1, of which 1 were waited for; matrix products, arithmetic and copies ran while one was open for 0% of the time, Pallas kernels for 0%

profile of v7, /device:TPU:1, one launch (start us, length us, event | category | flops | bytes accessed | tf_op | source)
XLA Modules:
  0.0 156.9 jit_solution(10820684131147755324)
XLA Ops:
  0.6 0.0 copy-start
  0.6 4.5 %shard_map.81 = (f32[4,8,1280]{2,1,0:T(8,128)S(1)}, f32[512,1024]{1,0:T(8,128)S(1)}, f32[8,512,1024]{2,1,0:T(8,128)S(1)}, f32[16,128]{1,0:T(8,128)S(1)}) custom-call(bf16[512,1024]{1,0:T(8,128)(2,1)} %cost_in_ref.1, f32[8]{0:T(128)} %slope_in_ref.1, f32[8,512]{1,0:T(8,128)} %productivity_ref.3, f32[4,128]{1,0:T(4,128)} %bitcast.81, f32[4,128]{1,0:T(4,128)} %bitcast.88), custom_call_target="tpu_custom_call" | custom-call | tf_op jit(solution)/shard_map/pallas_call | solution.py:233
  5.1 13.2 %all_to_all.127.got_ref = f32[4,8,1280]{2,1,0:T(8,128)S(1)} all-to-all(f32[4,8,1280]{2,1,0:T(8,128)S(1)} %get-tuple-element.211), channel_id=1, replica_groups={{0,128,256,384},{16,144,272,400},{32,160,288,416},{48,176,304,432},{64,..., dimensions={0} | all-to-all | bytes 327680 | tf_op jit(solution)/shard_map/all_to_all | solution.py:244
  18.3 16.6 %all_to_all.128.got_ref = f32[8,8,1280]{2,1,0:T(8,128)S(1)} all-to-all(f32[8,8,1280]{2,1,0:T(8,128)S(1)} %shard_map.82), channel_id=1, replica_groups={{0,16,32,48,64,80,96,112},{128,144,160,176,192,208,224,240},{256,272,28..., dimensions={0} | all-to-all | bytes 655360 | tf_op jit(solution)/shard_map/all_to_all | solution.py:244
  35.0 0.0 copy-done
  35.0 0.0 copy-start.1
  35.0 0.0 copy-start.3
  35.0 0.0 copy-start.4
  35.0 2.0 %shard_map.83 = f32[16,4,128]{2,1,0:T(4,128)S(1)} custom-call(f32[16,128]{1,0:T(8,128)S(1)} %get-tuple-element.208.facts_ref, f32[8,512,1024]{2,1,0:T(8,128)S(1)} %get-tuple-element.209.trade_ref, f32[512,1024]{1,0:T(8,128)S(1)} %get-tuple-element.210.spread_ref, f32[8,1024]{1,0:T(8,128)S(1)} %copy-done, f32[8,8,1280]{2,1,0:T(8,128)S(1)} %all_to_all.128.got_ref), custom_call_target="tpu_custom_call" | custom-call | tf_op jit(solution)/shard_map/pallas_call | solution.py:233
  37.0 23.9 %all_to_all.129.sales_ref = f32[16,4,128]{2,1,0:T(4,128)S(1)} all-to-all(f32[16,4,128]{2,1,0:T(4,128)S(1)} %shard_map.83), channel_id=1, replica_groups=mesh['orig'=32,'dest'=16] {'dest'}, dimensions={0} | all-to-all | bytes 65536 | tf_op jit(solution)/shard_map/all_to_all | solution.py:244
  60.8 0.0 copy-done.1
  60.9 0.0 copy-done.3
  60.9 0.0 copy-done.4
  60.9 1.9 %shard_map.84 = (f32[4,8,1152]{2,1,0:T(8,128)S(1)}, f32[512,1024]{1,0:T(8,128)S(1)}, f32[4,128]{1,0:T(4,128)S(1)}) custom-call(f32[16,128]{1,0:T(8,128)S(1)} %get-tuple-element.208.facts_ref, f32[8,512,1024]{2,1,0:T(8,128)S(1)} %get-tuple-element.209.trade_ref, f32[8,512]{1,0:T(8,128)S(1)} %copy-done.1, f32[4,128]{1,0:T(4,128)S(1)} %bitcast.82, ...), custom_call_target="tpu_custom_call" | custom-call | tf_op jit(solution)/shard_map/pallas_call | solution.py:233
  62.8 8.6 %all_to_all.130.got_ref = f32[4,8,1152]{2,1,0:T(8,128)S(1)} all-to-all(f32[4,8,1152]{2,1,0:T(8,128)S(1)} %get-tuple-element.214), channel_id=1, replica_groups={{0,128,256,384},{16,144,272,400},{32,160,288,416},{48,176,304,432},{64,..., dimensions={0} | all-to-all | bytes 294912 | tf_op jit(solution)/shard_map/all_to_all | solution.py:244
  71.4 12.2 %all_to_all.131.got_ref = f32[8,8,1152]{2,1,0:T(8,128)S(1)} all-to-all(f32[8,8,1152]{2,1,0:T(8,128)S(1)} %shard_map.85), channel_id=1, replica_groups={{0,16,32,48,64,80,96,112},{128,144,160,176,192,208,224,240},{256,272,28..., dimensions={0} | all-to-all | bytes 589824 | tf_op jit(solution)/shard_map/all_to_all | solution.py:244
  83.6 1.9 %shard_map.86 = f32[16,4,128]{2,1,0:T(4,128)S(1)} custom-call(f32[16,128]{1,0:T(8,128)S(1)} %get-tuple-element.208.facts_ref, f32[8,512,1024]{2,1,0:T(8,128)S(1)} %get-tuple-element.209.trade_ref, f32[512,1024]{1,0:T(8,128)S(1)} %get-tuple-element.213.spread_ref, f32[8,1024]{1,0:T(8,128)S(1)} %copy-done, f32[8,8,1152]{2,1,0:T(8,128)S(1)} %all_to_all.131.got_ref), custom_call_target="tpu_custom_call" | custom-call | tf_op jit(solution)/shard_map/pallas_call | solution.py:233
  85.5 15.8 %all_to_all.132.sales_ref = f32[16,4,128]{2,1,0:T(4,128)S(1)} all-to-all(f32[16,4,128]{2,1,0:T(4,128)S(1)} %shard_map.86), channel_id=1, replica_groups=mesh['orig'=32,'dest'=16] {'dest'}, dimensions={0} | all-to-all | bytes 65536 | tf_op jit(solution)/shard_map/all_to_all | solution.py:244
  101.4 1.9 %shard_map.87 = (f32[4,8,1152]{2,1,0:T(8,128)S(1)}, f32[512,1024]{1,0:T(8,128)S(1)}, f32[4,128]{1,0:T(4,128)S(1)}) custom-call(f32[16,128]{1,0:T(8,128)S(1)} %get-tuple-element.208.facts_ref, f32[8,512,1024]{2,1,0:T(8,128)S(1)} %get-tuple-element.209.trade_ref, f32[8,512]{1,0:T(8,128)S(1)} %copy-done.1, f32[4,128]{1,0:T(4,128)S(1)} %bitcast.83, ...), custom_call_target="tpu_custom_call" | custom-call | tf_op jit(solution)/shard_map/pallas_call | solution.py:233
  103.3 8.8 %all_to_all.133.got_ref = f32[4,8,1152]{2,1,0:T(8,128)S(1)} all-to-all(f32[4,8,1152]{2,1,0:T(8,128)S(1)} %get-tuple-element.217), channel_id=1, replica_groups={{0,128,256,384},{16,144,272,400},{32,160,288,416},{48,176,304,432},{64,..., dimensions={0} | all-to-all | bytes 294912 | tf_op jit(solution)/shard_map/all_to_all | solution.py:244
  112.1 12.2 %all_to_all.134.got_ref = f32[8,8,1152]{2,1,0:T(8,128)S(1)} all-to-all(f32[8,8,1152]{2,1,0:T(8,128)S(1)} %shard_map.88), channel_id=1, replica_groups={{0,16,32,48,64,80,96,112},{128,144,160,176,192,208,224,240},{256,272,28..., dimensions={0} | all-to-all | bytes 589824 | tf_op jit(solution)/shard_map/all_to_all | solution.py:244
  124.4 0.0 copy-start.2
  124.4 0.0 copy-start.5
  124.4 1.9 %shard_map.89 = (f32[16,4,128]{2,1,0:T(4,128)S(1)}, f32[8,1024]{1,0:T(8,128)S(1)}) custom-call(f32[16,128]{1,0:T(8,128)S(1)} %get-tuple-element.208.facts_ref, f32[8,512,1024]{2,1,0:T(8,128)S(1)} %get-tuple-element.209.trade_ref, f32[512,1024]{1,0:T(8,128)S(1)} %get-tuple-element.216.spread_ref, f32[8,1024]{1,0:T(8,128)S(1)} %copy-done, ...), custom_call_target="tpu_custom_call" | custom-call | tf_op jit(solution)/shard_map/pallas_call | solution.py:233
  126.3 15.8 %all_to_all.135.sales_ref = f32[16,4,128]{2,1,0:T(4,128)S(1)} all-to-all(f32[16,4,128]{2,1,0:T(4,128)S(1)} %get-tuple-element.218), channel_id=1, replica_groups=mesh['orig'=32,'dest'=16] {'dest'}, dimensions={0} | all-to-all | bytes 65536 | tf_op jit(solution)/shard_map/all_to_all | solution.py:244
  142.2 0.7 shard_map.90
  142.8 3.9 %all-to-all-start.25 = ((f32[32,2,128]{2,1,0:T(2,128)}), f32[32,2,128]{2,1,0:T(2,128)S(1)}, u32[]{:S(2)}, u32[]{:S(2)}) async-start(f32[32,2,128]{2,1,0:T(2,128)} %get-tuple-element.221), calls=%async_computation.25 | async-start | bytes 65536 | tf_op jit(solution)/shard_map/all_to_all | solution.py:244
  146.7 9.0 %all-to-all-done.25.got_ref = f32[32,2,128]{2,1,0:T(2,128)S(1)} async-done(((f32[32,2,128]{2,1,0:T(2,128)}), f32[32,2,128]{2,1,0:T(2,128)S(1)}, u32[]{:S(2)}, u32[]{:S(2)}) %all-to-all-start.25) | async-done | bytes 32800 | tf_op jit(solution)/shard_map/all_to_all | solution.py:244
  155.7 0.7 shard_map.91
  156.5 0.0 copy-done.2
  156.5 0.0 copy-done.5
  156.5 0.2 conditional.1
  (3 shorter events, 0.1 us)
Async XLA Ops:
  0.6 34.3 %copy-start = (f32[8,1024]{1,0:T(8,128)S(1)}, f32[8,1024]{1,0:T(8,128)}, u32[]{:S(2)}) copy-start(f32[8,1024]{1,0:T(8,128)} %preference_ref.5) | copy-start | bytes 98308
  35.0 25.9 %copy-start.1 = (f32[8,512]{1,0:T(8,128)S(1)}, f32[8,512]{1,0:T(8,128)}, u32[]{:S(2)}) copy-start(f32[8,512]{1,0:T(8,128)} %productivity_ref.3) | copy-start | bytes 49156
  35.0 25.9 %copy-start.3 = (f32[512]{0:T(512)S(1)}, f32[512]{0:T(512)}, u32[]{:S(2)}) copy-start(f32[512]{0:T(512)} %param.24) | copy-start | bytes 6148
  35.0 25.9 %copy-start.4 = (f32[512]{0:T(512)S(1)}, f32[512]{0:T(512)}, u32[]{:S(2)}) copy-start(f32[512]{0:T(512)} %param.25) | copy-start | bytes 6148
  124.4 32.1 %copy-start.2 = (bf16[512,1024]{1,0:T(8,128)(2,1)S(1)}, bf16[512,1024]{1,0:T(8,128)(2,1)}, u32[]{:S(2)}) copy-start(bf16[512,1024]{1,0:T(8,128)(2,1)} %cost_in_ref.1) | copy-start | bytes 3145732
  124.4 32.2 %copy-start.5 = (f32[8]{0:T(128)S(1)}, f32[8]{0:T(128)}, u32[]{:S(2)}) copy-start(f32[8]{0:T(128)} %slope_in_ref.1) | copy-start | bytes 100
  142.8 12.9 %all-to-all-start.25 = ((f32[32,2,128]{2,1,0:T(2,128)}), f32[32,2,128]{2,1,0:T(2,128)S(1)}, u32[]{:S(2)}, u32[]{:S(2)}) async-start(f32[32,2,128]{2,1,0:T(2,128)} %get-tuple-element.221), calls=%async_computation.25 | async-start | bytes 65536 | tf_op jit(solution)/shard_map/all_to_all | solution.py:244

commit v8 on v7

--- a/solution.py
+++ b/solution.py
@@ -342,7 +342,12 @@
 
 def on_device(*args):
     wage, log_price, world = fast(*args)
-    return lax.cond(jnp.isfinite(world), lambda: (wage, log_price), lambda: careful(*args))
+    done = lax.while_loop(
+        lambda state: ~state[2],
+        lambda state: (*careful(*args), jnp.bool_(True)),
+        (wage, log_price, jnp.isfinite(world)),
+    )
+    return done[:2]
 
 
 def solution(mesh):

time: 157 us -> 157 us (level)
  blocking collectives: 127 us -> 140 us
  waiting for transfers between devices: 9.02 us -> 0 us
  starting transfers between devices: 3.88 us -> 0 us
    all_to_all x9 -> x10, blocking collectives: 127 us -> 140 us  [exchange(): return lax.all_to_all(x, axis, 0, 0, tiled=True, axis_index_groups=groups)]
    all_to_all x1 -> x0, waiting for transfers between devices: 9.02 us -> none  [exchange(): return lax.all_to_all(x, axis, 0, 0, tiled=True, axis_index_groups=groups)]
    all_to_all x1 -> x0, starting transfers between devices: 3.88 us -> none  [exchange(): return lax.all_to_all(x, axis, 0, 0, tiled=True, axis_index_groups=groups)]
  transfers between devices with their start and end apart: 1 -> 0, of which waited for: 1 -> 0; matrix products, arithmetic and copies ran while one was open for 0% -> 0% of each run, Pallas kernels for 0% -> 0%
where the time goes in v8:
time: 157 us; the launch traced here: 156 us
  blocking collectives  140 us (89%)
  Pallas kernels  15 us (10%)
    all_to_all x10, blocking collectives, exchange(): return lax.all_to_all(x, axis, 0, 0, tiled=True, axis_index_groups=groups)  140 us
    pallas_call x11, Pallas kernels, call(): pl.pallas_call(body, out_shape=tuple(out_shape), in_specs=[SM] * len(scal...  15 us

profile of v8, /device:TPU:1, one launch (start us, length us, event | category | flops | bytes accessed | tf_op | source)
XLA Modules:
  0.0 156.1 jit_solution(6428404742807621285)
XLA Ops:
  0.6 0.0 copy-start.1
  0.6 4.5 %shard_map.77 = (f32[4,8,1280]{2,1,0:T(8,128)S(1)}, f32[512,1024]{1,0:T(8,128)S(1)}, f32[8,512,1024]{2,1,0:T(8,128)S(1)}, f32[16,128]{1,0:T(8,128)S(1)}) custom-call(bf16[512,1024]{1,0:T(8,128)(2,1)} %cost_in_ref.1, f32[8]{0:T(128)} %slope_in_ref.1, f32[8,512]{1,0:T(8,128)} %productivity_ref.3, f32[4,128]{1,0:T(4,128)} %bitcast.81, f32[4,128]{1,0:T(4,128)} %bitcast.88), custom_call_target="tpu_custom_call" | custom-call | tf_op jit(solution)/shard_map/pallas_call | solution.py:233
  5.1 13.2 %all_to_all.127.got_ref = f32[4,8,1280]{2,1,0:T(8,128)S(1)} all-to-all(f32[4,8,1280]{2,1,0:T(8,128)S(1)} %get-tuple-element.229), channel_id=1, replica_groups={{0,128,256,384},{16,144,272,400},{32,160,288,416},{48,176,304,432},{64,..., dimensions={0} | all-to-all | bytes 327680 | tf_op jit(solution)/shard_map/all_to_all | solution.py:244
  18.3 16.6 %all_to_all.128.got_ref = f32[8,8,1280]{2,1,0:T(8,128)S(1)} all-to-all(f32[8,8,1280]{2,1,0:T(8,128)S(1)} %shard_map.78), channel_id=1, replica_groups={{0,16,32,48,64,80,96,112},{128,144,160,176,192,208,224,240},{256,272,28..., dimensions={0} | all-to-all | bytes 655360 | tf_op jit(solution)/shard_map/all_to_all | solution.py:244
  35.0 0.0 copy-done.1
  35.0 0.0 copy-start
  35.0 0.0 copy-start.2
  35.0 0.0 copy-start.4
  35.0 2.0 %shard_map.79 = f32[16,4,128]{2,1,0:T(4,128)S(1)} custom-call(f32[16,128]{1,0:T(8,128)S(1)} %get-tuple-element.226.facts_ref, f32[8,512,1024]{2,1,0:T(8,128)S(1)} %get-tuple-element.227.trade_ref, f32[512,1024]{1,0:T(8,128)S(1)} %get-tuple-element.228.spread_ref, f32[8,1024]{1,0:T(8,128)S(1)} %copy-done.1, f32[8,8,1280]{2,1,0:T(8,128)S(1)} %all_to_all.128.got_ref), custom_call_target="tpu_custom_call" | custom-call | tf_op jit(solution)/shard_map/pallas_call | solution.py:233
  37.0 23.9 %all_to_all.129.sales_ref = f32[16,4,128]{2,1,0:T(4,128)S(1)} all-to-all(f32[16,4,128]{2,1,0:T(4,128)S(1)} %shard_map.79), channel_id=1, replica_groups=mesh['orig'=32,'dest'=16] {'dest'}, dimensions={0} | all-to-all | bytes 65536 | tf_op jit(solution)/shard_map/all_to_all | solution.py:244
  60.8 0.0 copy-done
  60.9 0.0 copy-done.2
  60.9 0.0 copy-done.4
  60.9 1.9 %shard_map.80 = (f32[4,8,1152]{2,1,0:T(8,128)S(1)}, f32[512,1024]{1,0:T(8,128)S(1)}, f32[4,128]{1,0:T(4,128)S(1)}) custom-call(f32[16,128]{1,0:T(8,128)S(1)} %get-tuple-element.226.facts_ref, f32[8,512,1024]{2,1,0:T(8,128)S(1)} %get-tuple-element.227.trade_ref, f32[8,512]{1,0:T(8,128)S(1)} %copy-done, f32[4,128]{1,0:T(4,128)S(1)} %bitcast.82, ...), custom_call_target="tpu_custom_call" | custom-call | tf_op jit(solution)/shard_map/pallas_call | solution.py:233
  62.8 8.6 %all_to_all.130.got_ref = f32[4,8,1152]{2,1,0:T(8,128)S(1)} all-to-all(f32[4,8,1152]{2,1,0:T(8,128)S(1)} %get-tuple-element.232), channel_id=1, replica_groups={{0,128,256,384},{16,144,272,400},{32,160,288,416},{48,176,304,432},{64,..., dimensions={0} | all-to-all | bytes 294912 | tf_op jit(solution)/shard_map/all_to_all | solution.py:244
  71.4 12.2 %all_to_all.131.got_ref = f32[8,8,1152]{2,1,0:T(8,128)S(1)} all-to-all(f32[8,8,1152]{2,1,0:T(8,128)S(1)} %shard_map.81), channel_id=1, replica_groups={{0,16,32,48,64,80,96,112},{128,144,160,176,192,208,224,240},{256,272,28..., dimensions={0} | all-to-all | bytes 589824 | tf_op jit(solution)/shard_map/all_to_all | solution.py:244
  83.6 1.9 %shard_map.82 = f32[16,4,128]{2,1,0:T(4,128)S(1)} custom-call(f32[16,128]{1,0:T(8,128)S(1)} %get-tuple-element.226.facts_ref, f32[8,512,1024]{2,1,0:T(8,128)S(1)} %get-tuple-element.227.trade_ref, f32[512,1024]{1,0:T(8,128)S(1)} %get-tuple-element.231.spread_ref, f32[8,1024]{1,0:T(8,128)S(1)} %copy-done.1, f32[8,8,1152]{2,1,0:T(8,128)S(1)} %all_to_all.131.got_ref), custom_call_target="tpu_custom_call" | custom-call | tf_op jit(solution)/shard_map/pallas_call | solution.py:233
  85.5 15.8 %all_to_all.132.sales_ref = f32[16,4,128]{2,1,0:T(4,128)S(1)} all-to-all(f32[16,4,128]{2,1,0:T(4,128)S(1)} %shard_map.82), channel_id=1, replica_groups=mesh['orig'=32,'dest'=16] {'dest'}, dimensions={0} | all-to-all | bytes 65536 | tf_op jit(solution)/shard_map/all_to_all | solution.py:244
  101.4 1.9 %shard_map.83 = (f32[4,8,1152]{2,1,0:T(8,128)S(1)}, f32[512,1024]{1,0:T(8,128)S(1)}, f32[4,128]{1,0:T(4,128)S(1)}) custom-call(f32[16,128]{1,0:T(8,128)S(1)} %get-tuple-element.226.facts_ref, f32[8,512,1024]{2,1,0:T(8,128)S(1)} %get-tuple-element.227.trade_ref, f32[8,512]{1,0:T(8,128)S(1)} %copy-done, f32[4,128]{1,0:T(4,128)S(1)} %bitcast.83, ...), custom_call_target="tpu_custom_call" | custom-call | tf_op jit(solution)/shard_map/pallas_call | solution.py:233
  103.3 8.8 %all_to_all.133.got_ref = f32[4,8,1152]{2,1,0:T(8,128)S(1)} all-to-all(f32[4,8,1152]{2,1,0:T(8,128)S(1)} %get-tuple-element.235), channel_id=1, replica_groups={{0,128,256,384},{16,144,272,400},{32,160,288,416},{48,176,304,432},{64,..., dimensions={0} | all-to-all | bytes 294912 | tf_op jit(solution)/shard_map/all_to_all | solution.py:244
  112.1 12.2 %all_to_all.134.got_ref = f32[8,8,1152]{2,1,0:T(8,128)S(1)} all-to-all(f32[8,8,1152]{2,1,0:T(8,128)S(1)} %shard_map.84), channel_id=1, replica_groups={{0,16,32,48,64,80,96,112},{128,144,160,176,192,208,224,240},{256,272,28..., dimensions={0} | all-to-all | bytes 589824 | tf_op jit(solution)/shard_map/all_to_all | solution.py:244
  124.4 0.0 copy-start.3
  124.4 0.0 copy-start.5
  124.4 1.9 %shard_map.85 = (f32[16,4,128]{2,1,0:T(4,128)S(1)}, f32[8,1024]{1,0:T(8,128)S(1)}) custom-call(f32[16,128]{1,0:T(8,128)S(1)} %get-tuple-element.226.facts_ref, f32[8,512,1024]{2,1,0:T(8,128)S(1)} %get-tuple-element.227.trade_ref, f32[512,1024]{1,0:T(8,128)S(1)} %get-tuple-element.234.spread_ref, f32[8,1024]{1,0:T(8,128)S(1)} %copy-done.1, ...), custom_call_target="tpu_custom_call" | custom-call | tf_op jit(solution)/shard_map/pallas_call | solution.py:233
  126.3 15.8 %all_to_all.135.sales_ref = f32[16,4,128]{2,1,0:T(4,128)S(1)} all-to-all(f32[16,4,128]{2,1,0:T(4,128)S(1)} %get-tuple-element.236), channel_id=1, replica_groups=mesh['orig'=32,'dest'=16] {'dest'}, dimensions={0} | all-to-all | bytes 65536 | tf_op jit(solution)/shard_map/all_to_all | solution.py:244
  142.2 12.7 %all_to_all.136.got_ref = f32[32,2,128]{2,1,0:T(2,128)S(1)} all-to-all(f32[32,2,128]{2,1,0:T(2,128)S(1)} %get-tuple-element.239), channel_id=1, replica_groups=mesh['orig'=32,'dest'=16] {'orig'}, dimensions={0} | all-to-all | bytes 65536 | tf_op jit(solution)/shard_map/all_to_all | solution.py:244
  154.9 0.7 shard_map.87
  155.7 0.0 copy-done.3
  155.7 0.0 copy-done.5
  155.7 0.2 while.65
  (4 shorter events, 0.1 us)
Async XLA Ops:
  0.6 34.3 %copy-start.1 = (f32[8,1024]{1,0:T(8,128)S(1)}, f32[8,1024]{1,0:T(8,128)}, u32[]{:S(2)}) copy-start(f32[8,1024]{1,0:T(8,128)} %preference_ref.5) | copy-start | bytes 98308
  35.0 25.9 %copy-start = (f32[8,512]{1,0:T(8,128)S(1)}, f32[8,512]{1,0:T(8,128)}, u32[]{:S(2)}) copy-start(f32[8,512]{1,0:T(8,128)} %productivity_ref.3) | copy-start | bytes 49156
  35.0 25.9 %copy-start.2 = (f32[512]{0:T(512)S(1)}, f32[512]{0:T(512)}, u32[]{:S(2)}) copy-start(f32[512]{0:T(512)} %param.24) | copy-start | bytes 6148
  35.0 25.9 %copy-start.4 = (f32[512]{0:T(512)S(1)}, f32[512]{0:T(512)}, u32[]{:S(2)}) copy-start(f32[512]{0:T(512)} %param.25) | copy-start | bytes 6148
  124.4 31.3 %copy-start.3 = (bf16[512,1024]{1,0:T(8,128)(2,1)S(1)}, bf16[512,1024]{1,0:T(8,128)(2,1)}, u32[]{:S(2)}) copy-start(bf16[512,1024]{1,0:T(8,128)(2,1)} %cost_in_ref.1) | copy-start | bytes 3145732
  124.4 31.3 %copy-start.5 = (f32[8]{0:T(128)S(1)}, f32[8]{0:T(128)}, u32[]{:S(2)}) copy-start(f32[8]{0:T(128)} %slope_in_ref.1) | copy-start | bytes 100

commit v9 on v8

--- a/solution.py
+++ b/solution.py
@@ -5,6 +5,7 @@
 from jax import lax
 from jax.experimental import pallas as pl
 from jax.experimental.pallas import tpu as pltpu
+from jax.sharding import Mesh
 from jax.sharding import PartitionSpec as P
 
 ITERS = 3
@@ -12,6 +13,7 @@
 CENTRE = 1024.0
 GAIN = 2.0
 INNER = 8
+ORIG = ("far", "near")
 SMALLEST, LARGEST = 1e-32, 1e30
 
 
@@ -116,7 +118,7 @@
         copies.append(pltpu.make_async_copy(cost_in_ref.at[some], cost_ref.at[some], arrived.at[i]))
     for copy in small + copies:
         copy.start()
-    part = lax.axis_index("orig") - lax.axis_index("dest") * (columns // rows)
+    part = lax.axis_index("far") * INNER + lax.axis_index("near") - lax.axis_index("dest") * (columns // rows)
     row = lax.broadcasted_iota(jnp.int32, (sectors, LANES), 0)
     facts_ref[sectors:, :] = jnp.where(row == part, 1.0, 0.0)
     for copy in small:
@@ -164,10 +166,13 @@
     send_phi(totals_ref, part_ref, send_ref)
 
 
-def sum_kernel(got_ref, send_ref):
-    total = jnp.sum(got_ref[...], axis=0)
+def sum_kernel(got_ref, send_ref, *rest):
+    width = send_ref.shape[2]
+    total = jnp.sum(got_ref[:, :, :width], axis=0)
     for copy in range(send_ref.shape[0]):
         send_ref[copy] = total
+    for incomes_ref in rest:
+        incomes_ref[...] = got_ref[:, :incomes_ref.shape[1], width:]
 
 
 def sales_kernel(last, cells, facts_ref, trade_ref, spread_ref, preference_ref, got_ref, send_ref, *rest):
@@ -209,13 +214,23 @@
         send_ref[:, p, :] = jnp.broadcast_to(piece, (send_ref.shape[0], LANES))
 
 
-def settle_kernel(workers_ref, wage_ref, sales_ref, raw_ref, send_ref):
-    raw = next_wage(wage_ref, workers_ref, sales_ref)
-    raw_ref[...] = raw
-    copies = send_ref.shape[0]
-    for row, wage in enumerate((raw, wage_ref[...])):
-        world = jnp.sum(wage * workers_ref[...], axis=0, keepdims=True)
-        send_ref[:, row, :] = jnp.broadcast_to(world, (copies, LANES))
+def settle_kernel(incomes_ref, wage_ref, sales_ref, raw_ref, send_ref):
+    far = incomes_ref.shape[0]
+    along = sales_ref.shape[0] // far
+    mine = lax.axis_index("far")
+    world = jnp.zeros((1, LANES), jnp.float32)
+    for i in range(far):
+        income = incomes_ref[i]
+        grown = jnp.sqrt(jnp.sum(sales_ref[i * along:(i + 1) * along], axis=0) / income)
+        world += jnp.sum(income * grown, axis=0, keepdims=True)
+
+        @pl.when(mine == i)
+        def _():
+            raw_ref[...] = wage_ref[...] * grown
+
+    before = jnp.sum(jnp.sum(incomes_ref[...], axis=0), axis=0, keepdims=True)
+    for row, sums in enumerate((world, before)):
+        send_ref[:, row, :] = jnp.broadcast_to(sums, (send_ref.shape[0], LANES))
 
 
 def finish_kernel(cells, raw_ref, price_ref, got_ref, wage_ref, log_price_ref, world_ref):
@@ -240,8 +255,8 @@
     )(*scalars, *arrays, *in_place)
 
 
-def exchange(x, axis, groups=None):
-    return lax.all_to_all(x, axis, 0, 0, tiled=True, axis_index_groups=groups)
+def exchange(x, axis):
+    return lax.all_to_all(x, axis, 0, 0, tiled=True)
 
 
 def gather(x, axis):
@@ -251,16 +266,16 @@
 def careful(log_cost, elasticity, productivity, preference, workers, start_wage):
     rows, columns = log_cost.shape
     sectors = elasticity.shape[0]
-    across = lax.axis_size("orig")
+    across = lax.axis_size(ORIG)
     cells, width = rows * across, columns // across
     spend_share = preference / jnp.sum(preference, axis=0, keepdims=True)
 
     def settle(raw_wage, wanted):
-        world_income = jnp.sum(gather(jnp.sum(raw_wage * workers, keepdims=True), "orig"))
+        world_income = jnp.sum(gather(jnp.sum(raw_wage * workers, keepdims=True), ORIG))
         wage = raw_wage * (cells / world_income)
         if not wanted:
             return wage, None
-        incomes = gather(wage * workers, "orig").reshape(cells)
+        incomes = gather(wage * workers, ORIG).reshape(cells)
         return wage, lax.dynamic_slice_in_dim(incomes, lax.axis_index("dest") * columns, columns)
 
     def kernel_of(slope):
@@ -273,14 +288,14 @@
         return jnp.dot(kernel_of(pair[0]), pair[1], precision=lax.Precision.HIGHEST)
 
     def whole(x):
-        return jnp.moveaxis(gather(x, "orig"), 0, 1).reshape(sectors, columns)
+        return jnp.moveaxis(gather(x, ORIG), 0, 1).reshape(sectors, columns)
 
     wage, dest_income = settle(start_wage, True)
     for step in range(ITERS):
         supply = productivity * jnp.exp(-elasticity[:, None] * jnp.log(wage)[None, :])
         spending = spend_share * dest_income[None, :]
         partial_phi = lax.map(phi_term, (elasticity, supply)).reshape(sectors, across, width)
-        phi = whole(jnp.sum(exchange(jnp.moveaxis(partial_phi, 1, 0), "orig"), axis=0))
+        phi = whole(jnp.sum(exchange(jnp.moveaxis(partial_phi, 1, 0), ORIG), axis=0))
         log_price = -jnp.log(phi) / elasticity[:, None]
         partial_sales = lax.map(sales_term, (elasticity, spending / phi))
         revenue = jnp.sum(gather(jnp.sum(supply * partial_sales, axis=0), "dest"), axis=0)
@@ -292,18 +307,16 @@
 def fast(log_cost, elasticity, productivity, preference, workers, start_wage):
     sectors, rows = productivity.shape
     columns = log_cost.shape[1]
-    across, along = lax.axis_size("orig"), lax.axis_size("dest")
-    cells = float(rows * across)
+    outer, along = lax.axis_size("far"), lax.axis_size("dest")
+    cells = float(rows * outer * INNER)
     pieces = rows // LANES
-    outer = across // INNER
-    by_inner = [[i * INNER + j for j in range(INNER)] for i in range(outer)]
-    by_outer = [[i * INNER + j for i in range(outer)] for j in range(INNER)]
     workers = workers.reshape(pieces, LANES)
     wage = start_wage.reshape(pieces, LANES)
     sales = trade = None
     for step in range(ITERS):
         last = step + 1 == ITERS
-        width = columns + (2 if step == 0 else 1) * LANES
+        width = columns + (1 if step == 1 else 2) * LANES
+        summed = columns + (2 if step == 0 else 1) * LANES
         outs = [f32(outer, sectors, width), f32(rows, sectors * LANES)]
         scratch = [(sectors, 8, columns), (sectors, rows), (sectors, width)]
         if step == 0:
@@ -320,19 +333,21 @@
                 outs + [f32(pieces, LANES)], [],
                 [facts, trade, productivity, workers, wage, sales], scratch,
             )
-        got = exchange(send, "orig", by_outer)
-        send, = call(sum_kernel, [f32(INNER, sectors, width)], [], [got])
-        got = exchange(send, "orig", by_inner)
+        got = exchange(send, "far")
+        send, *incomes = call(
+            sum_kernel, [f32(INNER, sectors, summed)] + ([f32(outer, pieces, LANES)] if last else []), [], [got]
+        )
+        got = exchange(send, "near")
         made = call(
             functools.partial(sales_kernel, last, cells),
-            [f32(along, pieces, LANES)] + ([f32(sectors, columns)] if last else []),
+            [f32(outer * along if last else along, pieces, LANES)] + ([f32(sectors, columns)] if last else []),
             [],
             [facts, trade, spread, preference, got],
-            [(rows, LANES), (sectors, columns), (sectors, width)],
+            [(rows, LANES), (sectors, columns), (sectors, summed)],
         )
-        sales = exchange(made[0], "dest")
-    raw, send = call(settle_kernel, [f32(pieces, LANES), f32(across, 2, LANES)], [], [workers, wage, sales])
-    got = exchange(send, "orig")
+        sales = exchange(made[0], ("far", "dest") if last else "dest")
+    raw, send = call(settle_kernel, [f32(pieces, LANES), f32(INNER, 2, LANES)], [], [*incomes, wage, sales])
+    got = exchange(send, "near")
     wage, log_price, world = call(
         functools.partial(finish_kernel, cells),
         [f32(pieces, LANES), f32(sectors, columns), f32(1, LANES)], [], [raw, made[1], got],
@@ -351,10 +366,12 @@
 
 
 def solution(mesh):
+    across, along = mesh.devices.shape
+    split = Mesh(mesh.devices.reshape(across // INNER, INNER, along), (*ORIG, "dest"))
     return jax.shard_map(
         on_device,
-        mesh=mesh,
-        in_specs=(P("orig", "dest"), P(), P(None, "orig"), P(None, "dest"), P("orig"), P("orig")),
-        out_specs=(P("orig"), P(None, "dest")),
+        mesh=split,
+        in_specs=(P(ORIG, "dest"), P(), P(None, ORIG), P(None, "dest"), P(ORIG), P(ORIG)),
+        out_specs=(P(ORIG), P(None, "dest")),
         check_vma=False,
     )

time: 157 us -> 156 us (level)
  no operation moved by 1% of the time
where the time goes in v9:
time: 156 us
  blocking collectives  140 us (90%)
  Pallas kernels  14.9 us (10%)
    all_to_all x10, blocking collectives, exchange(): return lax.all_to_all(x, axis, 0, 0, tiled=True)  140 us
    pallas_call x11, Pallas kernels, call(): pl.pallas_call(body, out_shape=tuple(out_shape), in_specs=[SM] * len(scal...  14.9 us

profile of v9, /device:TPU:1, one launch (start us, length us, event | category | flops | bytes accessed | tf_op | source)
XLA Modules:
  0.0 155.6 jit_solution(6010263073392960163)
XLA Ops:
  0.6 0.0 copy-start.1
  0.6 4.5 %shard_map.77 = (f32[4,8,1280]{2,1,0:T(8,128)S(1)}, f32[512,1024]{1,0:T(8,128)S(1)}, f32[8,512,1024]{2,1,0:T(8,128)S(1)}, f32[16,128]{1,0:T(8,128)S(1)}) custom-call(bf16[512,1024]{1,0:T(8,128)(2,1)} %cost_in_ref.1, f32[8]{0:T(128)} %slope_in_ref.1, f32[8,512]{1,0:T(8,128)} %productivity_ref.3, f32[4,128]{1,0:T(4,128)} %bitcast.81, f32[4,128]{1,0:T(4,128)} %bitcast.87), custom_call_target="tpu_custom_call" | custom-call | tf_op jit(solution)/shard_map/pallas_call | solution.py:248
  5.1 13.2 %all_to_all.127.got_ref = f32[4,8,1280]{2,1,0:T(8,128)S(1)} all-to-all(f32[4,8,1280]{2,1,0:T(8,128)S(1)} %get-tuple-element.231), channel_id=1, replica_groups=mesh['far'=4,'near'=8,'dest'=16] {'far'}, dimensions={0} | all-to-all | bytes 327680 | tf_op jit(solution)/shard_map/all_to_all | solution.py:259
  18.3 16.6 %all_to_all.128.got_ref = f32[8,8,1280]{2,1,0:T(8,128)S(1)} all-to-all(f32[8,8,1280]{2,1,0:T(8,128)S(1)} %shard_map.78), channel_id=1, replica_groups=mesh['far'=4,'near'=8,'dest'=16] {'near'}, dimensions={0} | all-to-all | bytes 655360 | tf_op jit(solution)/shard_map/all_to_all | solution.py:259
  35.0 0.0 copy-done.1
  35.0 0.0 copy-start
  35.0 0.0 copy-start.2
  35.0 0.0 copy-start.4
  35.0 2.0 %shard_map.79 = f32[16,4,128]{2,1,0:T(4,128)S(1)} custom-call(f32[16,128]{1,0:T(8,128)S(1)} %get-tuple-element.228.facts_ref, f32[8,512,1024]{2,1,0:T(8,128)S(1)} %get-tuple-element.229.trade_ref, f32[512,1024]{1,0:T(8,128)S(1)} %get-tuple-element.230.spread_ref, f32[8,1024]{1,0:T(8,128)S(1)} %copy-done.1, f32[8,8,1280]{2,1,0:T(8,128)S(1)} %all_to_all.128.got_ref), custom_call_target="tpu_custom_call" | custom-call | tf_op jit(solution)/shard_map/pallas_call | solution.py:248
  37.0 23.9 %all_to_all.129.sales_ref = f32[16,4,128]{2,1,0:T(4,128)S(1)} all-to-all(f32[16,4,128]{2,1,0:T(4,128)S(1)} %shard_map.79), channel_id=1, replica_groups=mesh['far'=4,'near'=8,'dest'=16] {'dest'}, dimensions={0} | all-to-all | bytes 65536 | tf_op jit(solution)/shard_map/all_to_all | solution.py:259
  60.8 0.0 copy-done
  60.9 0.0 copy-done.2
  60.9 0.0 copy-done.4
  60.9 1.9 %shard_map.80 = (f32[4,8,1152]{2,1,0:T(8,128)S(1)}, f32[512,1024]{1,0:T(8,128)S(1)}, f32[4,128]{1,0:T(4,128)S(1)}) custom-call(f32[16,128]{1,0:T(8,128)S(1)} %get-tuple-element.228.facts_ref, f32[8,512,1024]{2,1,0:T(8,128)S(1)} %get-tuple-element.229.trade_ref, f32[8,512]{1,0:T(8,128)S(1)} %copy-done, f32[4,128]{1,0:T(4,128)S(1)} %bitcast.82, ...), custom_call_target="tpu_custom_call" | custom-call | tf_op jit(solution)/shard_map/pallas_call | solution.py:248
  62.8 8.6 %all_to_all.130.got_ref = f32[4,8,1152]{2,1,0:T(8,128)S(1)} all-to-all(f32[4,8,1152]{2,1,0:T(8,128)S(1)} %get-tuple-element.234), channel_id=1, replica_groups=mesh['far'=4,'near'=8,'dest'=16] {'far'}, dimensions={0} | all-to-all | bytes 294912 | tf_op jit(solution)/shard_map/all_to_all | solution.py:259
  71.4 12.2 %all_to_all.131.got_ref = f32[8,8,1152]{2,1,0:T(8,128)S(1)} all-to-all(f32[8,8,1152]{2,1,0:T(8,128)S(1)} %shard_map.81), channel_id=1, replica_groups=mesh['far'=4,'near'=8,'dest'=16] {'near'}, dimensions={0} | all-to-all | bytes 589824 | tf_op jit(solution)/shard_map/all_to_all | solution.py:259
  83.6 1.9 %shard_map.82 = f32[16,4,128]{2,1,0:T(4,128)S(1)} custom-call(f32[16,128]{1,0:T(8,128)S(1)} %get-tuple-element.228.facts_ref, f32[8,512,1024]{2,1,0:T(8,128)S(1)} %get-tuple-element.229.trade_ref, f32[512,1024]{1,0:T(8,128)S(1)} %get-tuple-element.233.spread_ref, f32[8,1024]{1,0:T(8,128)S(1)} %copy-done.1, f32[8,8,1152]{2,1,0:T(8,128)S(1)} %all_to_all.131.got_ref), custom_call_target="tpu_custom_call" | custom-call | tf_op jit(solution)/shard_map/pallas_call | solution.py:248
  85.5 15.8 %all_to_all.132.sales_ref = f32[16,4,128]{2,1,0:T(4,128)S(1)} all-to-all(f32[16,4,128]{2,1,0:T(4,128)S(1)} %shard_map.82), channel_id=1, replica_groups=mesh['far'=4,'near'=8,'dest'=16] {'dest'}, dimensions={0} | all-to-all | bytes 65536 | tf_op jit(solution)/shard_map/all_to_all | solution.py:259
  101.4 1.8 %shard_map.83 = (f32[4,8,1280]{2,1,0:T(8,128)S(1)}, f32[512,1024]{1,0:T(8,128)S(1)}, f32[4,128]{1,0:T(4,128)S(1)}) custom-call(f32[16,128]{1,0:T(8,128)S(1)} %get-tuple-element.228.facts_ref, f32[8,512,1024]{2,1,0:T(8,128)S(1)} %get-tuple-element.229.trade_ref, f32[8,512]{1,0:T(8,128)S(1)} %copy-done, f32[4,128]{1,0:T(4,128)S(1)} %bitcast.83, ...), custom_call_target="tpu_custom_call" | custom-call | tf_op jit(solution)/shard_map/pallas_call | solution.py:248
  103.2 8.8 %all_to_all.133.got_ref = f32[4,8,1280]{2,1,0:T(8,128)S(1)} all-to-all(f32[4,8,1280]{2,1,0:T(8,128)S(1)} %get-tuple-element.235), channel_id=1, replica_groups=mesh['far'=4,'near'=8,'dest'=16] {'far'}, dimensions={0} | all-to-all | bytes 327680 | tf_op jit(solution)/shard_map/all_to_all | solution.py:259
  112.1 11.7 %all_to_all.134.got_ref = f32[8,8,1152]{2,1,0:T(8,128)S(1)} all-to-all(f32[8,8,1152]{2,1,0:T(8,128)S(1)} %get-tuple-element.239), channel_id=1, replica_groups=mesh['far'=4,'near'=8,'dest'=16] {'near'}, dimensions={0} | all-to-all | bytes 589824 | tf_op jit(solution)/shard_map/all_to_all | solution.py:259
  123.8 0.0 copy-start.3
  123.8 0.0 copy-start.5
  123.8 1.9 %shard_map.85 = (f32[64,4,128]{2,1,0:T(4,128)S(1)}, f32[8,1024]{1,0:T(8,128)S(1)}) custom-call(f32[16,128]{1,0:T(8,128)S(1)} %get-tuple-element.228.facts_ref, f32[8,512,1024]{2,1,0:T(8,128)S(1)} %get-tuple-element.229.trade_ref, f32[512,1024]{1,0:T(8,128)S(1)} %get-tuple-element.238.spread_ref, f32[8,1024]{1,0:T(8,128)S(1)} %copy-done.1, ...), custom_call_target="tpu_custom_call" | custom-call | tf_op jit(solution)/shard_map/pallas_call | solution.py:248
  125.7 19.7 %all_to_all.135.sales_ref = f32[64,4,128]{2,1,0:T(4,128)S(1)} all-to-all(f32[64,4,128]{2,1,0:T(4,128)S(1)} %get-tuple-element.240), channel_id=1, replica_groups=mesh['far'=4,'near'=8,'dest'=16] {'far','dest'}, dimensions={0} | all-to-all | bytes 262144 | tf_op jit(solution)/shard_map/all_to_all | solution.py:259
  145.4 0.1 shard_map.86
  145.5 8.9 %all_to_all.136.got_ref = f32[8,2,128]{2,1,0:T(2,128)S(1)} all-to-all(f32[8,2,128]{2,1,0:T(2,128)S(1)} %get-tuple-element.243), channel_id=1, replica_groups=mesh['far'=4,'near'=8,'dest'=16] {'near'}, dimensions={0} | all-to-all | bytes 16384 | tf_op jit(solution)/shard_map/all_to_all | solution.py:259
  154.4 0.7 shard_map.87
  155.2 0.0 copy-done.3
  155.2 0.0 copy-done.5
  155.2 0.2 while.65
  (3 shorter events, 0.1 us)
Async XLA Ops:
  0.6 34.3 %copy-start.1 = (f32[8,1024]{1,0:T(8,128)S(1)}, f32[8,1024]{1,0:T(8,128)}, u32[]{:S(2)}) copy-start(f32[8,1024]{1,0:T(8,128)} %preference_ref.5) | copy-start | bytes 98308
  35.0 25.9 %copy-start = (f32[8,512]{1,0:T(8,128)S(1)}, f32[8,512]{1,0:T(8,128)}, u32[]{:S(2)}) copy-start(f32[8,512]{1,0:T(8,128)} %productivity_ref.3) | copy-start | bytes 49156
  35.0 25.9 %copy-start.2 = (f32[512]{0:T(512)S(1)}, f32[512]{0:T(512)}, u32[]{:S(2)}) copy-start(f32[512]{0:T(512)} %param.24) | copy-start | bytes 6148
  35.0 25.9 %copy-start.4 = (f32[512]{0:T(512)S(1)}, f32[512]{0:T(512)}, u32[]{:S(2)}) copy-start(f32[512]{0:T(512)} %param.25) | copy-start | bytes 6148
  123.8 31.4 %copy-start.3 = (bf16[512,1024]{1,0:T(8,128)(2,1)S(1)}, bf16[512,1024]{1,0:T(8,128)(2,1)}, u32[]{:S(2)}) copy-start(bf16[512,1024]{1,0:T(8,128)(2,1)} %cost_in_ref.1) | copy-start | bytes 3145732
  123.8 31.4 %copy-start.5 = (f32[8]{0:T(128)S(1)}, f32[8]{0:T(128)}, u32[]{:S(2)}) copy-start(f32[8]{0:T(128)} %slope_in_ref.1) | copy-start | bytes 100

commit v10 on v8

--- a/solution.py
+++ b/solution.py
@@ -5,6 +5,7 @@
 from jax import lax
 from jax.experimental import pallas as pl
 from jax.experimental.pallas import tpu as pltpu
+from jax.sharding import Mesh
 from jax.sharding import PartitionSpec as P
 
 ITERS = 3
@@ -12,6 +13,7 @@
 CENTRE = 1024.0
 GAIN = 2.0
 INNER = 8
+ORIG = ("far", "near")
 SMALLEST, LARGEST = 1e-32, 1e30
 
 
@@ -116,7 +118,7 @@
         copies.append(pltpu.make_async_copy(cost_in_ref.at[some], cost_ref.at[some], arrived.at[i]))
     for copy in small + copies:
         copy.start()
-    part = lax.axis_index("orig") - lax.axis_index("dest") * (columns // rows)
+    part = lax.axis_index("far") * INNER + lax.axis_index("near") - lax.axis_index("dest") * (columns // rows)
     row = lax.broadcasted_iota(jnp.int32, (sectors, LANES), 0)
     facts_ref[sectors:, :] = jnp.where(row == part, 1.0, 0.0)
     for copy in small:
@@ -158,7 +160,7 @@
             return tuple(totals[k] + trade_ref[j, at, k * LANES:(k + 1) * LANES] * weight for k in range(blocks))
 
         zero = jnp.zeros((8, LANES), jnp.float32)
-        totals = lax.fori_loop(0, rows // 8, step, (zero,) * blocks, unroll=16)
+        totals = lax.fori_loop(0, rows // 8, step, (zero,) * blocks, unroll=64)
         for k in range(blocks):
             totals_ref[j, :, k * LANES:(k + 1) * LANES] = totals[k]
     send_phi(totals_ref, part_ref, send_ref)
@@ -203,7 +205,7 @@
             total_ref[at, :] = total if j == 0 else total_ref[at, :] + total
             return carry
 
-        lax.fori_loop(0, rows // 8, step, 0, unroll=8)
+        lax.fori_loop(0, rows // 8, step, 0, unroll=32)
     for p in range(rows // LANES):
         piece = jnp.sum(jnp.transpose(total_ref[p * LANES:(p + 1) * LANES, :]), axis=0, keepdims=True)
         send_ref[:, p, :] = jnp.broadcast_to(piece, (send_ref.shape[0], LANES))
@@ -212,10 +214,9 @@
 def settle_kernel(workers_ref, wage_ref, sales_ref, raw_ref, send_ref):
     raw = next_wage(wage_ref, workers_ref, sales_ref)
     raw_ref[...] = raw
-    copies = send_ref.shape[0]
     for row, wage in enumerate((raw, wage_ref[...])):
         world = jnp.sum(wage * workers_ref[...], axis=0, keepdims=True)
-        send_ref[:, row, :] = jnp.broadcast_to(world, (copies, LANES))
+        send_ref[:, row, :] = jnp.broadcast_to(world, (send_ref.shape[0], LANES))
 
 
 def finish_kernel(cells, raw_ref, price_ref, got_ref, wage_ref, log_price_ref, world_ref):
@@ -240,8 +241,8 @@
     )(*scalars, *arrays, *in_place)
 
 
-def exchange(x, axis, groups=None):
-    return lax.all_to_all(x, axis, 0, 0, tiled=True, axis_index_groups=groups)
+def exchange(x, axis):
+    return lax.all_to_all(x, axis, 0, 0, tiled=True)
 
 
 def gather(x, axis):
@@ -251,16 +252,16 @@
 def careful(log_cost, elasticity, productivity, preference, workers, start_wage):
     rows, columns = log_cost.shape
     sectors = elasticity.shape[0]
-    across = lax.axis_size("orig")
+    across = lax.axis_size(ORIG)
     cells, width = rows * across, columns // across
     spend_share = preference / jnp.sum(preference, axis=0, keepdims=True)
 
     def settle(raw_wage, wanted):
-        world_income = jnp.sum(gather(jnp.sum(raw_wage * workers, keepdims=True), "orig"))
+        world_income = jnp.sum(gather(jnp.sum(raw_wage * workers, keepdims=True), ORIG))
         wage = raw_wage * (cells / world_income)
         if not wanted:
             return wage, None
-        incomes = gather(wage * workers, "orig").reshape(cells)
+        incomes = gather(wage * workers, ORIG).reshape(cells)
         return wage, lax.dynamic_slice_in_dim(incomes, lax.axis_index("dest") * columns, columns)
 
     def kernel_of(slope):
@@ -273,14 +274,14 @@
         return jnp.dot(kernel_of(pair[0]), pair[1], precision=lax.Precision.HIGHEST)
 
     def whole(x):
-        return jnp.moveaxis(gather(x, "orig"), 0, 1).reshape(sectors, columns)
+        return jnp.moveaxis(gather(x, ORIG), 0, 1).reshape(sectors, columns)
 
     wage, dest_income = settle(start_wage, True)
     for step in range(ITERS):
         supply = productivity * jnp.exp(-elasticity[:, None] * jnp.log(wage)[None, :])
         spending = spend_share * dest_income[None, :]
         partial_phi = lax.map(phi_term, (elasticity, supply)).reshape(sectors, across, width)
-        phi = whole(jnp.sum(exchange(jnp.moveaxis(partial_phi, 1, 0), "orig"), axis=0))
+        phi = whole(jnp.sum(exchange(jnp.moveaxis(partial_phi, 1, 0), ORIG), axis=0))
         log_price = -jnp.log(phi) / elasticity[:, None]
         partial_sales = lax.map(sales_term, (elasticity, spending / phi))
         revenue = jnp.sum(gather(jnp.sum(supply * partial_sales, axis=0), "dest"), axis=0)
@@ -292,12 +293,9 @@
 def fast(log_cost, elasticity, productivity, preference, workers, start_wage):
     sectors, rows = productivity.shape
     columns = log_cost.shape[1]
-    across, along = lax.axis_size("orig"), lax.axis_size("dest")
-    cells = float(rows * across)
+    outer, along = lax.axis_size("far"), lax.axis_size("dest")
+    cells = float(rows * outer * INNER)
     pieces = rows // LANES
-    outer = across // INNER
-    by_inner = [[i * INNER + j for j in range(INNER)] for i in range(outer)]
-    by_outer = [[i * INNER + j for i in range(outer)] for j in range(INNER)]
     workers = workers.reshape(pieces, LANES)
     wage = start_wage.reshape(pieces, LANES)
     sales = trade = None
@@ -320,9 +318,9 @@
                 outs + [f32(pieces, LANES)], [],
                 [facts, trade, productivity, workers, wage, sales], scratch,
             )
-        got = exchange(send, "orig", by_outer)
+        got = exchange(send, "far")
         send, = call(sum_kernel, [f32(INNER, sectors, width)], [], [got])
-        got = exchange(send, "orig", by_inner)
+        got = exchange(send, "near")
         made = call(
             functools.partial(sales_kernel, last, cells),
             [f32(along, pieces, LANES)] + ([f32(sectors, columns)] if last else []),
@@ -331,8 +329,8 @@
             [(rows, LANES), (sectors, columns), (sectors, width)],
         )
         sales = exchange(made[0], "dest")
-    raw, send = call(settle_kernel, [f32(pieces, LANES), f32(across, 2, LANES)], [], [workers, wage, sales])
-    got = exchange(send, "orig")
+    raw, send = call(settle_kernel, [f32(pieces, LANES), f32(outer * INNER, 2, LANES)], [], [workers, wage, sales])
+    got = exchange(send, ORIG)
     wage, log_price, world = call(
         functools.partial(finish_kernel, cells),
         [f32(pieces, LANES), f32(sectors, columns), f32(1, LANES)], [], [raw, made[1], got],
@@ -351,10 +349,12 @@
 
 
 def solution(mesh):
+    across, along = mesh.devices.shape
+    split = Mesh(mesh.devices.reshape(across // INNER, INNER, along), (*ORIG, "dest"))
     return jax.shard_map(
         on_device,
-        mesh=mesh,
-        in_specs=(P("orig", "dest"), P(), P(None, "orig"), P(None, "dest"), P("orig"), P("orig")),
-        out_specs=(P("orig"), P(None, "dest")),
+        mesh=split,
+        in_specs=(P(ORIG, "dest"), P(), P(None, ORIG), P(None, "dest"), P(ORIG), P(ORIG)),
+        out_specs=(P(ORIG), P(None, "dest")),
         check_vma=False,
     )

time: 157 us -> 155 us (0.987)
  Pallas kernels: 15 us -> 13.3 us
    pallas_call x11, Pallas kernels: 15 us -> 13.3 us  [call(): pl.pallas_call(body, out_shape=tuple(out_shape), in_specs=[SM] * len(scal...]
where the time goes in v10:
time: 155 us; the launch traced here: 154 us
  blocking collectives  140 us (90%)
  Pallas kernels  13.3 us (9%)
    all_to_all x10, blocking collectives, exchange(): return lax.all_to_all(x, axis, 0, 0, tiled=True)  140 us
    pallas_call x11, Pallas kernels, call(): pl.pallas_call(body, out_shape=tuple(out_shape), in_specs=[SM] * len(scal...  13.3 us

profile of v10, /device:TPU:1, one launch (start us, length us, event | category | flops | bytes accessed | tf_op | source)
XLA Modules:
  0.0 154.4 jit_solution(13528691864093016645)
XLA Ops:
  0.6 0.0 copy-start.1
  0.6 4.5 %shard_map.77 = (f32[4,8,1280]{2,1,0:T(8,128)S(1)}, f32[512,1024]{1,0:T(8,128)S(1)}, f32[8,512,1024]{2,1,0:T(8,128)S(1)}, f32[16,128]{1,0:T(8,128)S(1)}) custom-call(bf16[512,1024]{1,0:T(8,128)(2,1)} %cost_in_ref.1, f32[8]{0:T(128)} %slope_in_ref.1, f32[8,512]{1,0:T(8,128)} %productivity_ref.3, f32[4,128]{1,0:T(4,128)} %bitcast.81, f32[4,128]{1,0:T(4,128)} %bitcast.88), custom_call_target="tpu_custom_call" | custom-call | tf_op jit(solution)/shard_map/pallas_call | solution.py:234
  5.1 13.2 %all_to_all.127.got_ref = f32[4,8,1280]{2,1,0:T(8,128)S(1)} all-to-all(f32[4,8,1280]{2,1,0:T(8,128)S(1)} %get-tuple-element.229), channel_id=1, replica_groups=mesh['far'=4,'near'=8,'dest'=16] {'far'}, dimensions={0} | all-to-all | bytes 327680 | tf_op jit(solution)/shard_map/all_to_all | solution.py:245
  18.3 16.6 %all_to_all.128.got_ref = f32[8,8,1280]{2,1,0:T(8,128)S(1)} all-to-all(f32[8,8,1280]{2,1,0:T(8,128)S(1)} %shard_map.78), channel_id=1, replica_groups=mesh['far'=4,'near'=8,'dest'=16] {'near'}, dimensions={0} | all-to-all | bytes 655360 | tf_op jit(solution)/shard_map/all_to_all | solution.py:245
  35.0 0.0 copy-done.1
  35.0 0.0 copy-start
  35.0 0.0 copy-start.2
  35.0 0.0 copy-start.4
  35.0 1.7 %shard_map.79 = f32[16,4,128]{2,1,0:T(4,128)S(1)} custom-call(f32[16,128]{1,0:T(8,128)S(1)} %get-tuple-element.226.facts_ref, f32[8,512,1024]{2,1,0:T(8,128)S(1)} %get-tuple-element.227.trade_ref, f32[512,1024]{1,0:T(8,128)S(1)} %get-tuple-element.228.spread_ref, f32[8,1024]{1,0:T(8,128)S(1)} %copy-done.1, f32[8,8,1280]{2,1,0:T(8,128)S(1)} %all_to_all.128.got_ref), custom_call_target="tpu_custom_call" | custom-call | tf_op jit(solution)/shard_map/pallas_call | solution.py:234
  36.7 23.9 %all_to_all.129.sales_ref = f32[16,4,128]{2,1,0:T(4,128)S(1)} all-to-all(f32[16,4,128]{2,1,0:T(4,128)S(1)} %shard_map.79), channel_id=1, replica_groups=mesh['far'=4,'near'=8,'dest'=16] {'dest'}, dimensions={0} | all-to-all | bytes 65536 | tf_op jit(solution)/shard_map/all_to_all | solution.py:245
  60.6 0.0 copy-done
  60.6 0.0 copy-done.2
  60.6 0.0 copy-done.4
  60.6 1.5 shard_map.80
  62.1 8.6 %all_to_all.130.got_ref = f32[4,8,1152]{2,1,0:T(8,128)S(1)} all-to-all(f32[4,8,1152]{2,1,0:T(8,128)S(1)} %get-tuple-element.232), channel_id=1, replica_groups=mesh['far'=4,'near'=8,'dest'=16] {'far'}, dimensions={0} | all-to-all | bytes 294912 | tf_op jit(solution)/shard_map/all_to_all | solution.py:245
  70.7 12.2 %all_to_all.131.got_ref = f32[8,8,1152]{2,1,0:T(8,128)S(1)} all-to-all(f32[8,8,1152]{2,1,0:T(8,128)S(1)} %shard_map.81), channel_id=1, replica_groups=mesh['far'=4,'near'=8,'dest'=16] {'near'}, dimensions={0} | all-to-all | bytes 589824 | tf_op jit(solution)/shard_map/all_to_all | solution.py:245
  82.9 1.6 %shard_map.82 = f32[16,4,128]{2,1,0:T(4,128)S(1)} custom-call(f32[16,128]{1,0:T(8,128)S(1)} %get-tuple-element.226.facts_ref, f32[8,512,1024]{2,1,0:T(8,128)S(1)} %get-tuple-element.227.trade_ref, f32[512,1024]{1,0:T(8,128)S(1)} %get-tuple-element.231.spread_ref, f32[8,1024]{1,0:T(8,128)S(1)} %copy-done.1, f32[8,8,1152]{2,1,0:T(8,128)S(1)} %all_to_all.131.got_ref), custom_call_target="tpu_custom_call" | custom-call | tf_op jit(solution)/shard_map/pallas_call | solution.py:234
  84.5 15.8 %all_to_all.132.sales_ref = f32[16,4,128]{2,1,0:T(4,128)S(1)} all-to-all(f32[16,4,128]{2,1,0:T(4,128)S(1)} %shard_map.82), channel_id=1, replica_groups=mesh['far'=4,'near'=8,'dest'=16] {'dest'}, dimensions={0} | all-to-all | bytes 65536 | tf_op jit(solution)/shard_map/all_to_all | solution.py:245
  100.4 1.5 shard_map.83
  101.9 8.8 %all_to_all.133.got_ref = f32[4,8,1152]{2,1,0:T(8,128)S(1)} all-to-all(f32[4,8,1152]{2,1,0:T(8,128)S(1)} %get-tuple-element.235), channel_id=1, replica_groups=mesh['far'=4,'near'=8,'dest'=16] {'far'}, dimensions={0} | all-to-all | bytes 294912 | tf_op jit(solution)/shard_map/all_to_all | solution.py:245
  110.7 12.2 %all_to_all.134.got_ref = f32[8,8,1152]{2,1,0:T(8,128)S(1)} all-to-all(f32[8,8,1152]{2,1,0:T(8,128)S(1)} %shard_map.84), channel_id=1, replica_groups=mesh['far'=4,'near'=8,'dest'=16] {'near'}, dimensions={0} | all-to-all | bytes 589824 | tf_op jit(solution)/shard_map/all_to_all | solution.py:245
  123.0 0.0 copy-start.3
  123.0 0.0 copy-start.5
  123.0 1.6 %shard_map.85 = (f32[16,4,128]{2,1,0:T(4,128)S(1)}, f32[8,1024]{1,0:T(8,128)S(1)}) custom-call(f32[16,128]{1,0:T(8,128)S(1)} %get-tuple-element.226.facts_ref, f32[8,512,1024]{2,1,0:T(8,128)S(1)} %get-tuple-element.227.trade_ref, f32[512,1024]{1,0:T(8,128)S(1)} %get-tuple-element.234.spread_ref, f32[8,1024]{1,0:T(8,128)S(1)} %copy-done.1, ...), custom_call_target="tpu_custom_call" | custom-call | tf_op jit(solution)/shard_map/pallas_call | solution.py:234
  124.6 15.8 %all_to_all.135.sales_ref = f32[16,4,128]{2,1,0:T(4,128)S(1)} all-to-all(f32[16,4,128]{2,1,0:T(4,128)S(1)} %get-tuple-element.236), channel_id=1, replica_groups=mesh['far'=4,'near'=8,'dest'=16] {'dest'}, dimensions={0} | all-to-all | bytes 65536 | tf_op jit(solution)/shard_map/all_to_all | solution.py:245
  140.5 12.7 %all_to_all.136.got_ref = f32[32,2,128]{2,1,0:T(2,128)S(1)} all-to-all(f32[32,2,128]{2,1,0:T(2,128)S(1)} %get-tuple-element.239), channel_id=1, replica_groups=mesh['far'=4,'near'=8,'dest'=16] {'far','near'}, dimensions={0} | all-to-all | bytes 65536 | tf_op jit(solution)/shard_map/all_to_all | solution.py:245
  153.2 0.7 shard_map.87
  154.0 0.0 copy-done.3
  154.0 0.0 copy-done.5
  154.0 0.2 while.65
  (4 shorter events, 0.1 us)
Async XLA Ops:
  0.6 34.3 %copy-start.1 = (f32[8,1024]{1,0:T(8,128)S(1)}, f32[8,1024]{1,0:T(8,128)}, u32[]{:S(2)}) copy-start(f32[8,1024]{1,0:T(8,128)} %preference_ref.5) | copy-start | bytes 98308
  35.0 25.6 %copy-start = (f32[8,512]{1,0:T(8,128)S(1)}, f32[8,512]{1,0:T(8,128)}, u32[]{:S(2)}) copy-start(f32[8,512]{1,0:T(8,128)} %productivity_ref.3) | copy-start | bytes 49156
  35.0 25.6 %copy-start.2 = (f32[512]{0:T(512)S(1)}, f32[512]{0:T(512)}, u32[]{:S(2)}) copy-start(f32[512]{0:T(512)} %param.24) | copy-start | bytes 6148
  35.0 25.6 %copy-start.4 = (f32[512]{0:T(512)S(1)}, f32[512]{0:T(512)}, u32[]{:S(2)}) copy-start(f32[512]{0:T(512)} %param.25) | copy-start | bytes 6148
  123.0 31.0 %copy-start.3 = (bf16[512,1024]{1,0:T(8,128)(2,1)S(1)}, bf16[512,1024]{1,0:T(8,128)(2,1)}, u32[]{:S(2)}) copy-start(bf16[512,1024]{1,0:T(8,128)(2,1)} %cost_in_ref.1) | copy-start | bytes 3145732
  123.0 31.0 %copy-start.5 = (f32[8]{0:T(128)S(1)}, f32[8]{0:T(128)}, u32[]{:S(2)}) copy-start(f32[8]{0:T(128)} %slope_in_ref.1) | copy-start | bytes 100

commit v11 on v10

--- a/solution.py
+++ b/solution.py
@@ -10,8 +10,8 @@
 
 ITERS = 3
 LANES = 128
-CENTRE = 1024.0
-GAIN = 2.0
+GAINS = (64.0, 4.0)
+SMALLEST, LARGEST = 1e-32, 1e30
 INNER = 8
 ORIG = ("far", "near")
 SMALLEST, LARGEST = 1e-32, 1e30
@@ -33,10 +33,6 @@
     for j in range(count):
         out = jnp.where(row == j, vector_ref[j], out)
     return out
-
-
-def total_of(x):
-    return jnp.sum(jnp.sum(x, axis=0, keepdims=True), axis=1, keepdims=True)
 
 
 def next_wage(wage_ref, workers_ref, sales_ref, gain=1.0):
@@ -82,9 +78,6 @@
     guarded = jnp.where(least > SMALLEST, income, jnp.nan)
     for i in range(columns // rows):
         part_ref[i * pieces:(i + 1) * pieces, columns:columns + LANES] = guarded * here[i:i + 1]
-    if part_ref.shape[1] > columns + LANES:
-        part_ref[:, columns + LANES:] = jnp.zeros((sectors, LANES), jnp.float32)
-        part_ref[:pieces, columns + LANES:] = income
 
 
 def send_phi(totals_ref, part_ref, send_ref):
@@ -143,7 +136,7 @@
 
     for i, copy in enumerate(copies):
         copy.wait()
-        lax.fori_loop(i * batch // height, (i + 1) * batch // height, step, 0)
+        lax.fori_loop(i * batch // height, (i + 1) * batch // height, step, 0, unroll=2)
     send_phi(totals_ref, part_ref, send_ref)
 
 
@@ -172,7 +165,7 @@
         send_ref[copy] = total
 
 
-def sales_kernel(last, cells, facts_ref, trade_ref, spread_ref, preference_ref, got_ref, send_ref, *rest):
+def sales_kernel(last, facts_ref, trade_ref, spread_ref, preference_ref, got_ref, send_ref, *rest):
     total_ref, ratio_ref, sums_ref = rest[-3:]
     sectors, rows, columns = trade_ref.shape
     blocks = columns // LANES
@@ -184,9 +177,6 @@
         phi = sums_ref[:, lanes]
         ratio = share[:, lanes] * sums_ref[k:k + 1, columns:columns + LANES] / phi
         ratio_ref[:, lanes] = jnp.where(phi < LARGEST, ratio, jnp.nan)
-    if sums_ref.shape[1] > columns + LANES:
-        centred = CENTRE * cells / total_of(sums_ref[:, columns + LANES:])
-        ratio_ref[...] *= centred * centred
     if last:
         slopes = facts_ref[:sectors]
         for k in range(blocks):
@@ -295,13 +285,12 @@
     columns = log_cost.shape[1]
     outer, along = lax.axis_size("far"), lax.axis_size("dest")
     cells = float(rows * outer * INNER)
-    pieces = rows // LANES
+    pieces, width = rows // LANES, columns + LANES
     workers = workers.reshape(pieces, LANES)
     wage = start_wage.reshape(pieces, LANES)
     sales = trade = None
     for step in range(ITERS):
         last = step + 1 == ITERS
-        width = columns + (2 if step == 0 else 1) * LANES
         outs = [f32(outer, sectors, width), f32(rows, sectors * LANES)]
         scratch = [(sectors, 8, columns), (sectors, rows), (sectors, width)]
         if step == 0:
@@ -314,7 +303,7 @@
             )
         else:
             send, spread, wage = call(
-                functools.partial(phi_kernel, 1.0 if step == 1 else GAIN),
+                functools.partial(phi_kernel, GAINS[step - 1]),
                 outs + [f32(pieces, LANES)], [],
                 [facts, trade, productivity, workers, wage, sales], scratch,
             )
@@ -322,7 +311,7 @@
         send, = call(sum_kernel, [f32(INNER, sectors, width)], [], [got])
         got = exchange(send, "near")
         made = call(
-            functools.partial(sales_kernel, last, cells),
+            functools.partial(sales_kernel, last),
             [f32(along, pieces, LANES)] + ([f32(sectors, columns)] if last else []),
             [],
             [facts, trade, spread, preference, got],

time: 155 us -> 154 us (level)
  no operation moved by 1% of the time
where the time goes in v11:
time: 154 us; the launch traced here: 153 us
  blocking collectives  139 us (90%)
  Pallas kernels  13.1 us (9%)
    all_to_all x10, blocking collectives, exchange(): return lax.all_to_all(x, axis, 0, 0, tiled=True)  139 us
    pallas_call x11, Pallas kernels, call(): pl.pallas_call(body, out_shape=tuple(out_shape), in_specs=[SM] * len(scal...  13.1 us

profile of v11, /device:TPU:1, one launch (start us, length us, event | category | flops | bytes accessed | tf_op | source)
XLA Modules:
  0.0 153.2 jit_solution(11844193947265919895)
XLA Ops:
  0.6 0.0 copy-start.1
  0.6 4.3 %shard_map.77 = (f32[4,8,1152]{2,1,0:T(8,128)S(1)}, f32[512,1024]{1,0:T(8,128)S(1)}, f32[8,512,1024]{2,1,0:T(8,128)S(1)}, f32[16,128]{1,0:T(8,128)S(1)}) custom-call(bf16[512,1024]{1,0:T(8,128)(2,1)} %cost_in_ref.1, f32[8]{0:T(128)} %slope_in_ref.1, f32[8,512]{1,0:T(8,128)} %productivity_ref.3, f32[4,128]{1,0:T(4,128)} %bitcast.81, f32[4,128]{1,0:T(4,128)} %bitcast.88), custom_call_target="tpu_custom_call" | custom-call | tf_op jit(solution)/shard_map/pallas_call | solution.py:224
  5.0 13.1 %all_to_all.127.got_ref = f32[4,8,1152]{2,1,0:T(8,128)S(1)} all-to-all(f32[4,8,1152]{2,1,0:T(8,128)S(1)} %get-tuple-element.229), channel_id=1, replica_groups=mesh['far'=4,'near'=8,'dest'=16] {'far'}, dimensions={0} | all-to-all | bytes 294912 | tf_op jit(solution)/shard_map/all_to_all | solution.py:235
  18.2 16.3 %all_to_all.128.got_ref = f32[8,8,1152]{2,1,0:T(8,128)S(1)} all-to-all(f32[8,8,1152]{2,1,0:T(8,128)S(1)} %shard_map.78), channel_id=1, replica_groups=mesh['far'=4,'near'=8,'dest'=16] {'near'}, dimensions={0} | all-to-all | bytes 589824 | tf_op jit(solution)/shard_map/all_to_all | solution.py:235
  34.5 0.0 copy-done.1
  34.5 0.0 copy-start
  34.5 0.0 copy-start.2
  34.5 0.0 copy-start.4
  34.5 1.6 %shard_map.79 = f32[16,4,128]{2,1,0:T(4,128)S(1)} custom-call(f32[16,128]{1,0:T(8,128)S(1)} %get-tuple-element.226.facts_ref, f32[8,512,1024]{2,1,0:T(8,128)S(1)} %get-tuple-element.227.trade_ref, f32[512,1024]{1,0:T(8,128)S(1)} %get-tuple-element.228.spread_ref, f32[8,1024]{1,0:T(8,128)S(1)} %copy-done.1, f32[8,8,1152]{2,1,0:T(8,128)S(1)} %all_to_all.128.got_ref), custom_call_target="tpu_custom_call" | custom-call | tf_op jit(solution)/shard_map/pallas_call | solution.py:224
  36.1 23.5 %all_to_all.129.sales_ref = f32[16,4,128]{2,1,0:T(4,128)S(1)} all-to-all(f32[16,4,128]{2,1,0:T(4,128)S(1)} %shard_map.79), channel_id=1, replica_groups=mesh['far'=4,'near'=8,'dest'=16] {'dest'}, dimensions={0} | all-to-all | bytes 65536 | tf_op jit(solution)/shard_map/all_to_all | solution.py:235
  59.6 0.0 copy-done
  59.6 0.0 copy-done.2
  59.6 0.0 copy-done.4
  59.6 1.5 shard_map.80
  61.2 8.3 %all_to_all.130.got_ref = f32[4,8,1152]{2,1,0:T(8,128)S(1)} all-to-all(f32[4,8,1152]{2,1,0:T(8,128)S(1)} %get-tuple-element.232), channel_id=1, replica_groups=mesh['far'=4,'near'=8,'dest'=16] {'far'}, dimensions={0} | all-to-all | bytes 294912 | tf_op jit(solution)/shard_map/all_to_all | solution.py:235
  69.5 12.2 %all_to_all.131.got_ref = f32[8,8,1152]{2,1,0:T(8,128)S(1)} all-to-all(f32[8,8,1152]{2,1,0:T(8,128)S(1)} %shard_map.81), channel_id=1, replica_groups=mesh['far'=4,'near'=8,'dest'=16] {'near'}, dimensions={0} | all-to-all | bytes 589824 | tf_op jit(solution)/shard_map/all_to_all | solution.py:235
  81.7 1.6 %shard_map.82 = f32[16,4,128]{2,1,0:T(4,128)S(1)} custom-call(f32[16,128]{1,0:T(8,128)S(1)} %get-tuple-element.226.facts_ref, f32[8,512,1024]{2,1,0:T(8,128)S(1)} %get-tuple-element.227.trade_ref, f32[512,1024]{1,0:T(8,128)S(1)} %get-tuple-element.231.spread_ref, f32[8,1024]{1,0:T(8,128)S(1)} %copy-done.1, f32[8,8,1152]{2,1,0:T(8,128)S(1)} %all_to_all.131.got_ref), custom_call_target="tpu_custom_call" | custom-call | tf_op jit(solution)/shard_map/pallas_call | solution.py:224
  83.3 15.8 %all_to_all.132.sales_ref = f32[16,4,128]{2,1,0:T(4,128)S(1)} all-to-all(f32[16,4,128]{2,1,0:T(4,128)S(1)} %shard_map.82), channel_id=1, replica_groups=mesh['far'=4,'near'=8,'dest'=16] {'dest'}, dimensions={0} | all-to-all | bytes 65536 | tf_op jit(solution)/shard_map/all_to_all | solution.py:235
  99.2 1.5 shard_map.83
  100.7 8.8 %all_to_all.133.got_ref = f32[4,8,1152]{2,1,0:T(8,128)S(1)} all-to-all(f32[4,8,1152]{2,1,0:T(8,128)S(1)} %get-tuple-element.235), channel_id=1, replica_groups=mesh['far'=4,'near'=8,'dest'=16] {'far'}, dimensions={0} | all-to-all | bytes 294912 | tf_op jit(solution)/shard_map/all_to_all | solution.py:235
  109.5 12.2 %all_to_all.134.got_ref = f32[8,8,1152]{2,1,0:T(8,128)S(1)} all-to-all(f32[8,8,1152]{2,1,0:T(8,128)S(1)} %shard_map.84), channel_id=1, replica_groups=mesh['far'=4,'near'=8,'dest'=16] {'near'}, dimensions={0} | all-to-all | bytes 589824 | tf_op jit(solution)/shard_map/all_to_all | solution.py:235
  121.8 0.0 copy-start.3
  121.8 0.0 copy-start.5
  121.8 1.6 %shard_map.85 = (f32[16,4,128]{2,1,0:T(4,128)S(1)}, f32[8,1024]{1,0:T(8,128)S(1)}) custom-call(f32[16,128]{1,0:T(8,128)S(1)} %get-tuple-element.226.facts_ref, f32[8,512,1024]{2,1,0:T(8,128)S(1)} %get-tuple-element.227.trade_ref, f32[512,1024]{1,0:T(8,128)S(1)} %get-tuple-element.234.spread_ref, f32[8,1024]{1,0:T(8,128)S(1)} %copy-done.1, ...), custom_call_target="tpu_custom_call" | custom-call | tf_op jit(solution)/shard_map/pallas_call | solution.py:224
  123.4 15.8 %all_to_all.135.sales_ref = f32[16,4,128]{2,1,0:T(4,128)S(1)} all-to-all(f32[16,4,128]{2,1,0:T(4,128)S(1)} %get-tuple-element.236), channel_id=1, replica_groups=mesh['far'=4,'near'=8,'dest'=16] {'dest'}, dimensions={0} | all-to-all | bytes 65536 | tf_op jit(solution)/shard_map/all_to_all | solution.py:235
  139.3 12.7 %all_to_all.136.got_ref = f32[32,2,128]{2,1,0:T(2,128)S(1)} all-to-all(f32[32,2,128]{2,1,0:T(2,128)S(1)} %get-tuple-element.239), channel_id=1, replica_groups=mesh['far'=4,'near'=8,'dest'=16] {'far','near'}, dimensions={0} | all-to-all | bytes 65536 | tf_op jit(solution)/shard_map/all_to_all | solution.py:235
  152.0 0.7 shard_map.87
  152.8 0.0 copy-done.3
  152.8 0.0 copy-done.5
  152.8 0.2 while.65
  (4 shorter events, 0.1 us)
Async XLA Ops:
  0.6 33.9 %copy-start.1 = (f32[8,1024]{1,0:T(8,128)S(1)}, f32[8,1024]{1,0:T(8,128)}, u32[]{:S(2)}) copy-start(f32[8,1024]{1,0:T(8,128)} %preference_ref.5) | copy-start | bytes 98308
  34.5 25.1 %copy-start = (f32[8,512]{1,0:T(8,128)S(1)}, f32[8,512]{1,0:T(8,128)}, u32[]{:S(2)}) copy-start(f32[8,512]{1,0:T(8,128)} %productivity_ref.3) | copy-start | bytes 49156
  34.5 25.1 %copy-start.2 = (f32[512]{0:T(512)S(1)}, f32[512]{0:T(512)}, u32[]{:S(2)}) copy-start(f32[512]{0:T(512)} %param.24) | copy-start | bytes 6148
  34.5 25.1 %copy-start.4 = (f32[512]{0:T(512)S(1)}, f32[512]{0:T(512)}, u32[]{:S(2)}) copy-start(f32[512]{0:T(512)} %param.25) | copy-start | bytes 6148
  121.8 31.0 %copy-start.3 = (bf16[512,1024]{1,0:T(8,128)(2,1)S(1)}, bf16[512,1024]{1,0:T(8,128)(2,1)}, u32[]{:S(2)}) copy-start(bf16[512,1024]{1,0:T(8,128)(2,1)} %cost_in_ref.1) | copy-start | bytes 3145732
  121.8 31.0 %copy-start.5 = (f32[8]{0:T(128)S(1)}, f32[8]{0:T(128)}, u32[]{:S(2)}) copy-start(f32[8]{0:T(128)} %slope_in_ref.1) | copy-start | bytes 100
